TPU v7x, 128 devices: a whole 4x4x4 slice. The times are simulated.
128 devices in a mesh: cells: 4 (over y_lo, core), genes: 32 (over x, z, y_hi).
Axes of the slice: x: 4, y: 4 (y_hi: 2, y_lo: 2; y = y_hi * 2 + y_lo), z: 4, core: 2. Of those that a mesh axis runs over, the one named last changes fastest.
Arguments:
- expression: float32 [640, 65536], P('cells', 'genes'), may hold values from -6 to 6
- omega_diag: float32 [256, 256, 256], P('genes'), may hold values from -0.25 to 2, as said below
- omega_offd: float32 [256, 6, 256, 256], P('genes'), may hold values from -0.3 to 0.3
- omega_src: int32 [256, 6], replicated, may hold values from 0 to 31, all different within a row; in each aligned block of 8 rows (0 to 7, 8 to 15, ...) at most 2 rows name the same one
- omega_off: int32 [256, 6], replicated, may hold values from 0 to 6
Outputs:
- new_diag: float32 [256, 256, 256], P(('genes', 'cells'))
- new_offd: float32 [256, 6, 256, 256], P(('genes', 'cells'))
Inputs may be any that keep to these rules, and one draw needn't show every extreme that they name: `omega_src`: the 6 values of one row are distinct. Among the 8 rows of one index of genes (rows i * 8 to (i+1) * 8 - 1) no value appears more than 2 times, and in every draw some such group of rows names some value exactly 2 times. `omega_diag`: diagonal entries lie in 0.5 to 2; all other entries lie in -0.25 to 0.25.
All inputs are finite; a program needn't handle non-finite values.
Results may differ from a plain program's by a relative error of at most 0.000075.
Values sent between devices are 32-bit elements; how exact they have to be, the bound alone decides.
No kernel may reach another device: no remote copies, remote signals or barrier semaphores. Data moves between devices by JAX's collectives and lax.ppermute only.
A program may use at most 192 MiB of HBM per device.

v0:
```python
import jax
import jax.numpy as jnp
from jax import lax
from jax.sharding import PartitionSpec as P


def stored_rows(omega_src, omega_off, per_dev):
    cols = lax.broadcasted_iota(jnp.int32, omega_src.shape, 0)
    bump = jnp.logical_and(omega_src == cols // per_dev, omega_off >= cols % per_dev).astype(
        jnp.int32
    )
    return omega_src * per_dev + omega_off + bump


def slot_ranks(src_groups, count):
    onehot = (src_groups[:, :, None] == lax.broadcasted_iota(jnp.int32, (1, 1, count), 2)).astype(
        jnp.int32
    )
    ranks = jnp.cumsum(onehot, axis=1) - 1
    return jnp.sum(onehot * ranks, axis=2)


def shrink(values, limit):
    return values - jnp.clip(values, -limit, limit)


def partials(own_x, own_y, far_x, far_y):
    highest = lax.Precision.HIGHEST
    diag_part = jnp.einsum("cjb,cje->jbe", own_x, own_y, precision=highest)
    diag_part = diag_part + jnp.swapaxes(diag_part, 1, 2)
    off_part = jnp.einsum("cjkb,cje->jkbe", far_x, own_y, precision=highest)
    off_part = off_part + jnp.einsum("cjkb,cje->jkbe", far_y, own_x, precision=highest)
    return (diag_part, off_part)


def per_device(expression, omega_diag, omega_offd, omega_src, omega_off):
    highest = lax.Precision.HIGHEST
    groups = lax.axis_size("genes")
    here = lax.axis_index("genes")
    per_dev = omega_diag.shape[0]
    fan = omega_src.shape[1]
    width = omega_diag.shape[1]
    cell_rows = expression.shape[0]
    most = max(2, (per_dev * fan + groups - 1) // groups)
    rows = stored_rows(omega_src, omega_off, per_dev)
    src_groups = omega_src.reshape(groups, per_dev * fan)
    local_groups = (rows % per_dev).reshape(groups, per_dev * fan)
    slots = slot_ranks(src_groups, groups)
    slot_iota = lax.broadcasted_iota(jnp.int32, (1, 1, most), 2)
    match = jnp.logical_and(
        (src_groups == here)[:, :, None], slots[:, :, None] == slot_iota
    ).astype(jnp.int32)
    send_index = jnp.sum(match * local_groups[:, :, None], axis=1).reshape(-1)
    mine_src = lax.dynamic_index_in_dim(src_groups, here, 0, keepdims=False)
    mine_slot = lax.dynamic_index_in_dim(slots, here, 0, keepdims=False)
    pick = mine_src * most + mine_slot
    local_x = expression.reshape(cell_rows, per_dev, width)
    sent_x = jnp.take(local_x, send_index, axis=1).reshape(cell_rows, groups, most, width)
    came_x = lax.all_to_all(sent_x, "genes", split_axis=1, concat_axis=1, tiled=True)
    far_x = jnp.take(came_x.reshape(cell_rows, groups * most, width), pick, axis=1).reshape(
        cell_rows, per_dev, fan, width
    )
    own_y = jnp.einsum("cjb,jbe->cje", local_x, omega_diag, precision=highest)
    own_y = own_y + jnp.einsum("cjkb,jkbe->cje", far_x, omega_offd, precision=highest)
    sent_y = jnp.take(own_y, send_index, axis=1).reshape(cell_rows, groups, most, width)
    came_y = lax.all_to_all(sent_y, "genes", split_axis=1, concat_axis=1, tiled=True)
    far_y = jnp.take(came_y.reshape(cell_rows, groups * most, width), pick, axis=1).reshape(
        cell_rows, per_dev, fan, width
    )
    share = per_dev // lax.axis_size("cells")
    where = lax.axis_index("cells")
    diag_part, off_part = partials(local_x, own_y, far_x, far_y)
    diag_all, off_all = lax.psum((diag_part, off_part), "cells")
    diag_sum = lax.dynamic_slice_in_dim(diag_all, where * share, share, 0)
    off_sum = lax.dynamic_slice_in_dim(off_all, where * share, share, 0)
    mine_diag = lax.dynamic_slice_in_dim(omega_diag, where * share, share, 0)
    mine_off = lax.dynamic_slice_in_dim(omega_offd, where * share, share, 0)
    step_size = 0.5
    limit = step_size * 0.04
    scale = 1.0 / (2.0 * cell_rows * lax.axis_size("cells"))
    eye = (
        lax.broadcasted_iota(jnp.int32, (width, width), 0)
        == lax.broadcasted_iota(jnp.int32, (width, width), 1)
    ).astype(jnp.float32)
    entries = jnp.sum(mine_diag * eye, axis=2)
    grad_diag = diag_sum * scale - eye * (1.0 / entries)[:, :, None]
    moved = mine_diag - step_size * grad_diag
    new_diag = eye * moved + (1.0 - eye) * shrink(moved, limit)
    new_offd = shrink(mine_off - step_size * (off_sum * scale), limit)
    return (new_diag, new_offd)


def solution(mesh):
    return jax.shard_map(
        per_device,
        mesh=mesh,
        in_specs=(
            P("cells", "genes"),
            P("genes", None, None),
            P("genes", None, None, None),
            P(),
            P(),
        ),
        out_specs=(P(("genes", "cells"), None, None), P(("genes", "cells"), None, None, None)),
        check_vma=False,
    )
```

profile of v0, /device:TPU:1, one launch (start us, length us, event | category | flops | bytes accessed | tf_op | source)
XLA Modules:
  0.0 741.2 jit_solution(5812072321096318471)
XLA Ops:
  7.2 0.8 copy.45
  8.0 0.7 add_select_fusion
  8.8 0.1 copy.49
  8.9 0.1 mul.94
  9.0 0.1 reshape.69
  9.1 0.1 copy.46
  9.2 1.3 select_reduce_fusion
  10.5 0.1 copy.48
  10.6 0.1 select_reduce_fusion.1
  10.7 0.1 copy.50
  10.8 0.1 reshape.70
  11.0 1.4 copy.67
  12.4 5.1 gather_fusion
  17.5 10.0 %broadcast_select_fusion.1 = f32[64,160,256]{2,1,0:T(8,128)} fusion(f32[64,160,256]{2,1,0:T(8,128)} %gather_fusion, pred[64]{0:T(512)(128)(4,1)S(1)} %compare_and_fusion.1), kind=kLoop, calls=%fused_computation.5 | loop fusion | flops 2621440 | bytes 20971584 | tf_op jit(solution)/shard_map/jit(_take)/select_n | solution.py:58
  27.5 11.8 %all-to-all-start = ((f32[160,32,2,256]{3,0,2,1:T(8,128)}), f32[160,32,2,256]{3,0,2,1:T(8,128)}, u32[]{:S(2)}, u32[]{:S(2)}) async-start(f32[160,32,2,256]{3,0,2,1:T(8,128)} %bitcast.49), calls=%async_computation | async-start | bytes 20971520 | tf_op jit(solution)/shard_map/all_to_all | solution.py:59
  39.3 0.2 add_reduce_fusion
  39.5 161.0 %all-to-all-done = f32[160,32,2,256]{3,0,2,1:T(8,128)} async-done(((f32[160,32,2,256]{3,0,2,1:T(8,128)}), f32[160,32,2,256]{3,0,2,1:T(8,128)}, u32[]{:S(2)}, u32[]{:S(2)}) %all-to-all-start) | async-done | bytes 10485792 | tf_op jit(solution)/shard_map/all_to_all | solution.py:59
  200.5 8.2 %gather_fusion.1 = f32[48,160,256]{2,1,0:T(8,128)} fusion(f32[160,64,256]{2,0,1:T(8,128)} %bitcast.3, s32[1024]{0:T(1024)S(1)} %pad_clamp_fusion), kind=kCustom, calls=%fused_computation.1.clone | custom fusion | bytes 15728832 | tf_op jit(solution)/shard_map/jit(_take)/gather | solution.py:60
  208.7 4.7 broadcast_select_fusion.3
  213.4 0.0 copy-start
  213.4 0.0 copy-start.1
  213.4 14.2 %convolution_bitcast_fusion.1 = f32[160,8,256]{2,0,1:T(8,128)S(1)} fusion(f32[160,8,6,256]{3,0,2,1:T(8,128)S(1)} %bitcast.46, f32[8,6,256,256]{3,2,1,0:T(8,128)} %param.11), kind=kOutput, calls=%fused_computation.13 | convolution fusion | flops 6039797760 | bytes 21757952 | tf_op jit(solution)/shard_map/cjkb,jkbe->cje/dot_general | solution.py:64
  227.6 0.0 copy-done
  227.6 0.0 copy-done.1
  227.6 3.2 fusion
  230.8 5.1 gather_fusion.2
  235.9 10.0 %broadcast_select_fusion = f32[64,160,256]{2,1,0:T(8,128)} fusion(f32[64,160,256]{2,1,0:T(8,128)} %gather_fusion.2, pred[64]{0:T(512)(128)(4,1)S(1)} %compare_and_fusion.1), kind=kLoop, calls=%fused_computation.4 | loop fusion | flops 2621440 | bytes 20971584 | tf_op jit(solution)/shard_map/jit(_take)/select_n | solution.py:65
  245.9 19.5 %all-to-all-start.1 = ((f32[160,32,2,256]{3,0,2,1:T(8,128)}), f32[160,32,2,256]{3,0,2,1:T(8,128)}, u32[]{:S(2)}, u32[]{:S(2)}) async-start(f32[160,32,2,256]{3,0,2,1:T(8,128)} %bitcast.50), calls=%async_computation.1 | async-start | bytes 20971520 | tf_op jit(solution)/shard_map/all_to_all | solution.py:66
  265.4 10.4 %all-reduce.3.cloned.1.call-start = ((), (), s32[]{:S(2)}) async-start(), calls=%async_computation.2 | async-start | bytes 29360128 | tf_op jit(solution)/shard_map/psum | solution.py:73
  275.7 1.6 copy.61
  277.3 4.8 fusion.15
  282.2 1.9 copy.53
  284.1 3.2 bitcast_add_fusion
  287.3 24.7 %fusion.1 = f32[8,6,256,256]{3,2,1,0:T(8,128)} fusion(f32[160,8,6,256]{3,0,2,1:T(8,128)} %bitcast.47, f32[160,8,256]{2,0,1:T(8,128)S(1)} %fusion), kind=kOutput, calls=%fused_computation.15 | convolution fusion | flops 6039797760 | bytes 21757952 | tf_op jit(solution)/shard_map/cjkb,cje->jkbe/dot_general | solution.py:31
  312.0 114.7 %all-to-all-done.1 = f32[160,32,2,256]{3,0,2,1:T(8,128)} async-done(((f32[160,32,2,256]{3,0,2,1:T(8,128)}), f32[160,32,2,256]{3,0,2,1:T(8,128)}, u32[]{:S(2)}, u32[]{:S(2)}) %all-to-all-start.1) | async-done | bytes 10485792 | tf_op jit(solution)/shard_map/all_to_all | solution.py:66
  426.7 8.2 %gather_fusion.3 = f32[48,160,256]{2,1,0:T(8,128)} fusion(f32[160,64,256]{2,0,1:T(8,128)} %bitcast.15, s32[1024]{0:T(1024)S(1)} %pad_clamp_fusion), kind=kCustom, calls=%fused_computation.3.clone | custom fusion | bytes 15728832 | tf_op jit(solution)/shard_map/jit(_take)/gather | solution.py:67
  434.9 0.0 copy-start.2
  434.9 4.2 broadcast_select_fusion.2
  439.1 0.0 copy-done.2
  439.1 24.8 %convolution_add_fusion = f32[8,6,256,256]{3,2,1,0:T(8,128)} fusion(f32[8,6,256,256]{3,2,1,0:T(8,128)} %fusion.1, f32[160,8,6,256]{3,0,2,1:T(8,128)S(1)} %bitcast.51, f32[160,8,256,1]{2,1,0,3:T(8,128)S(1)} %bitcast.56), kind=kOutput, calls=%fused_computation.7 | convolution fusion | flops 6042943488 | bytes 34340864 | tf_op jit(solution)/shard_map/cjkb,cje->jkbe/dot_general | solution.py:32
  464.0 0.0 copy-start.3
  464.0 0.0 all-reduce.3.cloned.1.call-update
  464.1 1.5 copy-done.3
  465.6 0.1 multiply_reduce_fusion
  465.7 261.3 %all-reduce.3.cloned.1.call-done = (f32[8,256,256]{2,1,0:T(8,128)}, f32[8,6,256,256]{3,2,1,0:T(8,128)}) async-done(((f32[8,256,256]{2,1,0:T(8,128)}, f32[8,6,256,256]{3,2,1,0:T(8,128)}), (f32[8,256,256]{2,1,0:T(8,128)}, f32[8,6,256,256]{3,2,1,0:T(8,128)})) %all-reduce.3.cloned.1.call-update) | async-done | bytes 14680080 | tf_op jit(solution)/shard_map/psum | solution.py:73
  727.0 5.1 clamp_subtract_fusion
  732.0 2.1 fusion.7
  (13 shorter events, 0.1 us)
Async XLA Ops:
  27.5 173.0 %all-to-all-start = ((f32[160,32,2,256]{3,0,2,1:T(8,128)}), f32[160,32,2,256]{3,0,2,1:T(8,128)}, u32[]{:S(2)}, u32[]{:S(2)}) async-start(f32[160,32,2,256]{3,0,2,1:T(8,128)} %bitcast.49), calls=%async_computation | async-start | bytes 20971520 | tf_op jit(solution)/shard_map/all_to_all | solution.py:59
  213.4 14.2 %copy-start = (f32[48,160,256]{2,1,0:T(8,128)}, f32[48,160,256]{2,1,0:T(8,128)S(1)}, u32[]{:S(2)}) copy-start(f32[48,160,256]{2,1,0:T(8,128)S(1)} %broadcast_select_fusion.3) | copy-start | bytes 23592964
  213.4 14.2 %copy-start.1 = (f32[160,2048]{1,0:T(8,128)S(1)}, f32[160,2048]{1,0:T(8,128)}, u32[]{:S(2)}) copy-start(f32[160,2048]{1,0:T(8,128)} %param.9) | copy-start | bytes 3932164
  245.9 180.8 %all-to-all-start.1 = ((f32[160,32,2,256]{3,0,2,1:T(8,128)}), f32[160,32,2,256]{3,0,2,1:T(8,128)}, u32[]{:S(2)}, u32[]{:S(2)}) async-start(f32[160,32,2,256]{3,0,2,1:T(8,128)} %bitcast.50), calls=%async_computation.1 | async-start | bytes 20971520 | tf_op jit(solution)/shard_map/all_to_all | solution.py:66
  265.4 461.6 %all-reduce.3.cloned.1.call-start = ((), (), s32[]{:S(2)}) async-start(), calls=%async_computation.2 | async-start | bytes 29360128 | tf_op jit(solution)/shard_map/psum | solution.py:73
  434.9 4.2 copy-start.2
  464.0 1.6 copy-start.3
Sparse Core Ops, SparseCore 0:
  464.1 262.8 all-reduce.2
where the time goes:
time: 746 us; the launch traced here: 741 us
  waiting for transfers between devices  537 us (72%)
  matrix products  71.7 us (10%)
  other arithmetic  41.8 us (6%)
  starting transfers between devices  41.7 us (6%)
  local copies, waits for them, and re-layouts  34.5 us (5%)
  between operations  14.5 us (2%)
    psum x1, waiting for transfers between devices, per_device(): diag_all, off_all = lax.psum((diag_part, off_part), 'cells')  261 us
    all_to_all x1, waiting for transfers between devices, per_device(): lax.all_to_all(sent_x, 'genes', split_axis=1, concat_axis=1, tiled=True)  161 us
    all_to_all x1, waiting for transfers between devices, per_device(): lax.all_to_all(sent_y, 'genes', split_axis=1, concat_axis=1, tiled=True)  115 us
    dot_general x1, matrix products, partials(): jnp.einsum('cjkb,cje->jkbe', far_y, own_x, precision=highest)  24.8 us
    dot_general x1, matrix products, partials(): off_part = jnp.einsum('cjkb,cje->jkbe', far_x, own_y, precision=highest)  24.7 us
    all_to_all x1, starting transfers between devices, per_device(): lax.all_to_all(sent_y, 'genes', split_axis=1, concat_axis=1, tiled=True)  19.5 us
  transfers between devices with their start and end apart: 3, of which 3 were waited for; matrix products, arithmetic and copies ran while one was open for 5% of the time, Pallas kernels for 0%

commit v1 on v0

v1 whole, which is shorter than its diff:
```python
import functools

import jax
import jax.numpy as jnp
from jax import lax
from jax.experimental import pallas as pl
from jax.experimental.pallas import tpu as pltpu
from jax.sharding import PartitionSpec as P

PLANE = 16
MOST = 2
SIZES = (64, 64, 32)
X_ORDER = (2, 0, 1)
Y_ORDER = (0, 1, 2)
STEP = 0.5
LIMIT = STEP * 0.04


def halves(values):
    high = values.astype(jnp.bfloat16)
    low = (values - high.astype(jnp.float32)).astype(jnp.bfloat16)
    return high, low


def dot(left, right):
    return jnp.dot(left, right, preferred_element_type=jnp.float32)


def shrink(values):
    return values - jnp.clip(values, -LIMIT, LIMIT)


def pack_kernel(index, own, other, out, sem):
    n, slots = own.shape[0], out.shape[0] * out.shape[1]
    width = out.shape[3]

    @pl.loop(0, slots)
    def _(i):
        b = index[i]
        cols = pl.ds(pl.multiple_of((b % 8) * width, width), width)
        to = out.at[i // 4, i % 4]

        @pl.when(b < 8)
        def _():
            pltpu.make_async_copy(own.at[:, cols], to, sem).start()

        @pl.when(b >= 8)
        def _():
            pltpu.make_async_copy(other.at[:, cols], to, sem).start()

    pltpu.make_async_copy(out, out, sem).wait()


def pack(index, own, other):
    n, width = own.shape[0], 256
    return pl.pallas_call(
        pack_kernel,
        out_shape=jax.ShapeDtypeStruct((PLANE, 4, n, width), jnp.float32),
        in_specs=[
            pl.BlockSpec(memory_space=pltpu.SMEM),
            pl.BlockSpec(memory_space=pltpu.VMEM),
            pl.BlockSpec(memory_space=pltpu.VMEM),
        ],
        out_specs=pl.BlockSpec(memory_space=pl.ANY),
        scratch_shapes=[pltpu.SemaphoreType.DMA],
        compiler_params=pltpu.CompilerParams(vmem_limit_bytes=8 << 20),
        cost_estimate=pl.CostEstimate(
            flops=0, bytes_accessed=PLANE * 4 * n * width * 4, transcendentals=0
        ),
    )(index, own, other)


def share_kernel(pick, came, own, *refs):
    outs, sem = refs[:4], refs[4]
    width = came.shape[2]
    me = pick[48]
    for flip in range(4):
        place = me ^ flip

        @pl.loop(0, 2)
        def _(jj):
            col = place * 2 + jj
            for k in range(6):
                pltpu.make_async_copy(
                    came.at[pick[col * 6 + k]], outs[flip].at[jj * 7 + k], sem
                ).start()
            cols = pl.ds(pl.multiple_of(col * width, width), width)
            pltpu.make_async_copy(own.at[:, cols], outs[flip].at[jj * 7 + 6], sem).start()

    for flip in range(4):
        pltpu.make_async_copy(outs[flip], outs[flip], sem).wait()


def share(pick, came, own):
    n, width = own.shape[0], 256
    part = jax.ShapeDtypeStruct((14, n, width), jnp.float32)
    parts = pl.pallas_call(
        share_kernel,
        out_shape=[part] * 4,
        in_specs=[
            pl.BlockSpec(memory_space=pltpu.SMEM),
            pl.BlockSpec(memory_space=pl.ANY),
            pl.BlockSpec(memory_space=pl.ANY),
        ],
        out_specs=[pl.BlockSpec(memory_space=pl.ANY)] * 4,
        scratch_shapes=[pltpu.SemaphoreType.DMA],
        cost_estimate=pl.CostEstimate(
            flops=0, bytes_accessed=2 * 56 * n * width * 4, transcendentals=0
        ),
    )(pick, came, own)
    flipped = [
        lax.ppermute(parts[flip], "cells", [(c, c ^ flip) for c in range(4)])
        for flip in (2, 3, 1)
    ]
    return [parts[0]] + flipped


def product_kernel(pick, own, f0, f1, f2, f3, f4, f5, diag, offd, out):
    n = own.shape[0]
    total = jnp.zeros(out.shape, jnp.float32)
    for k, far in enumerate((f0, f1, f2, f3, f4, f5, None)):
        block = own[...] if far is None else far[0]
        weight = diag[0] if far is None else offd[0, k]
        high, low = halves(block)
        w_high, w_low = halves(weight)
        both = dot(jnp.concatenate([high, low], axis=0), w_high)
        total += both[:n] + both[n:] + dot(high, w_low)
    out[...] = total


def product(pick, own, came, diag, offd):
    n, width = own.shape[0], 256

    def far(k):
        return pl.BlockSpec((1, n, width), lambda j, pick: (pick[j * 6 + k], 0, 0))

    return pl.pallas_call(
        product_kernel,
        out_shape=jax.ShapeDtypeStruct(own.shape, jnp.float32),
        grid_spec=pltpu.PrefetchScalarGridSpec(
            num_scalar_prefetch=1,
            grid=(8,),
            in_specs=[pl.BlockSpec((n, width), lambda j, pick: (0, j))]
            + [far(k) for k in range(6)]
            + [
                pl.BlockSpec((1, width, width), lambda j, pick: (j, 0, 0)),
                pl.BlockSpec((1, 6, width, width), lambda j, pick: (j, 0, 0, 0)),
            ],
            out_specs=pl.BlockSpec((n, width), lambda j, pick: (0, j)),
        ),
        compiler_params=pltpu.CompilerParams(vmem_limit_bytes=24 << 20),
        cost_estimate=pl.CostEstimate(
            flops=2 * 3 * 56 * n * width * width,
            bytes_accessed=56 * width * width * 4 + 64 * n * width * 4,
            transcendentals=0,
        ),
    )(pick, own, came, came, came, came, came, came, diag, offd)


def step_kernel(parts, me, *refs):
    far_x, far_y = refs[:parts], refs[parts : 2 * parts]
    own_x, own_y = refs[2 * parts : 3 * parts], refs[3 * parts : 4 * parts]
    diag, offd, new_diag, new_offd, left_high, left_low = refs[4 * parts :]
    k = pl.program_id(1)
    scale = 1.0 / (2.0 * 640)
    width = 256

    @pl.when(k == 0)
    def _():
        at = 0
        for group in (own_y, own_x):
            for ref in group:
                high, low = halves(ref[0].T)
                n = ref.shape[1]
                left_high[:, at : at + n] = high
                left_low[:, at : at + n] = low
                at += n

    @pl.when(k < 6)
    def _():
        right = jnp.concatenate([ref[0] for ref in far_x + far_y], axis=0)
        high, low = halves(right)
        total = dot(left_high[...], high) + dot(left_low[...], high) + dot(left_high[...], low)
        new_offd[0, 0] = shrink(offd[0, 0] - (STEP * scale) * total.T)

    @pl.when(k == 6)
    def _():
        cells = left_high.shape[1] // 2
        right = jnp.concatenate([ref[0] for ref in own_x], axis=0)
        high, low = halves(right)
        y_high, y_low = left_high[:, :cells], left_low[:, :cells]
        total = dot(y_high, high) + dot(y_low, high) + dot(y_high, low)
        total = total + total.T
        eye = lax.broadcasted_iota(jnp.int32, (width, width), 0) == lax.broadcasted_iota(
            jnp.int32, (width, width), 1
        )
        old = diag[0]
        moved = old - STEP * (total * scale - jnp.where(eye, 1.0 / old, 0.0))
        new_diag[0] = jnp.where(eye, moved, shrink(moved))


def step(me, xs, ys, diag, offd):
    width, parts = 256, len(xs)

    def far(a):
        return pl.BlockSpec((1, a.shape[1], width), lambda j, k, me: (j * 7 + jnp.minimum(k, 5), 0, 0))

    def own(a):
        return pl.BlockSpec((1, a.shape[1], width), lambda j, k, me: (j * 7 + 6, 0, 0))

    return pl.pallas_call(
        functools.partial(step_kernel, parts),
        out_shape=[
            jax.ShapeDtypeStruct((2, width, width), jnp.float32),
            jax.ShapeDtypeStruct((2, 6, width, width), jnp.float32),
        ],
        grid_spec=pltpu.PrefetchScalarGridSpec(
            num_scalar_prefetch=1,
            grid=(2, 7),
            in_specs=[far(a) for a in xs]
            + [far(a) for a in ys]
            + [own(a) for a in xs]
            + [own(a) for a in ys]
            + [
                pl.BlockSpec((1, width, width), lambda j, k, me: (me[0] * 2 + j, 0, 0)),
                pl.BlockSpec(
                    (1, 1, width, width),
                    lambda j, k, me: (me[0] * 2 + j, jnp.minimum(k, 5), 0, 0),
                ),
            ],
            out_specs=[
                pl.BlockSpec((1, width, width), lambda j, k, me: (j, 0, 0)),
                pl.BlockSpec((1, 1, width, width), lambda j, k, me: (j, jnp.minimum(k, 5), 0, 0)),
            ],
            scratch_shapes=[
                pltpu.VMEM((width, 1280), jnp.bfloat16),
                pltpu.VMEM((width, 1280), jnp.bfloat16),
            ],
        ),
        compiler_params=pltpu.CompilerParams(vmem_limit_bytes=40 << 20),
        cost_estimate=pl.CostEstimate(
            flops=2 * 3 * 26 * 640 * width * width,
            bytes_accessed=28 * 640 * width * 4 + 28 * width * width * 4,
            transcendentals=0,
        ),
    )(me, *xs, *ys, *xs, *ys, diag, offd)


def tables(omega_src, omega_off):
    here = lax.axis_index("genes")
    cols = lax.broadcasted_iota(jnp.int32, omega_src.shape, 0)
    bump = jnp.logical_and(omega_src == cols // 8, omega_off >= cols % 8).astype(jnp.int32)
    block = (omega_off + bump).reshape(32, 48)
    src = omega_src.reshape(32, 48)
    earlier = lax.broadcasted_iota(jnp.int32, (48, 48), 0) > lax.broadcasted_iota(
        jnp.int32, (48, 48), 1
    )
    same = jnp.logical_and(src[:, :, None] == src[:, None, :], earlier[None])
    rank = jnp.sum(same.astype(jnp.int32), axis=2)
    y_hi = here % 2
    to_src = lax.dynamic_index_in_dim(src.reshape(PLANE, 2, 48), y_hi, 1, keepdims=False)
    to_rank = lax.dynamic_index_in_dim(rank.reshape(PLANE, 2, 48), y_hi, 1, keepdims=False)
    to_block = lax.dynamic_index_in_dim(block.reshape(PLANE, 2, 48), y_hi, 1, keepdims=False)
    slot = lax.broadcasted_iota(jnp.int32, (1, 4, 1), 1)
    source = (here // 2) * 2 + slot // 2
    match = jnp.logical_and(to_src[:, None, :] == source, to_rank[:, None, :] == slot % 2)
    send = jnp.sum(match.astype(jnp.int32) * to_block[:, None, :], axis=2)
    send = send + jnp.where(slot[:, :, 0] // 2 == y_hi, 0, 8)
    mine = lax.dynamic_index_in_dim(src, here, 0, keepdims=False)
    mine_rank = lax.dynamic_index_in_dim(rank, here, 0, keepdims=False)
    return send.reshape(-1), mine * MOST + mine_rank


def per_device(expression, omega_diag, omega_offd, omega_src, omega_off):
    me = lax.axis_index("cells").astype(jnp.int32)
    send, pick = tables(omega_src, omega_off)
    pick = jnp.concatenate([pick, me[None]])
    swap = [(g, g ^ 1) for g in range(32)]
    planes = [[p * 2 + y for p in range(PLANE)] for y in range(2)]

    def exchange(own):
        other = lax.ppermute(own, "genes", swap)
        sent = pack(send, own, other)
        came = lax.all_to_all(sent, "genes", 0, 0, axis_index_groups=planes)
        return came.reshape(PLANE * 4, own.shape[0], 256)

    starts = [sum(SIZES[:i]) for i in range(len(SIZES))]
    own_x = {i: lax.slice_in_dim(expression, starts[i], starts[i] + SIZES[i], axis=0) for i in X_ORDER}
    came_x = {i: exchange(own_x[i]) for i in X_ORDER}
    own_y = {i: product(pick, own_x[i], came_x[i], omega_diag, omega_offd) for i in X_ORDER}
    came_y = {i: exchange(own_y[i]) for i in Y_ORDER}
    xs, ys = [], []
    for i in Y_ORDER:
        xs += share(pick, came_x[i], own_x[i])
        ys += share(pick, came_y[i], own_y[i])
    return tuple(step(me[None], xs, ys, omega_diag, omega_offd))


def solution(mesh):
    return jax.shard_map(
        per_device,
        mesh=mesh,
        in_specs=(
            P("cells", "genes"),
            P("genes", None, None),
            P("genes", None, None, None),
            P(),
            P(),
        ),
        out_specs=(P(("genes", "cells"), None, None), P(("genes", "cells"), None, None, None)),
        check_vma=False,
    )
```

time: 746 us -> 951 us (1.27)
  Pallas kernels: 0 us -> 622 us
  waiting for transfers between devices: 537 us -> 199 us
  matrix products: 71.7 us -> 0 us
  starting transfers between devices: 41.7 us -> 85.7 us
  other arithmetic: 41.8 us -> 1.99 us
  between operations: 14.5 us -> 1.37 us
    pallas_call x0 -> x16, Pallas kernels: none -> 622 us  [the longest x6 567 us: share(): pl.pallas_call(share_kernel, out_shape=[part] * 4, in_specs=[pl.BlockSpec...]
    psum x1 -> x0, waiting for transfers between devices: 261 us -> none  [per_device(): diag_all, off_all = lax.psum((diag_part, off_part), 'cells')]
    all_to_all x2 -> x6, waiting for transfers between devices: 276 us -> 102 us  [exchange(): came = lax.all_to_all(sent, 'genes', 0, 0, axis_index_groups=planes)]
    ppermute x0 -> x24, waiting for transfers between devices: none -> 97.4 us  [the longest x18 59.4 us: share(): lax.ppermute(parts[flip], 'cells', [(c, c ^ flip) for c in range(4)])]
    dot_general x5 -> x0, matrix products: 71.7 us -> none  [the longest x1 24.8 us: partials(): jnp.einsum('cjkb,cje->jkbe', far_y, own_x, precision=highest)]
    ppermute x0 -> x24, starting transfers between devices: none -> 35.1 us  [the longest x6 18.8 us: exchange(): other = lax.ppermute(own, 'genes', swap)]
    unnamed x10 -> x69, local copies, waits for them, and re-layouts: 3.93 us -> 35.3 us
    select_n x7 -> x1, other arithmetic: 29.7 us -> 0.01 us  [tables(): send = send + jnp.where(slot[:, :, 0] // 2 == y_hi, 0, 8)]
  transfers between devices with their start and end apart: 3 -> 30, of which waited for: 3 -> 14; matrix products, arithmetic and copies ran while one was open for 5% -> 1% of each run, Pallas kernels for 0% -> 62%
where the time goes in v1:
time: 951 us; the launch traced here: 949 us
  Pallas kernels  622 us (65%)
  waiting for transfers between devices  199 us (21%)
  starting transfers between devices  85.7 us (9%)
  local copies, waits for them, and re-layouts  38.2 us (4%)
    pallas_call x6, Pallas kernels, share(): pl.pallas_call(share_kernel, out_shape=[part] * 4, in_specs=[pl.BlockSpec...  567 us
    all_to_all x6, waiting for transfers between devices, exchange(): came = lax.all_to_all(sent, 'genes', 0, 0, axis_index_groups=planes)  102 us
    ppermute x18, waiting for transfers between devices, share(): lax.ppermute(parts[flip], 'cells', [(c, c ^ flip) for c in range(4)])  59.4 us
    all_to_all x6, starting transfers between devices, exchange(): came = lax.all_to_all(sent, 'genes', 0, 0, axis_index_groups=planes)  50.6 us
    ppermute x6, waiting for transfers between devices, exchange(): other = lax.ppermute(own, 'genes', swap)  38 us
    unnamed x69, local copies, waits for them, and re-layouts  35.3 us
    pallas_call x1, Pallas kernels, step(): pl.pallas_call(functools.partial(step_kernel, parts), out_shape=[jax.Shap...  20.6 us
  transfers between devices with their start and end apart: 30, of which 14 were waited for; matrix products, arithmetic and copies ran while one was open for 1% of the time, Pallas kernels for 62%

profile of v1, /device:TPU:1, one launch (start us, length us, event | category | flops | bytes accessed | tf_op | source)
XLA Modules:
  0.0 948.7 jit_solution(15235403720599001427)
XLA Ops:
  1.6 3.8 collective-permute-start.8
  8.9 2.3 collective-permute-done.8.other
  11.2 2.7 shard_map.72
  13.9 1.3 copy-done.12
  15.2 7.6 all-to-all-start.2
  22.9 25.5 %all-to-all-done.2 = f32[16,4,32,256]{3,2,1,0:T(8,128)S(1)} async-done(((f32[16,4,32,256]{3,2,1,0:T(8,128)}), f32[16,4,32,256]{3,2,1,0:T(8,128)S(1)}, u32[]{:S(2)}, u32[]{:S(2)}) %all-to-all-start.2) | async-done | bytes 2097184 | tf_op jit(solution)/shard_map/all_to_all | solution.py:284
  48.4 5.3 copy-done
  53.8 1.6 copy-done.4
  55.3 4.1 shard_map.80.own
  59.5 3.0 collective-permute-start.20
  62.5 3.8 collective-permute-done.20.other
  66.3 2.3 shard_map.81
  69.3 6.4 all-to-all-start.5
  75.7 1.3 fusion.7
  77.1 3.0 collective-permute-start
  80.0 8.4 collective-permute-done.other
  88.4 2.8 shard_map.68
  91.2 1.9 copy-done.8
  93.2 7.6 all-to-all-done.5
  100.8 6.0 all-to-all-start
  106.8 3.0 collective-permute-start.4
  109.8 7.3 collective-permute-done.4.other
  117.1 2.8 shard_map.70
  119.9 1.9 copy-done.9
  121.9 32.9 %all-to-all-done = f32[16,4,64,256]{3,2,1,0:T(8,128)} async-done(((f32[16,4,64,256]{3,2,1,0:T(8,128)}), f32[16,4,64,256]{3,2,1,0:T(8,128)}, u32[]{:S(2)}, u32[]{:S(2)}) %all-to-all-start) | async-done | bytes 4194336 | tf_op jit(solution)/shard_map/all_to_all | solution.py:284
  154.7 9.7 %all-to-all-start.1 = ((f32[16,4,64,256]{3,2,1,0:T(8,128)}), f32[16,4,64,256]{3,2,1,0:T(8,128)}, u32[]{:S(2)}, u32[]{:S(2)}) async-start(f32[16,4,64,256]{3,2,1,0:T(8,128)} %copy-done.9), calls=%async_computation.1 | async-start | bytes 8388608 | tf_op jit(solution)/shard_map/all_to_all | solution.py:284
  164.4 4.6 copy-done.1
  169.0 7.3 shard_map.74.own
  176.3 3.0 collective-permute-start.12
  179.3 8.3 collective-permute-done.12.other
  187.6 2.8 shard_map.75
  190.4 1.9 copy-done.7
  193.1 17.3 %all-to-all-done.1 = f32[16,4,64,256]{3,2,1,0:T(8,128)} async-done(((f32[16,4,64,256]{3,2,1,0:T(8,128)}), f32[16,4,64,256]{3,2,1,0:T(8,128)}, u32[]{:S(2)}, u32[]{:S(2)}) %all-to-all-start.1) | async-done | bytes 4194336 | tf_op jit(solution)/shard_map/all_to_all | solution.py:284
  210.3 10.4 %all-to-all-start.3 = ((f32[16,4,64,256]{3,2,1,0:T(8,128)}), f32[16,4,64,256]{3,2,1,0:T(8,128)}, u32[]{:S(2)}, u32[]{:S(2)}) async-start(f32[16,4,64,256]{3,2,1,0:T(8,128)} %copy-done.7), calls=%async_computation.3 | async-start | bytes 8388608 | tf_op jit(solution)/shard_map/all_to_all | solution.py:284
  220.8 4.6 copy-done.2
  225.3 7.3 shard_map.77.own
  232.7 3.0 collective-permute-start.16
  235.7 7.9 collective-permute-done.16.other
  243.6 2.8 shard_map.78
  246.4 2.1 copy-done.6
  248.4 18.7 %all-to-all-done.3 = f32[16,4,64,256]{3,2,1,0:T(8,128)} async-done(((f32[16,4,64,256]{3,2,1,0:T(8,128)}), f32[16,4,64,256]{3,2,1,0:T(8,128)}, u32[]{:S(2)}, u32[]{:S(2)}) %all-to-all-start.3) | async-done | bytes 4194336 | tf_op jit(solution)/shard_map/all_to_all | solution.py:284
  267.1 10.5 %all-to-all-start.4 = ((f32[16,4,64,256]{3,2,1,0:T(8,128)}), f32[16,4,64,256]{3,2,1,0:T(8,128)}, u32[]{:S(2)}, u32[]{:S(2)}) async-start(f32[16,4,64,256]{3,2,1,0:T(8,128)} %copy-done.6), calls=%async_computation.4 | async-start | bytes 8388608 | tf_op jit(solution)/shard_map/all_to_all | solution.py:284
  277.7 57.4 %shard_map.73 = (f32[14,32,256]{2,1,0:T(8,128)}, f32[14,32,256]{2,1,0:T(8,128)}, f32[14,32,256]{2,1,0:T(8,128)}, f32[14,32,256]{2,1,0:T(8,128)}) custom-call(s32[49]{0:T(128)} %copy-done.28, f32[64,32,256]{2,1,0:T(8,128)} %bitcast.19, f32[32,2048]{1,0:T(8,128)} %copy-done.15), custom_call_target="tpu_custom_call" | custom-call | bytes 3670016 | tf_op jit(solution)/shard_map/pallas_call | solution.py:97
  335.1 1.4 collective-permute-start.9
  336.4 4.0 collective-permute-start.10
  340.5 113.0 %shard_map.69 = (f32[14,64,256]{2,1,0:T(8,128)}, f32[14,64,256]{2,1,0:T(8,128)}, f32[14,64,256]{2,1,0:T(8,128)}, f32[14,64,256]{2,1,0:T(8,128)}) custom-call(s32[49]{0:T(128)} %copy-done.28, f32[64,64,256]{2,1,0:T(8,128)} %bitcast.6.came.f0.f1.f2.f3.f4.f5, f32[64,2048]{1,0:T(8,128)} %copy-done.11), custom_call_target="tpu_custom_call" | custom-call | bytes 7340032 | tf_op jit(solution)/shard_map/pallas_call | solution.py:97
  453.4 1.4 collective-permute-start.1
  455.6 57.4 %shard_map.82 = (f32[14,32,256]{2,1,0:T(8,128)}, f32[14,32,256]{2,1,0:T(8,128)}, f32[14,32,256]{2,1,0:T(8,128)}, f32[14,32,256]{2,1,0:T(8,128)}) custom-call(s32[49]{0:T(128)} %copy-done.28, f32[64,32,256]{2,1,0:T(8,128)} %bitcast.20, f32[32,2048]{1,0:T(8,128)} %copy-done.19), custom_call_target="tpu_custom_call" | custom-call | bytes 3670016 | tf_op jit(solution)/shard_map/pallas_call | solution.py:97
  513.0 1.4 collective-permute-start.21
  515.0 113.0 %shard_map.71 = (f32[14,64,256]{2,1,0:T(8,128)}, f32[14,64,256]{2,1,0:T(8,128)}, f32[14,64,256]{2,1,0:T(8,128)}, f32[14,64,256]{2,1,0:T(8,128)}) custom-call(s32[49]{0:T(128)} %copy-done.28, f32[64,64,256]{2,1,0:T(8,128)} %bitcast.7.came.f0.f1.f2.f3.f4.f5, f32[64,2048]{1,0:T(8,128)} %copy-done.10), custom_call_target="tpu_custom_call" | custom-call | bytes 7340032 | tf_op jit(solution)/shard_map/pallas_call | solution.py:97
  628.0 113.1 %shard_map.76 = (f32[14,64,256]{2,1,0:T(8,128)}, f32[14,64,256]{2,1,0:T(8,128)}, f32[14,64,256]{2,1,0:T(8,128)}, f32[14,64,256]{2,1,0:T(8,128)}) custom-call(s32[49]{0:T(128)} %copy-done.28, f32[64,64,256]{2,1,0:T(8,128)} %bitcast.9.came, f32[64,2048]{1,0:T(8,128)} %copy-done.14), custom_call_target="tpu_custom_call" | custom-call | bytes 7340032 | tf_op jit(solution)/shard_map/pallas_call | solution.py:97
  741.4 1.2 collective-permute-start.5
  743.4 1.4 collective-permute-start.13
  744.7 113.0 %shard_map.79 = (f32[14,64,256]{2,1,0:T(8,128)}, f32[14,64,256]{2,1,0:T(8,128)}, f32[14,64,256]{2,1,0:T(8,128)}, f32[14,64,256]{2,1,0:T(8,128)}) custom-call(s32[49]{0:T(128)} %copy-done.28, f32[64,64,256]{2,1,0:T(8,128)} %bitcast.10.came, f32[64,2048]{1,0:T(8,128)} %copy-done.13), custom_call_target="tpu_custom_call" | custom-call | bytes 7340032 | tf_op jit(solution)/shard_map/pallas_call | solution.py:97
  858.6 1.3 collective-permute-start.17
  860.9 20.0 %collective-permute-done.14.refs_14_.refs_38_ = f32[14,64,256]{2,1,0:T(8,128)S(1)} collective-permute-done((f32[14,64,256]{2,1,0:T(8,128)}, f32[14,64,256]{2,1,0:T(8,128)S(1)}, u32[]{:S(2)}, u32[]{:S(2)}) %collective-permute-start.14) | collective-permute-done | bytes 917536 | tf_op jit(solution)/shard_map/ppermute | solution.py:112
  880.9 19.7 %collective-permute-done.17.refs_17_.refs_41_ = f32[14,64,256]{2,1,0:T(8,128)S(1)} collective-permute-done((f32[14,64,256]{2,1,0:T(8,128)}, f32[14,64,256]{2,1,0:T(8,128)S(1)}, u32[]{:S(2)}, u32[]{:S(2)}) %collective-permute-start.17) | collective-permute-done | bytes 917536 | tf_op jit(solution)/shard_map/ppermute | solution.py:112
  900.6 19.7 %collective-permute-done.18.refs_18_.refs_42_ = f32[14,64,256]{2,1,0:T(8,128)S(1)} collective-permute-done((f32[14,64,256]{2,1,0:T(8,128)}, f32[14,64,256]{2,1,0:T(8,128)S(1)}, u32[]{:S(2)}, u32[]{:S(2)}) %collective-permute-start.18) | collective-permute-done | bytes 917536 | tf_op jit(solution)/shard_map/ppermute | solution.py:112
  921.5 1.2 copy-done.17
  922.7 1.2 copy-done.18
  923.9 1.0 copy-done.22
  925.9 1.0 copy-done.26
  926.9 1.0 copy-done.27
  927.9 20.6 %shard_map.83 = (f32[2,256,256]{2,1,0:T(8,128)}, f32[2,6,256,256]{3,2,1,0:T(8,128)}) custom-call(s32[1]{0:T(128)} %bitcast.me, f32[14,64,256]{2,1,0:T(8,128)S(1)} %copy-done.16, f32[14,64,256]{2,1,0:T(8,128)S(1)} %collective-permute-done.1.refs_1_.refs_25_, f32[14,64,256]{2,1,0:T(8,128)S(1)} %collective-permute-done.2.refs_2_.refs_26_, ...), custom_call_target="tpu_custom_call" | custom-call | flops 6543114240 | bytes 25690112 | tf_op jit(solution)/shard_map/pallas_call | solution.py:211
  (103 shorter events, 12.7 us)
Async XLA Ops:
  1.6 57.9 %copy-start.15 = (f32[32,2048]{1,0:T(8,128)}, f32[32,2048]{1,0:T(8,128)S(1)}, u32[]{:S(2)}) copy-start(f32[32,2048]{1,0:T(8,128)S(1)} %slice.11.own) | copy-start | bytes 786436
  1.6 9.6 %collective-permute-start.8 = (f32[32,2048]{1,0:T(8,128)S(1)}, f32[32,2048]{1,0:T(8,128)S(1)}, u32[]{:S(2)}, u32[]{:S(2)}) collective-permute-start(f32[32,2048]{1,0:T(8,128)S(1)} %slice.11.own), channel_id=1, source_target_pairs={{0,1},{1,0},{2,3},{3,2},{4,5},{5,4},{6,7},{7,6},{8,9},{9,8},{10,11... | collective-permute-start | bytes 786440 | tf_op jit(solution)/shard_map/ppermute | solution.py:282
  13.9 1.3 copy-start.12
  15.2 33.2 %all-to-all-start.2 = ((f32[16,4,32,256]{3,2,1,0:T(8,128)}), f32[16,4,32,256]{3,2,1,0:T(8,128)S(1)}, u32[]{:S(2)}, u32[]{:S(2)}) async-start(f32[16,4,32,256]{3,2,1,0:T(8,128)} %copy-done.12), calls=%async_computation.2 | async-start | bytes 4194304 | tf_op jit(solution)/shard_map/all_to_all | solution.py:284
  22.9 197.8 %copy-start.28 = (s32[49]{0:T(128)}, s32[49]{0:T(128)S(1)}, u32[]{:S(2)}) copy-start(s32[49]{0:T(128)S(1)} %pad_add_fusion.pick) | copy-start | bytes 592
  48.4 11.1 %copy-start.3 = (f32[16,4,32,256]{3,2,1,0:T(8,128)}, f32[16,4,32,256]{3,2,1,0:T(8,128)S(1)}, u32[]{:S(2)}) copy-start(f32[16,4,32,256]{3,2,1,0:T(8,128)S(1)} %all-to-all-done.2) | copy-start | bytes 6291460
  48.4 5.3 copy-start
  53.8 1.6 copy-start.4
  59.5 6.8 collective-permute-start.20
  68.6 0.7 copy-start.19
  69.3 31.4 %all-to-all-start.5 = ((f32[16,4,32,256]{3,2,1,0:T(8,128)}), f32[16,4,32,256]{3,2,1,0:T(8,128)S(1)}, u32[]{:S(2)}, u32[]{:S(2)}) async-start(f32[16,4,32,256]{3,2,1,0:T(8,128)} %shard_map.81), calls=%async_computation.5 | async-start | bytes 4194304 | tf_op jit(solution)/shard_map/all_to_all | solution.py:284
  77.0 87.4 %copy-start.11 = (f32[64,2048]{1,0:T(8,128)}, f32[64,2048]{1,0:T(8,128)S(1)}, u32[]{:S(2)}) copy-start(f32[64,2048]{1,0:T(8,128)S(1)} %get-tuple-element.51.own) | copy-start | bytes 1572868
  77.0 143.7 %copy-start.10 = (f32[64,2048]{1,0:T(8,128)}, f32[64,2048]{1,0:T(8,128)S(1)}, u32[]{:S(2)}) copy-start(f32[64,2048]{1,0:T(8,128)S(1)} %get-tuple-element.50.own) | copy-start | bytes 1572868
  77.1 11.4 %collective-permute-start = (f32[64,2048]{1,0:T(8,128)S(1)}, f32[64,2048]{1,0:T(8,128)S(1)}, u32[]{:S(2)}, u32[]{:S(2)}) collective-permute-start(f32[64,2048]{1,0:T(8,128)S(1)} %get-tuple-element.51.own), channel_id=1, source_target_pairs={{0,1},{1,0},{2,3},{3,2},{4,5},{5,4},{6,7},{7,6},{8,9},{9,8},{10,11... | collective-permute-start | bytes 1572872 | tf_op jit(solution)/shard_map/ppermute | solution.py:282
  91.2 1.9 copy-start.8
  100.8 6.0 copy-start.29
  100.8 53.9 %all-to-all-start = ((f32[16,4,64,256]{3,2,1,0:T(8,128)}), f32[16,4,64,256]{3,2,1,0:T(8,128)}, u32[]{:S(2)}, u32[]{:S(2)}) async-start(f32[16,4,64,256]{3,2,1,0:T(8,128)} %copy-done.8), calls=%async_computation | async-start | bytes 8388608 | tf_op jit(solution)/shard_map/all_to_all | solution.py:284
  106.8 10.3 %collective-permute-start.4 = (f32[64,2048]{1,0:T(8,128)S(1)}, f32[64,2048]{1,0:T(8,128)S(1)}, u32[]{:S(2)}, u32[]{:S(2)}) collective-permute-start(f32[64,2048]{1,0:T(8,128)S(1)} %get-tuple-element.50.own), channel_id=1, source_target_pairs={{0,1},{1,0},{2,3},{3,2},{4,5},{5,4},{6,7},{7,6},{8,9},{9,8},{10,11... | collective-permute-start | bytes 1572872 | tf_op jit(solution)/shard_map/ppermute | solution.py:282
  119.9 2.0 copy-start.9
  121.9 42.6 %copy-start.5 = (f32[8,256,256]{2,1,0:T(8,128)S(1)}, f32[8,256,256]{2,1,0:T(8,128)}, u32[]{:S(2)}) copy-start(f32[8,256,256]{2,1,0:T(8,128)} %refs_48_.1) | copy-start | bytes 6291460
  154.7 55.6 %all-to-all-start.1 = ((f32[16,4,64,256]{3,2,1,0:T(8,128)}), f32[16,4,64,256]{3,2,1,0:T(8,128)}, u32[]{:S(2)}, u32[]{:S(2)}) async-start(f32[16,4,64,256]{3,2,1,0:T(8,128)} %copy-done.9), calls=%async_computation.1 | async-start | bytes 8388608 | tf_op jit(solution)/shard_map/all_to_all | solution.py:284
  164.4 4.6 copy-start.1
  176.3 11.2 %collective-permute-start.12 = (f32[64,2048]{1,0:T(8,128)S(1)}, f32[64,2048]{1,0:T(8,128)S(1)}, u32[]{:S(2)}, u32[]{:S(2)}) collective-permute-start(f32[64,2048]{1,0:T(8,128)S(1)} %shard_map.74.own), channel_id=1, source_target_pairs={{0,1},{1,0},{2,3},{3,2},{4,5},{5,4},{6,7},{7,6},{8,9},{9,8},{10,11... | collective-permute-start | bytes 1572872 | tf_op jit(solution)/shard_map/ppermute | solution.py:282
  190.4 1.9 copy-start.7
  192.3 0.8 copy-start.14
  210.3 56.8 %all-to-all-start.3 = ((f32[16,4,64,256]{3,2,1,0:T(8,128)}), f32[16,4,64,256]{3,2,1,0:T(8,128)}, u32[]{:S(2)}, u32[]{:S(2)}) async-start(f32[16,4,64,256]{3,2,1,0:T(8,128)} %copy-done.7), calls=%async_computation.3 | async-start | bytes 8388608 | tf_op jit(solution)/shard_map/all_to_all | solution.py:284
  220.7 4.6 copy-start.2
  232.7 34.5 %copy-start.13 = (f32[64,2048]{1,0:T(8,128)}, f32[64,2048]{1,0:T(8,128)S(1)}, u32[]{:S(2)}) copy-start(f32[64,2048]{1,0:T(8,128)S(1)} %shard_map.77.own) | copy-start | bytes 1572868
  232.7 10.9 %collective-permute-start.16 = (f32[64,2048]{1,0:T(8,128)S(1)}, f32[64,2048]{1,0:T(8,128)S(1)}, u32[]{:S(2)}, u32[]{:S(2)}) collective-permute-start(f32[64,2048]{1,0:T(8,128)S(1)} %shard_map.77.own), channel_id=1, source_target_pairs={{0,1},{1,0},{2,3},{3,2},{4,5},{5,4},{6,7},{7,6},{8,9},{9,8},{10,11... | collective-permute-start | bytes 1572872 | tf_op jit(solution)/shard_map/ppermute | solution.py:282
  246.4 2.1 copy-start.6
  267.1 477.6 %all-to-all-start.4 = ((f32[16,4,64,256]{3,2,1,0:T(8,128)}), f32[16,4,64,256]{3,2,1,0:T(8,128)}, u32[]{:S(2)}, u32[]{:S(2)}) async-start(f32[16,4,64,256]{3,2,1,0:T(8,128)} %copy-done.6), calls=%async_computation.4 | async-start | bytes 8388608 | tf_op jit(solution)/shard_map/all_to_all | solution.py:284
  335.1 178.0 %collective-permute-start.9 = (f32[14,32,256]{2,1,0:T(8,128)}, f32[14,32,256]{2,1,0:T(8,128)S(1)}, u32[]{:S(2)}, u32[]{:S(2)}) collective-permute-start(f32[14,32,256]{2,1,0:T(8,128)} %get-tuple-element.35), channel_id=1, source_target_pairs={{0,64},{32,96},{64,0},{96,32},{1,65},{33,97},{65,1},{97,33},{2,66}... | collective-permute-start | bytes 1376264 | tf_op jit(solution)/shard_map/ppermute | solution.py:112
  336.4 178.0 %collective-permute-start.10 = (f32[14,32,256]{2,1,0:T(8,128)}, f32[14,32,256]{2,1,0:T(8,128)S(1)}, u32[]{:S(2)}, u32[]{:S(2)}) collective-permute-start(f32[14,32,256]{2,1,0:T(8,128)} %get-tuple-element.36), channel_id=1, source_target_pairs={{0,96},{32,64},{64,32},{96,0},{1,97},{33,65},{65,33},{97,1},{2,98}... | collective-permute-start | bytes 1376264 | tf_op jit(solution)/shard_map/ppermute | solution.py:112
  340.5 174.2 %collective-permute-start.11 = (f32[14,32,256]{2,1,0:T(8,128)}, f32[14,32,256]{2,1,0:T(8,128)S(1)}, u32[]{:S(2)}, u32[]{:S(2)}) collective-permute-start(f32[14,32,256]{2,1,0:T(8,128)} %get-tuple-element.37), channel_id=1, source_target_pairs={{0,32},{32,0},{64,96},{96,64},{1,33},{33,1},{65,97},{97,65},{2,34}... | collective-permute-start | bytes 1376264 | tf_op jit(solution)/shard_map/ppermute | solution.py:112
  453.4 289.9 %collective-permute-start.1 = (f32[14,64,256]{2,1,0:T(8,128)}, f32[14,64,256]{2,1,0:T(8,128)S(1)}, u32[]{:S(2)}, u32[]{:S(2)}) collective-permute-start(f32[14,64,256]{2,1,0:T(8,128)} %get-tuple-element.27), channel_id=1, source_target_pairs={{0,64},{32,96},{64,0},{96,32},{1,65},{33,97},{65,1},{97,33},{2,66}... | collective-permute-start | bytes 2752520 | tf_op jit(solution)/shard_map/ppermute | solution.py:112
  454.8 288.6 %collective-permute-start.2 = (f32[14,64,256]{2,1,0:T(8,128)}, f32[14,64,256]{2,1,0:T(8,128)S(1)}, u32[]{:S(2)}, u32[]{:S(2)}) collective-permute-start(f32[14,64,256]{2,1,0:T(8,128)} %get-tuple-element.28), channel_id=1, source_target_pairs={{0,96},{32,64},{64,32},{96,0},{1,97},{33,65},{65,33},{97,1},{2,98}... | collective-permute-start | bytes 2752520 | tf_op jit(solution)/shard_map/ppermute | solution.py:112
  513.0 114.9 %copy-start.21 = (f32[14,32,256]{2,1,0:T(8,128)}, f32[14,32,256]{2,1,0:T(8,128)S(1)}, u32[]{:S(2)}) copy-start(f32[14,32,256]{2,1,0:T(8,128)S(1)} %collective-permute-done.9.refs_9_.refs_33_) | copy-start | bytes 1376260
  513.0 228.1 %collective-permute-start.21 = (f32[14,32,256]{2,1,0:T(8,128)}, f32[14,32,256]{2,1,0:T(8,128)}, u32[]{:S(2)}, u32[]{:S(2)}) collective-permute-start(f32[14,32,256]{2,1,0:T(8,128)} %get-tuple-element.47), channel_id=1, source_target_pairs={{0,64},{32,96},{64,0},{96,32},{1,65},{33,97},{65,1},{97,33},{2,66}... | collective-permute-start | bytes 1376264 | tf_op jit(solution)/shard_map/ppermute | solution.py:112
  514.4 113.5 %copy-start.23 = (f32[14,32,256]{2,1,0:T(8,128)}, f32[14,32,256]{2,1,0:T(8,128)S(1)}, u32[]{:S(2)}) copy-start(f32[14,32,256]{2,1,0:T(8,128)S(1)} %collective-permute-done.10.refs_10_.refs_34_) | copy-start | bytes 1376260
  514.4 227.0 %collective-permute-start.22 = (f32[14,32,256]{2,1,0:T(8,128)}, f32[14,32,256]{2,1,0:T(8,128)}, u32[]{:S(2)}, u32[]{:S(2)}) collective-permute-start(f32[14,32,256]{2,1,0:T(8,128)} %get-tuple-element.48), channel_id=1, source_target_pairs={{0,96},{32,64},{64,32},{96,0},{1,97},{33,65},{65,33},{97,1},{2,98}... | collective-permute-start | bytes 1376264 | tf_op jit(solution)/shard_map/ppermute | solution.py:112
  514.7 113.3 %copy-start.25 = (f32[14,32,256]{2,1,0:T(8,128)}, f32[14,32,256]{2,1,0:T(8,128)S(1)}, u32[]{:S(2)}) copy-start(f32[14,32,256]{2,1,0:T(8,128)S(1)} %collective-permute-done.11.refs_11_.refs_35_) | copy-start | bytes 1376260
  514.7 227.9 %collective-permute-start.23 = (f32[14,32,256]{2,1,0:T(8,128)}, f32[14,32,256]{2,1,0:T(8,128)}, u32[]{:S(2)}, u32[]{:S(2)}) collective-permute-start(f32[14,32,256]{2,1,0:T(8,128)} %get-tuple-element.49), channel_id=1, source_target_pairs={{0,32},{32,0},{64,96},{96,64},{1,33},{33,1},{65,97},{97,65},{2,34}... | collective-permute-start | bytes 1376264 | tf_op jit(solution)/shard_map/ppermute | solution.py:112
  628.0 293.5 %copy-start.16 = (f32[14,64,256]{2,1,0:T(8,128)S(1)}, f32[14,64,256]{2,1,0:T(8,128)}, u32[]{:S(2)}) copy-start(f32[14,64,256]{2,1,0:T(8,128)} %get-tuple-element.26.refs_0_.refs_24_) | copy-start | bytes 2752516
  628.0 293.5 %copy-start.20 = (f32[14,32,256]{2,1,0:T(8,128)S(1)}, f32[14,32,256]{2,1,0:T(8,128)}, u32[]{:S(2)}) copy-start(f32[14,32,256]{2,1,0:T(8,128)} %get-tuple-element.34.refs_8_.refs_32_) | copy-start | bytes 1376260
  741.1 116.6 %collective-permute-start.3 = (f32[14,64,256]{2,1,0:T(8,128)}, f32[14,64,256]{2,1,0:T(8,128)}, u32[]{:S(2)}, u32[]{:S(2)}) collective-permute-start(f32[14,64,256]{2,1,0:T(8,128)} %get-tuple-element.29), channel_id=1, source_target_pairs={{0,32},{32,0},{64,96},{96,64},{1,33},{33,1},{65,97},{97,65},{2,34}... | collective-permute-start | bytes 2752520 | tf_op jit(solution)/shard_map/ppermute | solution.py:112
  741.4 117.1 %collective-permute-start.5 = (f32[14,64,256]{2,1,0:T(8,128)}, f32[14,64,256]{2,1,0:T(8,128)}, u32[]{:S(2)}, u32[]{:S(2)}) collective-permute-start(f32[14,64,256]{2,1,0:T(8,128)} %get-tuple-element.31), channel_id=1, source_target_pairs={{0,64},{32,96},{64,0},{96,32},{1,65},{33,97},{65,1},{97,33},{2,66}... | collective-permute-start | bytes 2752520 | tf_op jit(solution)/shard_map/ppermute | solution.py:112
  742.6 116.0 %collective-permute-start.6 = (f32[14,64,256]{2,1,0:T(8,128)}, f32[14,64,256]{2,1,0:T(8,128)}, u32[]{:S(2)}, u32[]{:S(2)}) collective-permute-start(f32[14,64,256]{2,1,0:T(8,128)} %get-tuple-element.32), channel_id=1, source_target_pairs={{0,96},{32,64},{64,32},{96,0},{1,97},{33,65},{65,33},{97,1},{2,98}... | collective-permute-start | bytes 2752520 | tf_op jit(solution)/shard_map/ppermute | solution.py:112
  743.4 116.6 %collective-permute-start.7 = (f32[14,64,256]{2,1,0:T(8,128)}, f32[14,64,256]{2,1,0:T(8,128)}, u32[]{:S(2)}, u32[]{:S(2)}) collective-permute-start(f32[14,64,256]{2,1,0:T(8,128)} %get-tuple-element.33), channel_id=1, source_target_pairs={{0,32},{32,0},{64,96},{96,64},{1,33},{33,1},{65,97},{97,65},{2,34}... | collective-permute-start | bytes 2752520 | tf_op jit(solution)/shard_map/ppermute | solution.py:112
  743.4 117.3 %collective-permute-start.13 = (f32[14,64,256]{2,1,0:T(8,128)}, f32[14,64,256]{2,1,0:T(8,128)}, u32[]{:S(2)}, u32[]{:S(2)}) collective-permute-start(f32[14,64,256]{2,1,0:T(8,128)} %get-tuple-element.39), channel_id=1, source_target_pairs={{0,64},{32,96},{64,0},{96,32},{1,65},{33,97},{65,1},{97,33},{2,66}... | collective-permute-start | bytes 2752520 | tf_op jit(solution)/shard_map/ppermute | solution.py:112
  857.7 23.2 %collective-permute-start.14 = (f32[14,64,256]{2,1,0:T(8,128)}, f32[14,64,256]{2,1,0:T(8,128)S(1)}, u32[]{:S(2)}, u32[]{:S(2)}) collective-permute-start(f32[14,64,256]{2,1,0:T(8,128)} %get-tuple-element.40), channel_id=1, source_target_pairs={{0,96},{32,64},{64,32},{96,0},{1,97},{33,65},{65,33},{97,1},{2,98}... | collective-permute-start | bytes 2752520 | tf_op jit(solution)/shard_map/ppermute | solution.py:112
  858.6 22.4 %collective-permute-start.15 = (f32[14,64,256]{2,1,0:T(8,128)}, f32[14,64,256]{2,1,0:T(8,128)S(1)}, u32[]{:S(2)}, u32[]{:S(2)}) collective-permute-start(f32[14,64,256]{2,1,0:T(8,128)} %get-tuple-element.41), channel_id=1, source_target_pairs={{0,32},{32,0},{64,96},{96,64},{1,33},{33,1},{65,97},{97,65},{2,34}... | collective-permute-start | bytes 2752520 | tf_op jit(solution)/shard_map/ppermute | solution.py:112
  858.6 42.0 %collective-permute-start.17 = (f32[14,64,256]{2,1,0:T(8,128)}, f32[14,64,256]{2,1,0:T(8,128)S(1)}, u32[]{:S(2)}, u32[]{:S(2)}) collective-permute-start(f32[14,64,256]{2,1,0:T(8,128)} %get-tuple-element.43), channel_id=1, source_target_pairs={{0,64},{32,96},{64,0},{96,32},{1,65},{33,97},{65,1},{97,33},{2,66}... | collective-permute-start | bytes 2752520 | tf_op jit(solution)/shard_map/ppermute | solution.py:112
  859.9 60.3 %collective-permute-start.18 = (f32[14,64,256]{2,1,0:T(8,128)}, f32[14,64,256]{2,1,0:T(8,128)S(1)}, u32[]{:S(2)}, u32[]{:S(2)}) collective-permute-start(f32[14,64,256]{2,1,0:T(8,128)} %get-tuple-element.44), channel_id=1, source_target_pairs={{0,96},{32,64},{64,32},{96,0},{1,97},{33,65},{65,33},{97,1},{2,98}... | collective-permute-start | bytes 2752520 | tf_op jit(solution)/shard_map/ppermute | solution.py:112
  860.7 59.5 %collective-permute-start.19 = (f32[14,64,256]{2,1,0:T(8,128)}, f32[14,64,256]{2,1,0:T(8,128)S(1)}, u32[]{:S(2)}, u32[]{:S(2)}) collective-permute-start(f32[14,64,256]{2,1,0:T(8,128)} %get-tuple-element.45), channel_id=1, source_target_pairs={{0,32},{32,0},{64,96},{96,64},{1,33},{33,1},{65,97},{97,65},{2,34}... | collective-permute-start | bytes 2752520 | tf_op jit(solution)/shard_map/ppermute | solution.py:112
  880.9 39.3 %copy-start.30 = (f32[14,64,256]{2,1,0:T(8,128)}, f32[14,64,256]{2,1,0:T(8,128)S(1)}, u32[]{:S(2)}) copy-start(f32[14,64,256]{2,1,0:T(8,128)S(1)} %collective-permute-done.15.refs_15_.refs_39_) | copy-start | bytes 2752516
  900.6 19.7 %copy-start.31 = (f32[14,64,256]{2,1,0:T(8,128)}, f32[14,64,256]{2,1,0:T(8,128)S(1)}, u32[]{:S(2)}) copy-start(f32[14,64,256]{2,1,0:T(8,128)S(1)} %collective-permute-done.17.refs_17_.refs_41_) | copy-start | bytes 2752516
  920.3 1.0 copy-start.32
  920.3 1.2 copy-start.33
  921.5 1.2 copy-start.17
  922.7 1.2 copy-start.18
  923.9 1.0 copy-start.22
  924.9 1.0 copy-start.24
  925.9 1.0 copy-start.26
  926.9 1.0 copy-start.27

commit v2 on v1

v2 whole, which is shorter than its diff:
```python
import functools

import jax
import jax.numpy as jnp
from jax import lax
from jax.experimental import pallas as pl
from jax.experimental.pallas import tpu as pltpu
from jax.sharding import PartitionSpec as P

PLANE = 16
MOST = 2
SIZES = (48, 40, 40, 32)
LATE = 2
FLIPS = (0, 2, 3, 1)
STEP = 0.5
LIMIT = STEP * 0.04


def halves(values):
    high = values.astype(jnp.bfloat16)
    low = (values - high.astype(jnp.float32)).astype(jnp.bfloat16)
    return high, low


def dot(left, right):
    return jnp.dot(left, right, preferred_element_type=jnp.float32)


def shrink(values):
    return values - jnp.clip(values, -LIMIT, LIMIT)


def pack_kernel(index, own, other, *refs):
    out, sem = refs[-2:]
    slots, width = out.shape[0] * out.shape[1], out.shape[3]

    @pl.loop(0, slots)
    def _(i):
        b = index[i]
        cols = pl.ds(pl.multiple_of((b % 8) * width, width), width)
        to = out.at[i // 4, i % 4]

        @pl.when(b < 8)
        def _():
            pltpu.make_async_copy(own.at[:, cols], to, sem).start()

        @pl.when(b >= 8)
        def _():
            pltpu.make_async_copy(other.at[:, cols], to, sem).start()

    pltpu.make_async_copy(out, out, sem).wait()


def pack(index, own, other, before=()):
    n, width = own.shape[0], 256
    return pl.pallas_call(
        pack_kernel,
        out_shape=pltpu.HBM((PLANE, 4, n, width), jnp.float32),
        in_specs=[
            pl.BlockSpec(memory_space=pltpu.SMEM),
            pl.BlockSpec(memory_space=pltpu.VMEM),
            pl.BlockSpec(memory_space=pltpu.VMEM),
        ]
        + [pl.BlockSpec(memory_space=pl.ANY)] * len(before),
        out_specs=pl.BlockSpec(memory_space=pltpu.HBM),
        scratch_shapes=[pltpu.SemaphoreType.DMA],
        compiler_params=pltpu.CompilerParams(vmem_limit_bytes=8 << 20),
        cost_estimate=pl.CostEstimate(
            flops=0, bytes_accessed=PLANE * 4 * n * width * 4, transcendentals=0
        ),
    )(index, own, other, *before)


def share_kernel(pick, came, *refs):
    outs, held, sem_in, sem_out = refs[-7:-3], refs[-3], refs[-2], refs[-1]
    width, each = came.shape[2], held.shape[1] // 2
    me = pick[48]
    for flip in (2, 3, 1, 0):
        place = me ^ flip

        @pl.loop(0, 2)
        def _(jj):
            col = place * 2 + jj
            for k in range(6):
                pltpu.make_async_copy(
                    came.at[pick[col * 6 + k]], held.at[flip, jj * each + k], sem_in.at[flip]
                ).start()
            if each == 7:
                cols = pl.ds(pl.multiple_of(col * width, width), width)
                pltpu.make_async_copy(
                    refs[0].at[:, cols], held.at[flip, jj * each + 6], sem_in.at[flip]
                ).start()

    for flip in (2, 3, 1, 0):
        pltpu.make_async_copy(outs[flip], held.at[flip], sem_in.at[flip]).wait()
        pltpu.make_async_copy(held.at[flip], outs[flip], sem_out.at[flip]).start()
    for flip in (2, 3, 1, 0):
        pltpu.make_async_copy(held.at[flip], outs[flip], sem_out.at[flip]).wait()


def share(pick, came, own=(), before=()):
    n, width = came.shape[1:]
    blocks = 12 + 2 * len(own)
    part = pltpu.HBM((blocks, n, width), jnp.float32)
    return pl.pallas_call(
        share_kernel,
        out_shape=[part] * 4,
        in_specs=[pl.BlockSpec(memory_space=pltpu.SMEM), pl.BlockSpec(memory_space=pl.ANY)]
        + [pl.BlockSpec(memory_space=pl.ANY)] * (len(own) + len(before)),
        out_specs=[pl.BlockSpec(memory_space=pltpu.HBM)] * 4,
        scratch_shapes=[
            pltpu.VMEM((4, blocks, n, width), jnp.float32),
            pltpu.SemaphoreType.DMA((4,)),
            pltpu.SemaphoreType.DMA((4,)),
        ],
        compiler_params=pltpu.CompilerParams(vmem_limit_bytes=12 << 20),
        cost_estimate=pl.CostEstimate(
            flops=0, bytes_accessed=8 * blocks * n * width * 4, transcendentals=0
        ),
    )(pick, came, *own, *before)


def handed(parts):
    return [
        lax.ppermute(parts[flip], "cells", [(c, c ^ flip) for c in range(4)]) if flip else parts[0]
        for flip in FLIPS
    ]


def product_kernel(pick, own, f0, f1, f2, f3, f4, f5, diag, offd, out):
    n = own.shape[0]
    total = jnp.zeros(out.shape, jnp.float32)
    for k, far in enumerate((f0, f1, f2, f3, f4, f5, None)):
        block = own[...] if far is None else far[0]
        weight = diag[0] if far is None else offd[0, k]
        high, low = halves(block)
        w_high, w_low = halves(weight)
        both = dot(jnp.concatenate([high, low], axis=0), w_high)
        total += both[:n] + both[n:] + dot(high, w_low)
    out[...] = total


def product(pick, own, came, diag, offd):
    n, width = own.shape[0], 256

    def far(k):
        return pl.BlockSpec((1, n, width), lambda j, pick: (pick[j * 6 + k], 0, 0))

    return pl.pallas_call(
        product_kernel,
        out_shape=jax.ShapeDtypeStruct(own.shape, jnp.float32),
        grid_spec=pltpu.PrefetchScalarGridSpec(
            num_scalar_prefetch=1,
            grid=(8,),
            in_specs=[pl.BlockSpec((n, width), lambda j, pick: (0, j))]
            + [far(k) for k in range(6)]
            + [
                pl.BlockSpec((1, width, width), lambda j, pick: (j, 0, 0)),
                pl.BlockSpec((1, 6, width, width), lambda j, pick: (j, 0, 0, 0)),
            ],
            out_specs=pl.BlockSpec((n, width), lambda j, pick: (0, j)),
        ),
        compiler_params=pltpu.CompilerParams(vmem_limit_bytes=56 << 20),
        cost_estimate=pl.CostEstimate(
            flops=2 * 3 * 56 * n * width * width,
            bytes_accessed=56 * width * width * 4 + 64 * n * width * 4,
            transcendentals=0,
        ),
    )(pick, own, came, came, came, came, came, came, diag, offd)


def gram_kernel(starts, last, me, *refs):
    parts = 4 * len(starts)
    far_x, ys, home = refs[:parts], refs[parts : 2 * parts], refs[2 * parts : 2 * parts + 4]
    if last:
        diag_sum, off_sum, diag, offd = refs[2 * parts + 4 : 2 * parts + 8]
    new_diag, new_offd, left_high, left_low = refs[-4:]
    cells = left_high.shape[1] // 2
    scale = 1.0 / (2.0 * 640)
    width = 256
    own_x = [
        ref[starts[i] : starts[i] + far_x[4 * i].shape[1], :]
        for i in range(len(starts))
        for ref in home
    ]
    own_x = jnp.concatenate(own_x, axis=0)
    own_y = jnp.concatenate([ref[6] for ref in ys], axis=0)
    for at, value in ((0, own_y), (cells, own_x)):
        high, low = halves(value.T)
        left_high[:, at : at + cells] = high
        left_low[:, at : at + cells] = low
    for k in range(6):
        right = jnp.concatenate([ref[k] for ref in far_x + ys], axis=0)
        high, low = halves(right)
        total = dot(left_high[...], high) + dot(left_low[...], high) + dot(left_high[...], low)
        total = total.T
        if last:
            total = shrink(offd[0, k] - (STEP * scale) * (total + off_sum[0, k]))
        new_offd[0, k] = total
    high, low = halves(own_x)
    y_high, y_low = left_high[:, :cells], left_low[:, :cells]
    total = dot(y_high, high) + dot(y_low, high) + dot(y_high, low)
    if last:
        total = total + diag_sum[0]
        total = total + total.T
        eye = lax.broadcasted_iota(jnp.int32, (width, width), 0) == lax.broadcasted_iota(
            jnp.int32, (width, width), 1
        )
        old = diag[0]
        moved = old - STEP * (total * scale - jnp.where(eye, 1.0 / old, 0.0))
        total = jnp.where(eye, moved, shrink(moved))
    new_diag[0] = total


def gram(me, starts, xs, ys, home, sums=(), old=()):
    width = 256
    cells = sum(a.shape[1] for a in xs)

    def block(a):
        return pl.BlockSpec((a.shape[0] // 2, a.shape[1], width), lambda j, me: (j, 0, 0))

    def pair(base):
        return [
            pl.BlockSpec((1, width, width), lambda j, me: (base(me) + j, 0, 0)),
            pl.BlockSpec((1, 6, width, width), lambda j, me: (base(me) + j, 0, 0, 0)),
        ]

    specs = [block(a) for a in [*xs, *ys]]
    specs += [pl.BlockSpec((a.shape[0], width), lambda j, me: (0, j)) for a in home]
    if sums:
        specs += pair(lambda me: 0) + pair(lambda me: me[0] * 2)
    return pl.pallas_call(
        functools.partial(gram_kernel, starts, bool(sums)),
        out_shape=[
            jax.ShapeDtypeStruct((2, width, width), jnp.float32),
            jax.ShapeDtypeStruct((2, 6, width, width), jnp.float32),
        ],
        grid_spec=pltpu.PrefetchScalarGridSpec(
            num_scalar_prefetch=1,
            grid=(2,),
            in_specs=specs,
            out_specs=pair(lambda me: 0),
            scratch_shapes=[pltpu.VMEM((width, 2 * cells), jnp.bfloat16)] * 2,
        ),
        compiler_params=pltpu.CompilerParams(vmem_limit_bytes=56 << 20),
        cost_estimate=pl.CostEstimate(
            flops=2 * 3 * 26 * cells * width * width,
            bytes_accessed=28 * cells * width * 4 + 28 * width * width * 4,
            transcendentals=0,
        ),
    )(me, *xs, *ys, *home, *sums, *old)


def tables(omega_src, omega_off):
    here = lax.axis_index("genes")
    cols = lax.broadcasted_iota(jnp.int32, omega_src.shape, 0)
    bump = jnp.logical_and(omega_src == cols // 8, omega_off >= cols % 8).astype(jnp.int32)
    block = (omega_off + bump).reshape(32, 48)
    src = omega_src.reshape(32, 48)
    earlier = lax.broadcasted_iota(jnp.int32, (48, 48), 0) > lax.broadcasted_iota(
        jnp.int32, (48, 48), 1
    )
    same = jnp.logical_and(src[:, :, None] == src[:, None, :], earlier[None])
    rank = jnp.sum(same.astype(jnp.int32), axis=2)
    y_hi = here % 2
    to_src = lax.dynamic_index_in_dim(src.reshape(PLANE, 2, 48), y_hi, 1, keepdims=False)
    to_rank = lax.dynamic_index_in_dim(rank.reshape(PLANE, 2, 48), y_hi, 1, keepdims=False)
    to_block = lax.dynamic_index_in_dim(block.reshape(PLANE, 2, 48), y_hi, 1, keepdims=False)
    slot = lax.broadcasted_iota(jnp.int32, (1, 4, 1), 1)
    source = (here // 2) * 2 + slot // 2
    match = jnp.logical_and(to_src[:, None, :] == source, to_rank[:, None, :] == slot % 2)
    send = jnp.sum(match.astype(jnp.int32) * to_block[:, None, :], axis=2)
    send = send + jnp.where(slot[:, :, 0] // 2 == y_hi, 0, 8)
    mine = lax.dynamic_index_in_dim(src, here, 0, keepdims=False)
    mine_rank = lax.dynamic_index_in_dim(rank, here, 0, keepdims=False)
    return send.reshape(-1), mine * MOST + mine_rank


def per_device(expression, omega_diag, omega_offd, omega_src, omega_off):
    me = lax.axis_index("cells").astype(jnp.int32)
    send, pick = tables(omega_src, omega_off)
    pick = jnp.concatenate([pick, me[None]])
    swap = [(g, g ^ 1) for g in range(32)]
    planes = [[p * 2 + y for p in range(PLANE)] for y in range(2)]

    def exchange(sent):
        came = lax.all_to_all(sent, "genes", 0, 0, axis_index_groups=planes)
        return came.reshape(PLANE * 4, sent.shape[2], 256)

    runs = range(len(SIZES))
    starts = tuple(sum(SIZES[:i]) for i in runs)
    turns = [("x", i) for i in runs] + [("y", i) for i in runs]
    own, other, shared, parts = {}, {}, {}, {}
    slices = [lax.slice_in_dim(expression, starts[i], starts[i] + SIZES[i], axis=0) for i in runs]
    own["x", 0] = slices[0]
    other["x", 0] = lax.ppermute(slices[0], "genes", swap)
    sent = pack(send, own["x", 0], other["x", 0])
    sent, expression, *slices[1:] = lax.optimization_barrier((sent, expression, *slices[1:]))
    for i in runs[1:]:
        own["x", i] = slices[i]
        other["x", i] = lax.ppermute(slices[i], "genes", swap)
    home = handed(
        [lax.dynamic_slice_in_dim(expression, (me ^ flip) * 512, 512, axis=1) for flip in range(4)]
    )

    def summed(which, *rest):
        xs, ys = ([part for i in which for part in parts[kind, i]] for kind in "xy")
        return gram(me[None], tuple(starts[i] for i in which), xs, ys, home, *rest)

    for at, turn in enumerate(turns):
        kind, i = turn
        arrived = exchange(sent)
        if at + 1 < len(turns):
            then = turns[at + 1]
            if at == 0:
                before, ties = [other["x", j] for j in runs[2:]], home[1:]
            else:
                last = turns[at - 1]
                before, ties = [shared[last][0]], [parts[last][1], parts[last][3]]
                if last[0] == "x":
                    before.append(own["y", last[1]])
            if at >= 2:
                ties.append(parts[turns[at - 2]][2])
            if at >= 1 and last[0] == "x":
                ties.append(other["y", last[1]])
            sent = pack(send, own[then], other[then], before)
            sent, arrived, *ties = lax.optimization_barrier((sent, arrived, *ties))
            if at == 0:
                home[1:] = ties
            else:
                parts[last][1], parts[last][3] = ties[:2]
            if at >= 2:
                parts[turns[at - 2]][2] = ties[2]
            if at >= 1 and last[0] == "x":
                other["y", last[1]] = ties[-1]
        if kind == "x":
            shared[turn] = share(pick, arrived)
            own["y", i] = product(pick, own[turn], arrived, omega_diag, omega_offd)
            other["y", i] = lax.ppermute(own["y", i], "genes", swap)
        else:
            before = []
            if at + 1 == len(turns):
                sums = summed(runs[:-LATE])
                before = [sums[0]]
                last = turns[at - 1]
                arrived, *parts[last] = lax.optimization_barrier((arrived, *parts[last]))
            shared[turn] = share(pick, arrived, [own[turn]], before)
        parts[turn] = handed(shared[turn])
    return tuple(summed(runs[-LATE:], sums, (omega_diag, omega_offd)))


def solution(mesh):
    return jax.shard_map(
        per_device,
        mesh=mesh,
        in_specs=(
            P("cells", "genes"),
            P("genes", None, None),
            P("genes", None, None, None),
            P(),
            P(),
        ),
        out_specs=(P(("genes", "cells"), None, None), P(("genes", "cells"), None, None, None)),
        check_vma=False,
    )
```

time: 951 us -> 406 us (0.43)
  Pallas kernels: 622 us -> 113 us
  waiting for transfers between devices: 199 us -> 153 us
  starting transfers between devices: 85.7 us -> 108 us
  local copies, waits for them, and re-layouts: 38.2 us -> 22.2 us
    pallas_call x6 -> x8, Pallas kernels: 567 us -> 32 us  [share(): pl.pallas_call(share_kernel, out_shape=[part] * 4, in_specs=[pl.BlockSpec...]
    all_to_all x6 -> x8, waiting for transfers between devices: 102 us -> 9.16 us  [exchange(): came = lax.all_to_all(sent, 'genes', 0, 0, axis_index_groups=planes)]
    ppermute x24 -> x35, waiting for transfers between devices: 97.4 us -> 144 us  [the longest x27 94.7 us: handed(): lax.ppermute(parts[flip], 'cells', [(c, c ^ flip) for c in range(4)])]
    pallas_call x3 -> x4, Pallas kernels: 18.8 us -> 43.2 us  [product(): pl.pallas_call(product_kernel, out_shape=jax.ShapeDtypeStruct(own.shape,...]
    unnamed x69 -> x117, local copies, waits for them, and re-layouts: 35.3 us -> 15.7 us
    ppermute x24 -> x35, starting transfers between devices: 35.1 us -> 49 us  [the longest x27 31.3 us: handed(): lax.ppermute(parts[flip], 'cells', [(c, c ^ flip) for c in range(4)])]
    all_to_all x6 -> x8, starting transfers between devices: 50.6 us -> 59.5 us  [exchange(): came = lax.all_to_all(sent, 'genes', 0, 0, axis_index_groups=planes)]
    pallas_call x7 -> x10, Pallas kernels: 36.7 us -> 38 us  [the longest x8 19 us: pack(): pl.pallas_call(pack_kernel, out_shape=pltpu.HBM((PLANE, 4, n, width), jnp...]
  transfers between devices with their start and end apart: 30 -> 43, of which waited for: 14 -> 18; matrix products, arithmetic and copies ran while one was open for 1% -> 2% of each run, Pallas kernels for 62% -> 24%
where the time goes in v2:
time: 406 us; the launch traced here: 401 us
  waiting for transfers between devices  153 us (38%)
  Pallas kernels  113 us (28%)
  starting transfers between devices  108 us (27%)
  local copies, waits for them, and re-layouts  22.2 us (5%)
    ppermute x27, waiting for transfers between devices, handed(): lax.ppermute(parts[flip], 'cells', [(c, c ^ flip) for c in range(4)])  94.7 us
    all_to_all x8, starting transfers between devices, exchange(): came = lax.all_to_all(sent, 'genes', 0, 0, axis_index_groups=planes)  59.5 us
    pallas_call x4, Pallas kernels, product(): pl.pallas_call(product_kernel, out_shape=jax.ShapeDtypeStruct(own.shape,...  43.2 us
    ppermute x4, waiting for transfers between devices, per_device(): other['y', i] = lax.ppermute(own['y', i], 'genes', swap)  38.1 us
    pallas_call x8, Pallas kernels, share(): pl.pallas_call(share_kernel, out_shape=[part] * 4, in_specs=[pl.BlockSpec...  32 us
    ppermute x27, starting transfers between devices, handed(): lax.ppermute(parts[flip], 'cells', [(c, c ^ flip) for c in range(4)])  31.3 us
    pallas_call x8, Pallas kernels, pack(): pl.pallas_call(pack_kernel, out_shape=pltpu.HBM((PLANE, 4, n, width), jnp...  19 us
    pallas_call x2, Pallas kernels, gram(): pl.pallas_call(functools.partial(gram_kernel, starts, bool(sums)), out_sh...  18.9 us
  transfers between devices with their start and end apart: 43, of which 18 were waited for; matrix products, arithmetic and copies ran while one was open for 2% of the time, Pallas kernels for 24%

profile of v2, /device:TPU:1, one launch (start us, length us, event | category | flops | bytes accessed | tf_op | source)
XLA Modules:
  0.0 401.3 jit_solution(8933834501337055125)
XLA Ops:
  1.8 3.8 collective-permute-start
  6.7 1.7 slice.15.own
  11.7 2.5 collective-permute-done.other
  14.2 2.3 shard_map.68
  16.6 7.8 %all-to-all-start = ((f32[16,4,48,256]{3,2,1,0:T(8,128)}), f32[16,4,48,256]{3,2,1,0:T(8,128)S(1)}, u32[]{:S(2)}, u32[]{:S(2)}) async-start(f32[16,4,48,256]{3,2,1,0:T(8,128)} %shard_map.68), calls=%async_computation | async-start | bytes 6291456 | tf_op jit(solution)/shard_map/all_to_all | solution.py:287
  24.3 3.0 collective-permute-start.1
  27.4 2.8 collective-permute-start.3
  30.3 2.1 constant_dynamic-slice_fusion
  32.8 3.9 collective-permute-start.5
  37.3 1.8 collective-permute-done.2.refs_0_.other
  39.1 7.0 %collective-permute-done.3.other = f32[40,2048]{1,0:T(8,128)S(1)} collective-permute-done((f32[40,2048]{1,0:T(8,128)}, f32[40,2048]{1,0:T(8,128)S(1)}, u32[]{:S(2)}, u32[]{:S(2)}) %collective-permute-start.3) | collective-permute-done | bytes 327712 | tf_op jit(solution)/shard_map/ppermute | solution.py:301
  46.1 2.3 shard_map.69
  48.5 5.0 %collective-permute-done.4.refs_17_ = f32[160,512]{1,0:T(8,128)S(1)} collective-permute-done((f32[160,512]{1,0:T(8,128)S(1)}, f32[160,512]{1,0:T(8,128)S(1)}, u32[]{:S(2)}, u32[]{:S(2)}) %collective-permute-start.4) | collective-permute-done | bytes 327712 | tf_op jit(solution)/shard_map/ppermute | solution.py:125
  53.5 9.1 %collective-permute-done.5.refs_18_ = f32[160,512]{1,0:T(8,128)S(1)} collective-permute-done((f32[160,512]{1,0:T(8,128)S(1)}, f32[160,512]{1,0:T(8,128)S(1)}, u32[]{:S(2)}, u32[]{:S(2)}) %collective-permute-start.5) | collective-permute-done | bytes 327712 | tf_op jit(solution)/shard_map/ppermute | solution.py:125
  63.3 6.9 %all-to-all-start.1 = ((f32[16,4,40,256]{3,2,1,0:T(8,128)}), f32[16,4,40,256]{3,2,1,0:T(8,128)}, u32[]{:S(2)}, u32[]{:S(2)}) async-start(f32[16,4,40,256]{3,2,1,0:T(8,128)} %shard_map.69), calls=%async_computation.1 | async-start | bytes 5242880 | tf_op jit(solution)/shard_map/all_to_all | solution.py:287
  71.0 5.4 %shard_map.70 = (f32[12,48,256]{2,1,0:T(8,128)}, f32[12,48,256]{2,1,0:T(8,128)}, f32[12,48,256]{2,1,0:T(8,128)}, f32[12,48,256]{2,1,0:T(8,128)}) custom-call(s32[49]{0:T(128)S(1)} %pad_add_fusion.pick, f32[64,48,256]{2,1,0:T(8,128)S(1)} %bitcast.15), custom_call_target="tpu_custom_call" | custom-call | bytes 4718592 | tf_op jit(solution)/shard_map/pallas_call | solution.py:105
  77.6 2.9 collective-permute-start.8
  80.5 10.7 %shard_map.71.refs_1_.own.refs_0_ = f32[48,2048]{1,0:T(8,128)} custom-call(s32[49]{0:T(128)} %copy-done.31, f32[48,2048]{1,0:T(8,128)} %copy-done.12, f32[64,48,256]{2,1,0:T(8,128)} %bitcast.16, f32[64,48,256]{2,1,0:T(8,128)} %bitcast.17, f32[64,48,256]{2,1,0:T(8,128)} %bitcast.18, f32[64,48,256]{2,1,0:T(8,128)} %bitcast.19, f32[64,48,256]{2,1,0:T(8,128)} %bitcast.20, ...), custom_call_target="tpu_custom_call" | custom-call | flops 1056964608 | bytes 17825792 | tf_op jit(solution)/shard_map/pallas_call | solution.py:149
  91.2 2.6 collective-permute-start.9
  94.9 2.3 shard_map.72
  97.2 6.4 %collective-permute-done.9.other = f32[48,2048]{1,0:T(8,128)S(1)} collective-permute-done((f32[48,2048]{1,0:T(8,128)}, f32[48,2048]{1,0:T(8,128)S(1)}, u32[]{:S(2)}, u32[]{:S(2)}) %collective-permute-start.9) | collective-permute-done | bytes 393248 | tf_op jit(solution)/shard_map/ppermute | solution.py:339
  103.6 6.7 %all-to-all-start.2 = ((f32[16,4,40,256]{3,2,1,0:T(8,128)}), f32[16,4,40,256]{3,2,1,0:T(8,128)S(1)}, u32[]{:S(2)}, u32[]{:S(2)}) async-start(f32[16,4,40,256]{3,2,1,0:T(8,128)} %shard_map.72), calls=%async_computation.2 | async-start | bytes 5242880 | tf_op jit(solution)/shard_map/all_to_all | solution.py:287
  110.4 2.1 collective-permute-start.12
  112.4 2.9 shard_map.73
  116.0 10.9 %shard_map.74.refs_1_.own.refs_0_ = f32[40,2048]{1,0:T(8,128)} custom-call(s32[49]{0:T(128)} %copy-done.31, f32[40,2048]{1,0:T(8,128)} %get-tuple-element.86.own, f32[64,40,256]{2,1,0:T(8,128)} %bitcast.7.came.f0.f1.f2.f3.f4.f5, f32[64,40,256]{2,1,0:T(8,128)} %bitcast.7.came.f0.f1.f2.f3.f4.f5, f32[64,40,256]{2,1,0:T(8,128)} %bitcast.7.came.f0.f1.f2.f3.f4.f5, ...), custom_call_target="tpu_custom_call" | custom-call | flops 880803840 | bytes 17301504 | tf_op jit(solution)/shard_map/pallas_call | solution.py:149
  126.9 2.6 collective-permute-start.13
  130.5 2.7 shard_map.75
  133.2 12.9 %collective-permute-done.13.other = f32[40,2048]{1,0:T(8,128)S(1)} collective-permute-done((f32[40,2048]{1,0:T(8,128)}, f32[40,2048]{1,0:T(8,128)S(1)}, u32[]{:S(2)}, u32[]{:S(2)}) %collective-permute-start.13) | collective-permute-done | bytes 327712 | tf_op jit(solution)/shard_map/ppermute | solution.py:339
  146.9 6.7 %all-to-all-start.3 = ((f32[16,4,32,256]{3,2,1,0:T(8,128)}), f32[16,4,32,256]{3,2,1,0:T(8,128)}, u32[]{:S(2)}, u32[]{:S(2)}) async-start(f32[16,4,32,256]{3,2,1,0:T(8,128)} %shard_map.75), calls=%async_computation.3 | async-start | bytes 4194304 | tf_op jit(solution)/shard_map/all_to_all | solution.py:287
  153.8 4.7 %shard_map.76 = (f32[12,40,256]{2,1,0:T(8,128)}, f32[12,40,256]{2,1,0:T(8,128)}, f32[12,40,256]{2,1,0:T(8,128)}, f32[12,40,256]{2,1,0:T(8,128)}) custom-call(s32[49]{0:T(128)S(1)} %copy-done.33, f32[64,40,256]{2,1,0:T(8,128)S(1)} %bitcast.22), custom_call_target="tpu_custom_call" | custom-call | bytes 3932160 | tf_op jit(solution)/shard_map/pallas_call | solution.py:105
  158.5 2.1 collective-permute-start.14
  160.7 10.9 %shard_map.77.refs_1_.own.refs_0_ = f32[40,2048]{1,0:T(8,128)} custom-call(s32[49]{0:T(128)} %copy-done.31, f32[40,2048]{1,0:T(8,128)} %get-tuple-element.85.own, f32[64,40,256]{2,1,0:T(8,128)} %bitcast.23, f32[64,40,256]{2,1,0:T(8,128)} %bitcast.24, f32[64,40,256]{2,1,0:T(8,128)} %bitcast.25, f32[64,40,256]{2,1,0:T(8,128)} %bitcast.26, ...), custom_call_target="tpu_custom_call" | custom-call | flops 880803840 | bytes 17301504 | tf_op jit(solution)/shard_map/pallas_call | solution.py:149
  173.2 2.3 shard_map.78
  175.6 9.9 %collective-permute-done.17.other = f32[40,2048]{1,0:T(8,128)S(1)} collective-permute-done((f32[40,2048]{1,0:T(8,128)}, f32[40,2048]{1,0:T(8,128)S(1)}, u32[]{:S(2)}, u32[]{:S(2)}) %collective-permute-start.17) | collective-permute-done | bytes 327712 | tf_op jit(solution)/shard_map/ppermute | solution.py:339
  187.3 6.3 %all-to-all-start.4 = ((f32[16,4,48,256]{3,2,1,0:T(8,128)}), f32[16,4,48,256]{3,2,1,0:T(8,128)S(1)}, u32[]{:S(2)}, u32[]{:S(2)}) async-start(f32[16,4,48,256]{3,2,1,0:T(8,128)} %shard_map.78), calls=%async_computation.4 | async-start | bytes 6291456 | tf_op jit(solution)/shard_map/all_to_all | solution.py:287
  194.3 2.7 shard_map.79
  198.6 10.7 %shard_map.80.refs_1_.own.refs_0_ = f32[32,2048]{1,0:T(8,128)} custom-call(s32[49]{0:T(128)} %copy-done.31, f32[32,2048]{1,0:T(8,128)} %slice.15.own, f32[64,32,256]{2,1,0:T(8,128)} %bitcast.9.came.f0.f1.f2.f3.f4.f5, f32[64,32,256]{2,1,0:T(8,128)} %bitcast.9.came.f0.f1.f2.f3.f4.f5, f32[64,32,256]{2,1,0:T(8,128)} %bitcast.9.came.f0.f1.f2.f3.f4.f5, ...), custom_call_target="tpu_custom_call" | custom-call | flops 704643072 | bytes 16777216 | tf_op jit(solution)/shard_map/pallas_call | solution.py:149
  209.3 2.0 collective-permute-start.21
  212.3 2.3 shard_map.81
  214.7 8.8 %collective-permute-done.21.other = f32[32,2048]{1,0:T(8,128)S(1)} collective-permute-done((f32[32,2048]{1,0:T(8,128)}, f32[32,2048]{1,0:T(8,128)S(1)}, u32[]{:S(2)}, u32[]{:S(2)}) %collective-permute-start.21) | collective-permute-done | bytes 262176 | tf_op jit(solution)/shard_map/ppermute | solution.py:339
  225.0 9.1 %all-to-all-done.4 = f32[16,4,48,256]{3,2,1,0:T(8,128)S(1)} async-done(((f32[16,4,48,256]{3,2,1,0:T(8,128)}), f32[16,4,48,256]{3,2,1,0:T(8,128)S(1)}, u32[]{:S(2)}, u32[]{:S(2)}) %all-to-all-start.4) | async-done | bytes 3145760 | tf_op jit(solution)/shard_map/all_to_all | solution.py:287
  234.2 11.0 %all-to-all-start.5 = ((f32[16,4,40,256]{3,2,1,0:T(8,128)}), f32[16,4,40,256]{3,2,1,0:T(8,128)}, u32[]{:S(2)}, u32[]{:S(2)}) async-start(f32[16,4,40,256]{3,2,1,0:T(8,128)} %shard_map.81), calls=%async_computation.5 | async-start | bytes 5242880 | tf_op jit(solution)/shard_map/all_to_all | solution.py:287
  245.2 5.6 %shard_map.82 = (f32[14,48,256]{2,1,0:T(8,128)}, f32[14,48,256]{2,1,0:T(8,128)}, f32[14,48,256]{2,1,0:T(8,128)}, f32[14,48,256]{2,1,0:T(8,128)}) custom-call(s32[49]{0:T(128)S(1)} %copy-done.35, f32[64,48,256]{2,1,0:T(8,128)S(1)} %bitcast.29, f32[48,2048]{1,0:T(8,128)S(1)} %copy-done.3), custom_call_target="tpu_custom_call" | custom-call | bytes 5505024 | tf_op jit(solution)/shard_map/pallas_call | solution.py:105
  250.9 2.1 collective-permute-start.23
  255.5 2.3 shard_map.83
  257.8 19.0 %collective-permute-done.24.refs_6_ = f32[12,32,256]{2,1,0:T(8,128)} collective-permute-done((f32[12,32,256]{2,1,0:T(8,128)S(1)}, f32[12,32,256]{2,1,0:T(8,128)}, u32[]{:S(2)}, u32[]{:S(2)}) %collective-permute-start.24) | collective-permute-done | bytes 393248 | tf_op jit(solution)/shard_map/ppermute | solution.py:125
  276.9 7.0 %all-to-all-start.6 = ((f32[16,4,40,256]{3,2,1,0:T(8,128)}), f32[16,4,40,256]{3,2,1,0:T(8,128)S(1)}, u32[]{:S(2)}, u32[]{:S(2)}) async-start(f32[16,4,40,256]{3,2,1,0:T(8,128)} %shard_map.83), calls=%async_computation.6 | async-start | bytes 5242880 | tf_op jit(solution)/shard_map/all_to_all | solution.py:287
  283.9 2.8 collective-permute-start.27
  286.7 3.0 shard_map.84
  292.3 2.3 shard_map.85
  294.6 7.4 %collective-permute-done.27.refs_10_ = f32[14,48,256]{2,1,0:T(8,128)S(1)} collective-permute-done((f32[14,48,256]{2,1,0:T(8,128)}, f32[14,48,256]{2,1,0:T(8,128)S(1)}, u32[]{:S(2)}, u32[]{:S(2)}) %collective-permute-start.27) | collective-permute-done | bytes 688160 | tf_op jit(solution)/shard_map/ppermute | solution.py:125
  302.1 13.4 %collective-permute-done.25.refs_13_ = f32[14,40,256]{2,1,0:T(8,128)S(1)} collective-permute-done((f32[14,40,256]{2,1,0:T(8,128)}, f32[14,40,256]{2,1,0:T(8,128)S(1)}, u32[]{:S(2)}, u32[]{:S(2)}) %collective-permute-start.25) | collective-permute-done | bytes 573472 | tf_op jit(solution)/shard_map/ppermute | solution.py:125
  316.3 7.0 %all-to-all-start.7 = ((f32[16,4,32,256]{3,2,1,0:T(8,128)}), f32[16,4,32,256]{3,2,1,0:T(8,128)}, u32[]{:S(2)}, u32[]{:S(2)}) async-start(f32[16,4,32,256]{3,2,1,0:T(8,128)} %shard_map.85), calls=%async_computation.7 | async-start | bytes 4194304 | tf_op jit(solution)/shard_map/all_to_all | solution.py:287
  323.3 2.0 collective-permute-start.31
  325.3 4.9 %shard_map.86 = (f32[14,40,256]{2,1,0:T(8,128)}, f32[14,40,256]{2,1,0:T(8,128)}, f32[14,40,256]{2,1,0:T(8,128)}, f32[14,40,256]{2,1,0:T(8,128)}) custom-call(s32[49]{0:T(128)S(1)} %copy-done.35, f32[64,40,256]{2,1,0:T(8,128)S(1)} %bitcast.30, f32[40,2048]{1,0:T(8,128)S(1)} %copy-done.6), custom_call_target="tpu_custom_call" | custom-call | bytes 4587520 | tf_op jit(solution)/shard_map/pallas_call | solution.py:105
  332.2 6.1 %collective-permute-done.31.refs_14_ = f32[14,40,256]{2,1,0:T(8,128)S(1)} collective-permute-done((f32[14,40,256]{2,1,0:T(8,128)}, f32[14,40,256]{2,1,0:T(8,128)S(1)}, u32[]{:S(2)}, u32[]{:S(2)}) %collective-permute-start.31) | collective-permute-done | bytes 573472 | tf_op jit(solution)/shard_map/ppermute | solution.py:125
  339.2 8.8 %shard_map.87 = (f32[2,256,256]{2,1,0:T(8,128)}, f32[2,6,256,256]{3,2,1,0:T(8,128)}) custom-call(s32[1]{0:T(128)} %bitcast.me, f32[12,48,256]{2,1,0:T(8,128)} %get-tuple-element.90.refs_0_, f32[12,48,256]{2,1,0:T(8,128)} %collective-permute-done.7.refs_1_, f32[12,48,256]{2,1,0:T(8,128)} %copy-done.52, f32[12,48,256]{2,1,0:T(8,128)} %collective-permute-done.8.refs_3_, ...), custom_call_target="tpu_custom_call" | custom-call | flops 3598712832 | bytes 17432576 | tf_op jit(solution)/shard_map/pallas_call | solution.py:232
  347.9 4.5 %collective-permute-done.28.refs_9_ = f32[14,40,256]{2,1,0:T(8,128)S(1)} collective-permute-done((f32[14,40,256]{2,1,0:T(8,128)}, f32[14,40,256]{2,1,0:T(8,128)S(1)}, u32[]{:S(2)}, u32[]{:S(2)}) %collective-permute-start.28) | collective-permute-done | bytes 573472 | tf_op jit(solution)/shard_map/ppermute | solution.py:125
  352.5 10.3 %collective-permute-done.29.refs_10_ = f32[14,40,256]{2,1,0:T(8,128)S(1)} collective-permute-done((f32[14,40,256]{2,1,0:T(8,128)}, f32[14,40,256]{2,1,0:T(8,128)S(1)}, u32[]{:S(2)}, u32[]{:S(2)}) %collective-permute-start.29) | collective-permute-done | bytes 573472 | tf_op jit(solution)/shard_map/ppermute | solution.py:125
  364.3 2.8 shard_map.88
  367.1 2.1 collective-permute-start.32
  370.3 8.7 %collective-permute-done.32.refs_13_ = f32[14,32,256]{2,1,0:T(8,128)S(1)} collective-permute-done((f32[14,32,256]{2,1,0:T(8,128)}, f32[14,32,256]{2,1,0:T(8,128)S(1)}, u32[]{:S(2)}, u32[]{:S(2)}) %collective-permute-start.32) | collective-permute-done | bytes 458784 | tf_op jit(solution)/shard_map/ppermute | solution.py:125
  379.0 11.0 %collective-permute-done.33.refs_14_ = f32[14,32,256]{2,1,0:T(8,128)S(1)} collective-permute-done((f32[14,32,256]{2,1,0:T(8,128)}, f32[14,32,256]{2,1,0:T(8,128)S(1)}, u32[]{:S(2)}, u32[]{:S(2)}) %collective-permute-start.33) | collective-permute-done | bytes 458784 | tf_op jit(solution)/shard_map/ppermute | solution.py:125
  390.9 10.2 %shard_map.89 = (f32[2,256,256]{2,1,0:T(8,128)}, f32[2,6,256,256]{3,2,1,0:T(8,128)}) custom-call(s32[1]{0:T(128)} %bitcast.me, f32[12,40,256]{2,1,0:T(8,128)} %get-tuple-element.101.refs_0_, f32[12,40,256]{2,1,0:T(8,128)} %copy-done.40, f32[12,40,256]{2,1,0:T(8,128)} %copy-done.42, f32[12,40,256]{2,1,0:T(8,128)} %copy-done.41, ...), custom_call_target="tpu_custom_call" | custom-call | flops 2944401408 | bytes 15597568 | tf_op jit(solution)/shard_map/pallas_call | solution.py:232
  (185 shorter events, 33.2 us)
Async XLA Ops:
  1.8 14.7 %copy-start.12 = (f32[48,2048]{1,0:T(8,128)}, f32[48,2048]{1,0:T(8,128)S(1)}, u32[]{:S(2)}) copy-start(f32[48,2048]{1,0:T(8,128)S(1)} %slice.12.own) | copy-start | bytes 1179652
  1.8 12.4 %collective-permute-start = (f32[48,2048]{1,0:T(8,128)S(1)}, f32[48,2048]{1,0:T(8,128)S(1)}, u32[]{:S(2)}, u32[]{:S(2)}) collective-permute-start(f32[48,2048]{1,0:T(8,128)S(1)} %slice.12.own), channel_id=1, source_target_pairs={{0,1},{1,0},{2,3},{3,2},{4,5},{5,4},{6,7},{7,6},{8,9},{9,8},{10,11... | collective-permute-start | bytes 1179656 | tf_op jit(solution)/shard_map/ppermute | solution.py:296
  16.6 46.8 %all-to-all-start = ((f32[16,4,48,256]{3,2,1,0:T(8,128)}), f32[16,4,48,256]{3,2,1,0:T(8,128)S(1)}, u32[]{:S(2)}, u32[]{:S(2)}) async-start(f32[16,4,48,256]{3,2,1,0:T(8,128)} %shard_map.68), calls=%async_computation | async-start | bytes 6291456 | tf_op jit(solution)/shard_map/all_to_all | solution.py:287
  24.3 12.4 %collective-permute-start.1 = (f32[32,2048]{1,0:T(8,128)}, f32[32,2048]{1,0:T(8,128)}, u32[]{:S(2)}, u32[]{:S(2)}) collective-permute-start(f32[32,2048]{1,0:T(8,128)} %slice.15.own), channel_id=1, source_target_pairs={{0,1},{1,0},{2,3},{3,2},{4,5},{5,4},{6,7},{7,6},{8,9},{9,8},{10,11... | collective-permute-start | bytes 786440 | tf_op jit(solution)/shard_map/ppermute | solution.py:301
  27.3 18.8 %copy-start.14 = (f32[40,2048]{1,0:T(8,128)S(1)}, f32[40,2048]{1,0:T(8,128)}, u32[]{:S(2)}) copy-start(f32[40,2048]{1,0:T(8,128)} %get-tuple-element.86.own) | copy-start | bytes 983044
  27.3 11.8 %collective-permute-start.2 = (f32[40,2048]{1,0:T(8,128)S(1)}, f32[40,2048]{1,0:T(8,128)S(1)}, u32[]{:S(2)}, u32[]{:S(2)}) collective-permute-start(f32[40,2048]{1,0:T(8,128)S(1)} %copy-done.13), channel_id=1, source_target_pairs={{0,1},{1,0},{2,3},{3,2},{4,5},{5,4},{6,7},{7,6},{8,9},{9,8},{10,11... | collective-permute-start | bytes 983048 | tf_op jit(solution)/shard_map/ppermute | solution.py:301
  27.4 18.7 %collective-permute-start.3 = (f32[40,2048]{1,0:T(8,128)}, f32[40,2048]{1,0:T(8,128)S(1)}, u32[]{:S(2)}, u32[]{:S(2)}) collective-permute-start(f32[40,2048]{1,0:T(8,128)} %get-tuple-element.86.own), channel_id=1, source_target_pairs={{0,1},{1,0},{2,3},{3,2},{4,5},{5,4},{6,7},{7,6},{8,9},{9,8},{10,11... | collective-permute-start | bytes 983048 | tf_op jit(solution)/shard_map/ppermute | solution.py:301
  32.4 21.1 %collective-permute-start.4 = (f32[160,512]{1,0:T(8,128)S(1)}, f32[160,512]{1,0:T(8,128)S(1)}, u32[]{:S(2)}, u32[]{:S(2)}) collective-permute-start(f32[160,512]{1,0:T(8,128)S(1)} %get-tuple-element.169), channel_id=1, source_target_pairs={{0,64},{32,96},{64,0},{96,32},{1,65},{33,97},{65,1},{97,33},{2,66}... | collective-permute-start | bytes 983048 | tf_op jit(solution)/shard_map/ppermute | solution.py:125
  32.8 29.7 %collective-permute-start.5 = (f32[160,512]{1,0:T(8,128)S(1)}, f32[160,512]{1,0:T(8,128)S(1)}, u32[]{:S(2)}, u32[]{:S(2)}) collective-permute-start(f32[160,512]{1,0:T(8,128)S(1)} %get-tuple-element.168), channel_id=1, source_target_pairs={{0,96},{32,64},{64,32},{96,0},{1,97},{33,65},{65,33},{97,1},{2,98}... | collective-permute-start | bytes 983048 | tf_op jit(solution)/shard_map/ppermute | solution.py:125
  36.7 26.6 %collective-permute-start.6 = (f32[160,512]{1,0:T(8,128)S(1)}, f32[160,512]{1,0:T(8,128)}, u32[]{:S(2)}, u32[]{:S(2)}) collective-permute-start(f32[160,512]{1,0:T(8,128)S(1)} %get-tuple-element.167), channel_id=1, source_target_pairs={{0,32},{32,0},{64,96},{96,64},{1,33},{33,1},{65,97},{97,65},{2,34}... | collective-permute-start | bytes 983048 | tf_op jit(solution)/shard_map/ppermute | solution.py:125
  39.1 23.5 %copy-start.19 = (f32[40,2048]{1,0:T(8,128)}, f32[40,2048]{1,0:T(8,128)S(1)}, u32[]{:S(2)}) copy-start(f32[40,2048]{1,0:T(8,128)S(1)} %collective-permute-done.2.refs_0_.other) | copy-start | bytes 983044
  63.3 40.3 %all-to-all-start.1 = ((f32[16,4,40,256]{3,2,1,0:T(8,128)}), f32[16,4,40,256]{3,2,1,0:T(8,128)}, u32[]{:S(2)}, u32[]{:S(2)}) async-start(f32[16,4,40,256]{3,2,1,0:T(8,128)} %shard_map.69), calls=%async_computation.1 | async-start | bytes 5242880 | tf_op jit(solution)/shard_map/all_to_all | solution.py:287
  76.5 27.1 %collective-permute-start.7 = (f32[12,48,256]{2,1,0:T(8,128)}, f32[12,48,256]{2,1,0:T(8,128)}, u32[]{:S(2)}, u32[]{:S(2)}) collective-permute-start(f32[12,48,256]{2,1,0:T(8,128)} %get-tuple-element.92), channel_id=1, source_target_pairs={{0,64},{32,96},{64,0},{96,32},{1,65},{33,97},{65,1},{97,33},{2,66}... | collective-permute-start | bytes 1769480 | tf_op jit(solution)/shard_map/ppermute | solution.py:125
  77.6 16.2 %copy-start.20 = (f32[40,2048]{1,0:T(8,128)S(1)}, f32[40,2048]{1,0:T(8,128)}, u32[]{:S(2)}) copy-start(f32[40,2048]{1,0:T(8,128)} %copy-done.19) | copy-start | bytes 983044
  77.6 16.2 %copy-start.22 = (f32[12,48,256]{2,1,0:T(8,128)S(1)}, f32[12,48,256]{2,1,0:T(8,128)}, u32[]{:S(2)}) copy-start(f32[12,48,256]{2,1,0:T(8,128)} %get-tuple-element.90.refs_0_) | copy-start | bytes 1769476
  77.6 26.0 %collective-permute-start.8 = (f32[12,48,256]{2,1,0:T(8,128)}, f32[12,48,256]{2,1,0:T(8,128)}, u32[]{:S(2)}, u32[]{:S(2)}) collective-permute-start(f32[12,48,256]{2,1,0:T(8,128)} %get-tuple-element.93), channel_id=1, source_target_pairs={{0,32},{32,0},{64,96},{96,64},{1,33},{33,1},{65,97},{97,65},{2,34}... | collective-permute-start | bytes 1769480 | tf_op jit(solution)/shard_map/ppermute | solution.py:125
  91.2 12.4 %collective-permute-start.9 = (f32[48,2048]{1,0:T(8,128)}, f32[48,2048]{1,0:T(8,128)S(1)}, u32[]{:S(2)}, u32[]{:S(2)}) collective-permute-start(f32[48,2048]{1,0:T(8,128)} %shard_map.71.refs_1_.own.refs_0_), channel_id=1, source_target_pairs={{0,1},{1,0},{2,3},{3,2},{4,5},{5,4},{6,7},{7,6},{8,9},{9,8},{10,11... | collective-permute-start | bytes 1179656 | tf_op jit(solution)/shard_map/ppermute | solution.py:339
  103.6 43.3 %all-to-all-start.2 = ((f32[16,4,40,256]{3,2,1,0:T(8,128)}), f32[16,4,40,256]{3,2,1,0:T(8,128)S(1)}, u32[]{:S(2)}, u32[]{:S(2)}) async-start(f32[16,4,40,256]{3,2,1,0:T(8,128)} %shard_map.72), calls=%async_computation.2 | async-start | bytes 5242880 | tf_op jit(solution)/shard_map/all_to_all | solution.py:287
  110.4 22.8 %collective-permute-start.12 = (f32[12,48,256]{2,1,0:T(8,128)}, f32[12,48,256]{2,1,0:T(8,128)S(1)}, u32[]{:S(2)}, u32[]{:S(2)}) collective-permute-start(f32[12,48,256]{2,1,0:T(8,128)} %get-tuple-element.99), channel_id=1, source_target_pairs={{0,96},{32,64},{64,32},{96,0},{1,97},{33,65},{65,33},{97,1},{2,98}... | collective-permute-start | bytes 1769480 | tf_op jit(solution)/shard_map/ppermute | solution.py:125
  115.3 31.5 %collective-permute-start.10 = (f32[12,40,256]{2,1,0:T(8,128)}, f32[12,40,256]{2,1,0:T(8,128)S(1)}, u32[]{:S(2)}, u32[]{:S(2)}) collective-permute-start(f32[12,40,256]{2,1,0:T(8,128)} %get-tuple-element.97), channel_id=1, source_target_pairs={{0,64},{32,96},{64,0},{96,32},{1,65},{33,97},{65,1},{97,33},{2,66}... | collective-permute-start | bytes 1474568 | tf_op jit(solution)/shard_map/ppermute | solution.py:125
  116.0 13.5 %copy-start.15 = (f32[32,2048]{1,0:T(8,128)S(1)}, f32[32,2048]{1,0:T(8,128)}, u32[]{:S(2)}) copy-start(f32[32,2048]{1,0:T(8,128)} %slice.15.own) | copy-start | bytes 786436
  116.0 13.5 %copy-start.24 = (f32[12,40,256]{2,1,0:T(8,128)S(1)}, f32[12,40,256]{2,1,0:T(8,128)}, u32[]{:S(2)}) copy-start(f32[12,40,256]{2,1,0:T(8,128)} %get-tuple-element.95.refs_0_.refs_4_) | copy-start | bytes 1474564
  116.0 30.9 %collective-permute-start.11 = (f32[12,40,256]{2,1,0:T(8,128)}, f32[12,40,256]{2,1,0:T(8,128)}, u32[]{:S(2)}, u32[]{:S(2)}) collective-permute-start(f32[12,40,256]{2,1,0:T(8,128)} %get-tuple-element.98), channel_id=1, source_target_pairs={{0,32},{32,0},{64,96},{96,64},{1,33},{33,1},{65,97},{97,65},{2,34}... | collective-permute-start | bytes 1474568 | tf_op jit(solution)/shard_map/ppermute | solution.py:125
  126.9 19.3 %collective-permute-start.13 = (f32[40,2048]{1,0:T(8,128)}, f32[40,2048]{1,0:T(8,128)S(1)}, u32[]{:S(2)}, u32[]{:S(2)}) collective-permute-start(f32[40,2048]{1,0:T(8,128)} %shard_map.74.refs_1_.own.refs_0_), channel_id=1, source_target_pairs={{0,1},{1,0},{2,3},{3,2},{4,5},{5,4},{6,7},{7,6},{8,9},{9,8},{10,11... | collective-permute-start | bytes 983048 | tf_op jit(solution)/shard_map/ppermute | solution.py:339
  133.2 20.6 %copy-start.33 = (s32[49]{0:T(128)S(1)}, s32[49]{0:T(128)}, u32[]{:S(2)}) copy-start(s32[49]{0:T(128)} %copy-done.31) | copy-start | bytes 592
  133.2 13.7 %copy-start.52 = (f32[12,48,256]{2,1,0:T(8,128)}, f32[12,48,256]{2,1,0:T(8,128)S(1)}, u32[]{:S(2)}) copy-start(f32[12,48,256]{2,1,0:T(8,128)S(1)} %collective-permute-done.12.refs_2_) | copy-start | bytes 1769476
  146.9 11.6 %copy-start.55 = (f32[12,40,256]{2,1,0:T(8,128)}, f32[12,40,256]{2,1,0:T(8,128)S(1)}, u32[]{:S(2)}) copy-start(f32[12,40,256]{2,1,0:T(8,128)S(1)} %collective-permute-done.10.refs_5_) | copy-start | bytes 1474564
  146.9 11.6 %copy-start.1 = (f32[16,4,40,256]{3,2,1,0:T(8,128)}, f32[16,4,40,256]{3,2,1,0:T(8,128)S(1)}, u32[]{:S(2)}) copy-start(f32[16,4,40,256]{3,2,1,0:T(8,128)S(1)} %all-to-all-done.2) | copy-start | bytes 7864324
  146.9 39.4 %all-to-all-start.3 = ((f32[16,4,32,256]{3,2,1,0:T(8,128)}), f32[16,4,32,256]{3,2,1,0:T(8,128)}, u32[]{:S(2)}, u32[]{:S(2)}) async-start(f32[16,4,32,256]{3,2,1,0:T(8,128)} %shard_map.75), calls=%async_computation.3 | async-start | bytes 4194304 | tf_op jit(solution)/shard_map/all_to_all | solution.py:287
  153.7 21.9 %collective-permute-start.16 = (f32[12,40,256]{2,1,0:T(8,128)}, f32[12,40,256]{2,1,0:T(8,128)S(1)}, u32[]{:S(2)}, u32[]{:S(2)}) collective-permute-start(f32[12,40,256]{2,1,0:T(8,128)} %get-tuple-element.106), channel_id=1, source_target_pairs={{0,96},{32,64},{64,32},{96,0},{1,97},{33,65},{65,33},{97,1},{2,98}... | collective-permute-start | bytes 1474568 | tf_op jit(solution)/shard_map/ppermute | solution.py:125
  158.5 27.8 %collective-permute-start.14 = (f32[12,40,256]{2,1,0:T(8,128)}, f32[12,40,256]{2,1,0:T(8,128)S(1)}, u32[]{:S(2)}, u32[]{:S(2)}) collective-permute-start(f32[12,40,256]{2,1,0:T(8,128)} %get-tuple-element.104), channel_id=1, source_target_pairs={{0,64},{32,96},{64,0},{96,32},{1,65},{33,97},{65,1},{97,33},{2,66}... | collective-permute-start | bytes 1474568 | tf_op jit(solution)/shard_map/ppermute | solution.py:125
  160.6 11.7 %copy-start.3 = (f32[48,2048]{1,0:T(8,128)S(1)}, f32[48,2048]{1,0:T(8,128)}, u32[]{:S(2)}) copy-start(f32[48,2048]{1,0:T(8,128)} %shard_map.71.refs_1_.own.refs_0_) | copy-start | bytes 1179652
  160.6 11.7 %copy-start.17 = (f32[12,40,256]{2,1,0:T(8,128)S(1)}, f32[12,40,256]{2,1,0:T(8,128)}, u32[]{:S(2)}) copy-start(f32[12,40,256]{2,1,0:T(8,128)} %get-tuple-element.101.refs_0_) | copy-start | bytes 1474564
  160.6 25.7 %collective-permute-start.15 = (f32[12,40,256]{2,1,0:T(8,128)}, f32[12,40,256]{2,1,0:T(8,128)S(1)}, u32[]{:S(2)}, u32[]{:S(2)}) collective-permute-start(f32[12,40,256]{2,1,0:T(8,128)} %get-tuple-element.105), channel_id=1, source_target_pairs={{0,32},{32,0},{64,96},{96,64},{1,33},{33,1},{65,97},{97,65},{2,34}... | collective-permute-start | bytes 1474568 | tf_op jit(solution)/shard_map/ppermute | solution.py:125
  171.6 14.0 %collective-permute-start.17 = (f32[40,2048]{1,0:T(8,128)}, f32[40,2048]{1,0:T(8,128)S(1)}, u32[]{:S(2)}, u32[]{:S(2)}) collective-permute-start(f32[40,2048]{1,0:T(8,128)} %shard_map.77.refs_1_.own.refs_0_), channel_id=1, source_target_pairs={{0,1},{1,0},{2,3},{3,2},{4,5},{5,4},{6,7},{7,6},{8,9},{9,8},{10,11... | collective-permute-start | bytes 983048 | tf_op jit(solution)/shard_map/ppermute | solution.py:339
  187.3 46.9 %all-to-all-start.4 = ((f32[16,4,48,256]{3,2,1,0:T(8,128)}), f32[16,4,48,256]{3,2,1,0:T(8,128)S(1)}, u32[]{:S(2)}, u32[]{:S(2)}) async-start(f32[16,4,48,256]{3,2,1,0:T(8,128)} %shard_map.78), calls=%async_computation.4 | async-start | bytes 6291456 | tf_op jit(solution)/shard_map/all_to_all | solution.py:287
  193.6 21.1 %collective-permute-start.20 = (f32[12,40,256]{2,1,0:T(8,128)}, f32[12,40,256]{2,1,0:T(8,128)S(1)}, u32[]{:S(2)}, u32[]{:S(2)}) collective-permute-start(f32[12,40,256]{2,1,0:T(8,128)} %get-tuple-element.114), channel_id=1, source_target_pairs={{0,96},{32,64},{64,32},{96,0},{1,97},{33,65},{65,33},{97,1},{2,98}... | collective-permute-start | bytes 1474568 | tf_op jit(solution)/shard_map/ppermute | solution.py:125
  197.0 27.3 %collective-permute-start.18 = (f32[12,32,256]{2,1,0:T(8,128)}, f32[12,32,256]{2,1,0:T(8,128)S(1)}, u32[]{:S(2)}, u32[]{:S(2)}) collective-permute-start(f32[12,32,256]{2,1,0:T(8,128)} %get-tuple-element.112), channel_id=1, source_target_pairs={{0,64},{32,96},{64,0},{96,32},{1,65},{33,97},{65,1},{97,33},{2,66}... | collective-permute-start | bytes 1179656 | tf_op jit(solution)/shard_map/ppermute | solution.py:125
  198.5 12.9 %copy-start.8 = (f32[40,2048]{1,0:T(8,128)S(1)}, f32[40,2048]{1,0:T(8,128)}, u32[]{:S(2)}) copy-start(f32[40,2048]{1,0:T(8,128)} %shard_map.74.refs_1_.own.refs_0_) | copy-start | bytes 983044
  198.5 12.9 %copy-start.18 = (f32[12,32,256]{2,1,0:T(8,128)S(1)}, f32[12,32,256]{2,1,0:T(8,128)}, u32[]{:S(2)}) copy-start(f32[12,32,256]{2,1,0:T(8,128)} %get-tuple-element.110.refs_0_.refs_4_) | copy-start | bytes 1179652
  198.5 12.9 %copy-start.26 = (f32[40,2048]{1,0:T(8,128)S(1)}, f32[40,2048]{1,0:T(8,128)}, u32[]{:S(2)}) copy-start(f32[40,2048]{1,0:T(8,128)} %copy-done.25) | copy-start | bytes 983044
  198.5 26.5 %collective-permute-start.19 = (f32[12,32,256]{2,1,0:T(8,128)}, f32[12,32,256]{2,1,0:T(8,128)}, u32[]{:S(2)}, u32[]{:S(2)}) collective-permute-start(f32[12,32,256]{2,1,0:T(8,128)} %get-tuple-element.113), channel_id=1, source_target_pairs={{0,32},{32,0},{64,96},{96,64},{1,33},{33,1},{65,97},{97,65},{2,34}... | collective-permute-start | bytes 1179656 | tf_op jit(solution)/shard_map/ppermute | solution.py:125
  209.3 14.2 %collective-permute-start.21 = (f32[32,2048]{1,0:T(8,128)}, f32[32,2048]{1,0:T(8,128)S(1)}, u32[]{:S(2)}, u32[]{:S(2)}) collective-permute-start(f32[32,2048]{1,0:T(8,128)} %shard_map.80.refs_1_.own.refs_0_), channel_id=1, source_target_pairs={{0,1},{1,0},{2,3},{3,2},{4,5},{5,4},{6,7},{7,6},{8,9},{9,8},{10,11... | collective-permute-start | bytes 786440 | tf_op jit(solution)/shard_map/ppermute | solution.py:339
  234.2 42.7 %all-to-all-start.5 = ((f32[16,4,40,256]{3,2,1,0:T(8,128)}), f32[16,4,40,256]{3,2,1,0:T(8,128)}, u32[]{:S(2)}, u32[]{:S(2)}) async-start(f32[16,4,40,256]{3,2,1,0:T(8,128)} %shard_map.81), calls=%async_computation.5 | async-start | bytes 5242880 | tf_op jit(solution)/shard_map/all_to_all | solution.py:287
  250.8 26.1 %collective-permute-start.22 = (f32[14,48,256]{2,1,0:T(8,128)}, f32[14,48,256]{2,1,0:T(8,128)}, u32[]{:S(2)}, u32[]{:S(2)}) collective-permute-start(f32[14,48,256]{2,1,0:T(8,128)} %get-tuple-element.122), channel_id=1, source_target_pairs={{0,64},{32,96},{64,0},{96,32},{1,65},{33,97},{65,1},{97,33},{2,66}... | collective-permute-start | bytes 2064392 | tf_op jit(solution)/shard_map/ppermute | solution.py:125
  250.9 25.9 %collective-permute-start.23 = (f32[14,48,256]{2,1,0:T(8,128)}, f32[14,48,256]{2,1,0:T(8,128)}, u32[]{:S(2)}, u32[]{:S(2)}) collective-permute-start(f32[14,48,256]{2,1,0:T(8,128)} %get-tuple-element.123), channel_id=1, source_target_pairs={{0,32},{32,0},{64,96},{96,64},{1,33},{33,1},{65,97},{97,65},{2,34}... | collective-permute-start | bytes 2064392 | tf_op jit(solution)/shard_map/ppermute | solution.py:125
  253.1 23.8 %collective-permute-start.24 = (f32[12,32,256]{2,1,0:T(8,128)S(1)}, f32[12,32,256]{2,1,0:T(8,128)}, u32[]{:S(2)}, u32[]{:S(2)}) collective-permute-start(f32[12,32,256]{2,1,0:T(8,128)S(1)} %copy-done.57), channel_id=1, source_target_pairs={{0,96},{32,64},{64,32},{96,0},{1,97},{33,65},{65,33},{97,1},{2,98}... | collective-permute-start | bytes 1179656 | tf_op jit(solution)/shard_map/ppermute | solution.py:125
  276.9 39.4 %all-to-all-start.6 = ((f32[16,4,40,256]{3,2,1,0:T(8,128)}), f32[16,4,40,256]{3,2,1,0:T(8,128)S(1)}, u32[]{:S(2)}, u32[]{:S(2)}) async-start(f32[16,4,40,256]{3,2,1,0:T(8,128)} %shard_map.83), calls=%async_computation.6 | async-start | bytes 5242880 | tf_op jit(solution)/shard_map/all_to_all | solution.py:287
  283.9 18.2 %collective-permute-start.27 = (f32[14,48,256]{2,1,0:T(8,128)}, f32[14,48,256]{2,1,0:T(8,128)S(1)}, u32[]{:S(2)}, u32[]{:S(2)}) collective-permute-start(f32[14,48,256]{2,1,0:T(8,128)} %get-tuple-element.133), channel_id=1, source_target_pairs={{0,96},{32,64},{64,32},{96,0},{1,97},{33,65},{65,33},{97,1},{2,98}... | collective-permute-start | bytes 2064392 | tf_op jit(solution)/shard_map/ppermute | solution.py:125
  289.7 25.7 %collective-permute-start.25 = (f32[14,40,256]{2,1,0:T(8,128)}, f32[14,40,256]{2,1,0:T(8,128)S(1)}, u32[]{:S(2)}, u32[]{:S(2)}) collective-permute-start(f32[14,40,256]{2,1,0:T(8,128)} %get-tuple-element.131), channel_id=1, source_target_pairs={{0,64},{32,96},{64,0},{96,32},{1,65},{33,97},{65,1},{97,33},{2,66}... | collective-permute-start | bytes 1720328 | tf_op jit(solution)/shard_map/ppermute | solution.py:125
  291.2 25.1 %collective-permute-start.26 = (f32[14,40,256]{2,1,0:T(8,128)}, f32[14,40,256]{2,1,0:T(8,128)}, u32[]{:S(2)}, u32[]{:S(2)}) collective-permute-start(f32[14,40,256]{2,1,0:T(8,128)} %get-tuple-element.132), channel_id=1, source_target_pairs={{0,32},{32,0},{64,96},{96,64},{1,33},{33,1},{65,97},{97,65},{2,34}... | collective-permute-start | bytes 1720328 | tf_op jit(solution)/shard_map/ppermute | solution.py:125
  294.6 30.7 %copy-start.6 = (f32[40,2048]{1,0:T(8,128)S(1)}, f32[40,2048]{1,0:T(8,128)}, u32[]{:S(2)}) copy-start(f32[40,2048]{1,0:T(8,128)} %shard_map.77.refs_1_.own.refs_0_) | copy-start | bytes 983044
  302.0 13.4 %copy-start.51 = (f32[14,48,256]{2,1,0:T(8,128)}, f32[14,48,256]{2,1,0:T(8,128)S(1)}, u32[]{:S(2)}) copy-start(f32[14,48,256]{2,1,0:T(8,128)S(1)} %collective-permute-done.27.refs_10_) | copy-start | bytes 2064388
  316.3 46.5 %all-to-all-start.7 = ((f32[16,4,32,256]{3,2,1,0:T(8,128)}), f32[16,4,32,256]{3,2,1,0:T(8,128)}, u32[]{:S(2)}, u32[]{:S(2)}) async-start(f32[16,4,32,256]{3,2,1,0:T(8,128)} %shard_map.85), calls=%async_computation.7 | async-start | bytes 4194304 | tf_op jit(solution)/shard_map/all_to_all | solution.py:287
  323.3 15.1 %collective-permute-start.31 = (f32[14,40,256]{2,1,0:T(8,128)}, f32[14,40,256]{2,1,0:T(8,128)S(1)}, u32[]{:S(2)}, u32[]{:S(2)}) collective-permute-start(f32[14,40,256]{2,1,0:T(8,128)} %get-tuple-element.155), channel_id=1, source_target_pairs={{0,96},{32,64},{64,32},{96,0},{1,97},{33,65},{65,33},{97,1},{2,98}... | collective-permute-start | bytes 1720328 | tf_op jit(solution)/shard_map/ppermute | solution.py:125
  330.2 22.2 %collective-permute-start.28 = (f32[14,40,256]{2,1,0:T(8,128)}, f32[14,40,256]{2,1,0:T(8,128)S(1)}, u32[]{:S(2)}, u32[]{:S(2)}) collective-permute-start(f32[14,40,256]{2,1,0:T(8,128)} %get-tuple-element.137), channel_id=1, source_target_pairs={{0,64},{32,96},{64,0},{96,32},{1,65},{33,97},{65,1},{97,33},{2,66}... | collective-permute-start | bytes 1720328 | tf_op jit(solution)/shard_map/ppermute | solution.py:125
  331.7 31.1 %collective-permute-start.29 = (f32[14,40,256]{2,1,0:T(8,128)}, f32[14,40,256]{2,1,0:T(8,128)S(1)}, u32[]{:S(2)}, u32[]{:S(2)}) collective-permute-start(f32[14,40,256]{2,1,0:T(8,128)} %get-tuple-element.138), channel_id=1, source_target_pairs={{0,96},{32,64},{64,32},{96,0},{1,97},{33,65},{65,33},{97,1},{2,98}... | collective-permute-start | bytes 1720328 | tf_op jit(solution)/shard_map/ppermute | solution.py:125
  332.0 30.8 %collective-permute-start.30 = (f32[14,40,256]{2,1,0:T(8,128)}, f32[14,40,256]{2,1,0:T(8,128)S(1)}, u32[]{:S(2)}, u32[]{:S(2)}) collective-permute-start(f32[14,40,256]{2,1,0:T(8,128)} %get-tuple-element.139), channel_id=1, source_target_pairs={{0,32},{32,0},{64,96},{96,64},{1,33},{33,1},{65,97},{97,65},{2,34}... | collective-permute-start | bytes 1720328 | tf_op jit(solution)/shard_map/ppermute | solution.py:125
  352.5 37.5 %copy-start.37 = (f32[14,40,256]{2,1,0:T(8,128)}, f32[14,40,256]{2,1,0:T(8,128)S(1)}, u32[]{:S(2)}) copy-start(f32[14,40,256]{2,1,0:T(8,128)S(1)} %collective-permute-done.28.refs_9_) | copy-start | bytes 1720324
  362.8 27.2 %copy-start.38 = (f32[14,40,256]{2,1,0:T(8,128)}, f32[14,40,256]{2,1,0:T(8,128)S(1)}, u32[]{:S(2)}) copy-start(f32[14,40,256]{2,1,0:T(8,128)S(1)} %collective-permute-done.29.refs_10_) | copy-start | bytes 1720324
  362.8 27.2 %copy-start.39 = (f32[14,40,256]{2,1,0:T(8,128)}, f32[14,40,256]{2,1,0:T(8,128)S(1)}, u32[]{:S(2)}) copy-start(f32[14,40,256]{2,1,0:T(8,128)S(1)} %collective-permute-done.30.refs_11_) | copy-start | bytes 1720324
  367.1 12.0 %collective-permute-start.32 = (f32[14,32,256]{2,1,0:T(8,128)}, f32[14,32,256]{2,1,0:T(8,128)S(1)}, u32[]{:S(2)}, u32[]{:S(2)}) collective-permute-start(f32[14,32,256]{2,1,0:T(8,128)} %get-tuple-element.162), channel_id=1, source_target_pairs={{0,64},{32,96},{64,0},{96,32},{1,65},{33,97},{65,1},{97,33},{2,66}... | collective-permute-start | bytes 1376264 | tf_op jit(solution)/shard_map/ppermute | solution.py:125
  369.2 20.8 %collective-permute-start.33 = (f32[14,32,256]{2,1,0:T(8,128)}, f32[14,32,256]{2,1,0:T(8,128)S(1)}, u32[]{:S(2)}, u32[]{:S(2)}) collective-permute-start(f32[14,32,256]{2,1,0:T(8,128)} %get-tuple-element.163), channel_id=1, source_target_pairs={{0,96},{32,64},{64,32},{96,0},{1,97},{33,65},{65,33},{97,1},{2,98}... | collective-permute-start | bytes 1376264 | tf_op jit(solution)/shard_map/ppermute | solution.py:125
  370.3 19.7 %collective-permute-start.34 = (f32[14,32,256]{2,1,0:T(8,128)}, f32[14,32,256]{2,1,0:T(8,128)S(1)}, u32[]{:S(2)}, u32[]{:S(2)}) collective-permute-start(f32[14,32,256]{2,1,0:T(8,128)} %get-tuple-element.164), channel_id=1, source_target_pairs={{0,32},{32,0},{64,96},{96,64},{1,33},{33,1},{65,97},{97,65},{2,34}... | collective-permute-start | bytes 1376264 | tf_op jit(solution)/shard_map/ppermute | solution.py:125
  (37 other events, 189.5 us)

commit v3 on v2

--- a/solution.py
+++ b/solution.py
@@ -11,6 +11,7 @@
 MOST = 2
 SIZES = (48, 40, 40, 32)
 LATE = 2
+SWAPPED = (0, 0, 0, 0)
 FLIPS = (0, 2, 3, 1)
 STEP = 0.5
 LIMIT = STEP * 0.04
@@ -120,11 +121,8 @@
     )(pick, came, *own, *before)
 
 
-def handed(parts):
-    return [
-        lax.ppermute(parts[flip], "cells", [(c, c ^ flip) for c in range(4)]) if flip else parts[0]
-        for flip in FLIPS
-    ]
+def handed(part, flip):
+    return lax.ppermute(part, "cells", [(c, c ^ flip) for c in range(4)])
 
 
 def product_kernel(pick, own, f0, f1, f2, f3, f4, f5, diag, offd, out):
@@ -169,11 +167,13 @@
     )(pick, own, came, came, came, came, came, came, diag, offd)
 
 
-def gram_kernel(starts, last, me, *refs):
+def gram_kernel(starts, more, last, me, *refs):
     parts = 4 * len(starts)
     far_x, ys, home = refs[:parts], refs[parts : 2 * parts], refs[2 * parts : 2 * parts + 4]
+    if more:
+        diag_sum, off_sum = refs[2 * parts + 4 : 2 * parts + 6]
     if last:
-        diag_sum, off_sum, diag, offd = refs[2 * parts + 4 : 2 * parts + 8]
+        diag, offd = refs[2 * parts + 6 : 2 * parts + 8]
     new_diag, new_offd, left_high, left_low = refs[-4:]
     cells = left_high.shape[1] // 2
     scale = 1.0 / (2.0 * 640)
@@ -194,14 +194,17 @@
         high, low = halves(right)
         total = dot(left_high[...], high) + dot(left_low[...], high) + dot(left_high[...], low)
         total = total.T
+        if more:
+            total = total + off_sum[0, k]
         if last:
-            total = shrink(offd[0, k] - (STEP * scale) * (total + off_sum[0, k]))
+            total = shrink(offd[0, k] - (STEP * scale) * total)
         new_offd[0, k] = total
     high, low = halves(own_x)
     y_high, y_low = left_high[:, :cells], left_low[:, :cells]
     total = dot(y_high, high) + dot(y_low, high) + dot(y_high, low)
+    if more:
+        total = total + diag_sum[0]
     if last:
-        total = total + diag_sum[0]
         total = total + total.T
         eye = lax.broadcasted_iota(jnp.int32, (width, width), 0) == lax.broadcasted_iota(
             jnp.int32, (width, width), 1
@@ -228,9 +231,11 @@
     specs = [block(a) for a in [*xs, *ys]]
     specs += [pl.BlockSpec((a.shape[0], width), lambda j, me: (0, j)) for a in home]
     if sums:
-        specs += pair(lambda me: 0) + pair(lambda me: me[0] * 2)
+        specs += pair(lambda me: 0)
+    if old:
+        specs += pair(lambda me: me[0] * 2)
     return pl.pallas_call(
-        functools.partial(gram_kernel, starts, bool(sums)),
+        functools.partial(gram_kernel, starts, bool(sums), bool(old)),
         out_shape=[
             jax.ShapeDtypeStruct((2, width, width), jnp.float32),
             jax.ShapeDtypeStruct((2, 6, width, width), jnp.float32),
@@ -299,9 +304,10 @@
     for i in runs[1:]:
         own["x", i] = slices[i]
         other["x", i] = lax.ppermute(slices[i], "genes", swap)
-    home = handed(
-        [lax.dynamic_slice_in_dim(expression, (me ^ flip) * 512, 512, axis=1) for flip in range(4)]
-    )
+    home = [
+        lax.dynamic_slice_in_dim(expression, (me ^ flip) * 512, 512, axis=1) for flip in FLIPS
+    ]
+    home[1:] = [handed(piece, flip) for piece, flip in zip(home[1:], FLIPS[1:])]
 
     def summed(which, *rest):
         xs, ys = ([part for i in which for part in parts[kind, i]] for kind in "xy")
@@ -311,42 +317,48 @@
         kind, i = turn
         arrived = exchange(sent)
         if at + 1 < len(turns):
-            then = turns[at + 1]
+            then, before, ties = turns[at + 1], [], [arrived]
             if at == 0:
-                before, ties = [other["x", j] for j in runs[2:]], home[1:]
+                before = [other["x", j] for j in runs[2:]]
+                ties += home[1:]
             else:
                 last = turns[at - 1]
-                before, ties = [shared[last][0]], [parts[last][1], parts[last][3]]
+                before = [shared[last][0]]
+                ties += [shared[last][3], parts[last][1], parts[last][3]]
                 if last[0] == "x":
                     before.append(own["y", last[1]])
-            if at >= 2:
-                ties.append(parts[turns[at - 2]][2])
-            if at >= 1 and last[0] == "x":
-                ties.append(other["y", last[1]])
+                if at >= 2:
+                    ties.append(parts[turns[at - 2]][2])
+                due = [j for j in runs if j + 1 + SWAPPED[j] == at]
+                ties += [other["y", j] for j in due]
             sent = pack(send, own[then], other[then], before)
-            sent, arrived, *ties = lax.optimization_barrier((sent, arrived, *ties))
+            sent, arrived, *ties = lax.optimization_barrier((sent, *ties))
             if at == 0:
                 home[1:] = ties
             else:
-                parts[last][1], parts[last][3] = ties[:2]
-            if at >= 2:
-                parts[turns[at - 2]][2] = ties[2]
-            if at >= 1 and last[0] == "x":
-                other["y", last[1]] = ties[-1]
+                for j in reversed(due):
+                    other["y", j] = ties.pop()
+                if at >= 2:
+                    parts[turns[at - 2]][2] = ties.pop()
+                parts[last][2] = handed(ties[0], 3)
+                parts[last][1], parts[last][3] = ties[1:]
+        before = []
+        if at + 1 == len(turns):
+            last = turns[at - 1]
+            parts[last][2] = handed(shared[last][3], 3)
+            sums = summed(runs[:-LATE])
+            before = [sums[0]]
         if kind == "x":
             shared[turn] = share(pick, arrived)
             own["y", i] = product(pick, own[turn], arrived, omega_diag, omega_offd)
             other["y", i] = lax.ppermute(own["y", i], "genes", swap)
         else:
-            before = []
-            if at + 1 == len(turns):
-                sums = summed(runs[:-LATE])
-                before = [sums[0]]
-                last = turns[at - 1]
-                arrived, *parts[last] = lax.optimization_barrier((arrived, *parts[last]))
             shared[turn] = share(pick, arrived, [own[turn]], before)
-        parts[turn] = handed(shared[turn])
-    return tuple(summed(runs[-LATE:], sums, (omega_diag, omega_offd)))
+        parts[turn] = [shared[turn][0], handed(shared[turn][2], 2), None, handed(shared[turn][1], 1)]
+    parts[turn][2] = handed(shared[turn][3], 3)
+    for i in runs[-LATE:-1]:
+        sums = summed([i], sums)
+    return tuple(summed(runs[-1:], sums, (omega_diag, omega_offd)))
 
 
 def solution(mesh):

time: 406 us -> 391 us (0.963)
  waiting for transfers between devices: 153 us -> 132 us
    ppermute x27, waiting for transfers between devices: 94.7 us -> 73 us  [handed(): return lax.ppermute(part, 'cells', [(c, c ^ flip) for c in range(4)])]
    ppermute x27, starting transfers between devices: 31.3 us -> 37.3 us  [handed(): return lax.ppermute(part, 'cells', [(c, c ^ flip) for c in range(4)])]
    all_to_all x8, starting transfers between devices: 59.5 us -> 54.9 us  [exchange(): came = lax.all_to_all(sent, 'genes', 0, 0, axis_index_groups=planes)]
    pallas_call x2 -> x3, Pallas kernels: 18.9 us -> 22.9 us  [gram(): pl.pallas_call(functools.partial(gram_kernel, starts, bool(sums), bool(ol...]
    unnamed x117 -> x119, local copies, waits for them, and re-layouts: 15.7 us -> 18.9 us
  transfers between devices with their start and end apart: 43 -> 43, of which waited for: 18 -> 17; matrix products, arithmetic and copies ran while one was open for 2% -> 2% of each run, Pallas kernels for 24% -> 28%
where the time goes in v3:
time: 391 us; the launch traced here: 389 us
  waiting for transfers between devices  132 us (34%)
  Pallas kernels  117 us (30%)
  starting transfers between devices  110 us (28%)
  local copies, waits for them, and re-layouts  25.4 us (6%)
    ppermute x27, waiting for transfers between devices, handed(): return lax.ppermute(part, 'cells', [(c, c ^ flip) for c in range(4)])  73 us
    all_to_all x8, starting transfers between devices, exchange(): came = lax.all_to_all(sent, 'genes', 0, 0, axis_index_groups=planes)  54.9 us
    pallas_call x4, Pallas kernels, product(): pl.pallas_call(product_kernel, out_shape=jax.ShapeDtypeStruct(own.shape,...  43.1 us
    ppermute x4, waiting for transfers between devices, per_device(): other['y', i] = lax.ppermute(own['y', i], 'genes', swap)  39.7 us
    ppermute x27, starting transfers between devices, handed(): return lax.ppermute(part, 'cells', [(c, c ^ flip) for c in range(4)])  37.3 us
    pallas_call x8, Pallas kernels, share(): pl.pallas_call(share_kernel, out_shape=[part] * 4, in_specs=[pl.BlockSpec...  32 us
    pallas_call x3, Pallas kernels, gram(): pl.pallas_call(functools.partial(gram_kernel, starts, bool(sums), bool(ol...  22.9 us
    pallas_call x8, Pallas kernels, pack(): pl.pallas_call(pack_kernel, out_shape=pltpu.HBM((PLANE, 4, n, width), jnp...  19.1 us
  transfers between devices with their start and end apart: 43, of which 17 were waited for; matrix products, arithmetic and copies ran while one was open for 2% of the time, Pallas kernels for 28%

profile of v3, /device:TPU:1, one launch (start us, length us, event | category | flops | bytes accessed | tf_op | source)
XLA Modules:
  0.0 388.7 jit_solution(8788542148022688849)
XLA Ops:
  1.8 3.8 collective-permute-start
  6.7 1.7 slice.15.own
  11.7 2.5 collective-permute-done.other
  14.2 2.3 shard_map.68
  16.6 7.8 %all-to-all-start = ((f32[16,4,48,256]{3,2,1,0:T(8,128)}), f32[16,4,48,256]{3,2,1,0:T(8,128)S(1)}, u32[]{:S(2)}, u32[]{:S(2)}) async-start(f32[16,4,48,256]{3,2,1,0:T(8,128)} %shard_map.68), calls=%async_computation | async-start | bytes 6291456 | tf_op jit(solution)/shard_map/all_to_all | solution.py:292
  24.3 3.0 collective-permute-start.3
  27.4 2.8 collective-permute-start.2
  30.3 2.2 constant_dynamic-slice_fusion
  32.9 3.9 collective-permute-start.5
  37.3 1.8 collective-permute-done.1.other
  39.1 7.0 %collective-permute-done.2.refs_0_.other = f32[40,2048]{1,0:T(8,128)S(1)} collective-permute-done((f32[40,2048]{1,0:T(8,128)S(1)}, f32[40,2048]{1,0:T(8,128)S(1)}, u32[]{:S(2)}, u32[]{:S(2)}) %collective-permute-start.2) | collective-permute-done | bytes 327712 | tf_op jit(solution)/shard_map/ppermute | solution.py:306
  46.1 2.4 shard_map.69
  48.5 5.0 %collective-permute-done.4.refs_17_.refs_9_ = f32[160,512]{1,0:T(8,128)S(1)} collective-permute-done((f32[160,512]{1,0:T(8,128)S(1)}, f32[160,512]{1,0:T(8,128)S(1)}, u32[]{:S(2)}, u32[]{:S(2)}) %collective-permute-start.4) | collective-permute-done | bytes 327712 | tf_op jit(solution)/shard_map/ppermute | solution.py:125
  53.5 9.1 %collective-permute-done.5.refs_18_.refs_10_ = f32[160,512]{1,0:T(8,128)S(1)} collective-permute-done((f32[160,512]{1,0:T(8,128)S(1)}, f32[160,512]{1,0:T(8,128)S(1)}, u32[]{:S(2)}, u32[]{:S(2)}) %collective-permute-start.5) | collective-permute-done | bytes 327712 | tf_op jit(solution)/shard_map/ppermute | solution.py:125
  63.3 6.9 %all-to-all-start.1 = ((f32[16,4,40,256]{3,2,1,0:T(8,128)}), f32[16,4,40,256]{3,2,1,0:T(8,128)}, u32[]{:S(2)}, u32[]{:S(2)}) async-start(f32[16,4,40,256]{3,2,1,0:T(8,128)} %shard_map.69), calls=%async_computation.1 | async-start | bytes 5242880 | tf_op jit(solution)/shard_map/all_to_all | solution.py:292
  71.0 5.3 %shard_map.71 = (f32[12,48,256]{2,1,0:T(8,128)}, f32[12,48,256]{2,1,0:T(8,128)}, f32[12,48,256]{2,1,0:T(8,128)}, f32[12,48,256]{2,1,0:T(8,128)}) custom-call(s32[49]{0:T(128)S(1)} %pad_add_fusion.pick, f32[64,48,256]{2,1,0:T(8,128)S(1)} %bitcast.15), custom_call_target="tpu_custom_call" | custom-call | bytes 4718592 | tf_op jit(solution)/shard_map/pallas_call | solution.py:106
  77.5 2.9 collective-permute-start.8
  80.4 10.7 %shard_map.70.refs_1_.own.refs_0_ = f32[48,2048]{1,0:T(8,128)} custom-call(s32[49]{0:T(128)} %copy-done.31, f32[48,2048]{1,0:T(8,128)} %copy-done.12, f32[64,48,256]{2,1,0:T(8,128)} %bitcast.16, f32[64,48,256]{2,1,0:T(8,128)} %bitcast.17, f32[64,48,256]{2,1,0:T(8,128)} %bitcast.18, f32[64,48,256]{2,1,0:T(8,128)} %bitcast.19, f32[64,48,256]{2,1,0:T(8,128)} %bitcast.20, ...), custom_call_target="tpu_custom_call" | custom-call | flops 1056964608 | bytes 17825792 | tf_op jit(solution)/shard_map/pallas_call | solution.py:147
  91.1 2.6 collective-permute-start.9
  94.8 2.3 shard_map.72
  97.1 6.4 %collective-permute-done.9.other = f32[48,2048]{1,0:T(8,128)S(1)} collective-permute-done((f32[48,2048]{1,0:T(8,128)}, f32[48,2048]{1,0:T(8,128)S(1)}, u32[]{:S(2)}, u32[]{:S(2)}) %collective-permute-start.9) | collective-permute-done | bytes 393248 | tf_op jit(solution)/shard_map/ppermute | solution.py:354
  103.6 6.7 %all-to-all-start.2 = ((f32[16,4,40,256]{3,2,1,0:T(8,128)}), f32[16,4,40,256]{3,2,1,0:T(8,128)S(1)}, u32[]{:S(2)}, u32[]{:S(2)}) async-start(f32[16,4,40,256]{3,2,1,0:T(8,128)} %shard_map.72), calls=%async_computation.2 | async-start | bytes 5242880 | tf_op jit(solution)/shard_map/all_to_all | solution.py:292
  110.3 2.2 collective-permute-start.12
  112.5 3.0 shard_map.73
  116.0 10.9 %shard_map.74.refs_1_.own.refs_0_ = f32[40,2048]{1,0:T(8,128)} custom-call(s32[49]{0:T(128)} %copy-done.31, f32[40,2048]{1,0:T(8,128)} %get-tuple-element.87.own, f32[64,40,256]{2,1,0:T(8,128)} %bitcast.7.came.f0.f1.f2.f3.f4.f5, f32[64,40,256]{2,1,0:T(8,128)} %bitcast.7.came.f0.f1.f2.f3.f4.f5, f32[64,40,256]{2,1,0:T(8,128)} %bitcast.7.came.f0.f1.f2.f3.f4.f5, ...), custom_call_target="tpu_custom_call" | custom-call | flops 880803840 | bytes 17301504 | tf_op jit(solution)/shard_map/pallas_call | solution.py:147
  126.9 2.6 collective-permute-start.13
  130.5 2.7 shard_map.75
  133.2 12.8 %collective-permute-done.13.other = f32[40,2048]{1,0:T(8,128)S(1)} collective-permute-done((f32[40,2048]{1,0:T(8,128)}, f32[40,2048]{1,0:T(8,128)S(1)}, u32[]{:S(2)}, u32[]{:S(2)}) %collective-permute-start.13) | collective-permute-done | bytes 327712 | tf_op jit(solution)/shard_map/ppermute | solution.py:354
  147.6 6.7 %all-to-all-start.3 = ((f32[16,4,32,256]{3,2,1,0:T(8,128)}), f32[16,4,32,256]{3,2,1,0:T(8,128)}, u32[]{:S(2)}, u32[]{:S(2)}) async-start(f32[16,4,32,256]{3,2,1,0:T(8,128)} %shard_map.75), calls=%async_computation.3 | async-start | bytes 4194304 | tf_op jit(solution)/shard_map/all_to_all | solution.py:292
  154.4 4.7 %shard_map.76 = (f32[12,40,256]{2,1,0:T(8,128)}, f32[12,40,256]{2,1,0:T(8,128)}, f32[12,40,256]{2,1,0:T(8,128)}, f32[12,40,256]{2,1,0:T(8,128)}) custom-call(s32[49]{0:T(128)S(1)} %copy-done.33, f32[64,40,256]{2,1,0:T(8,128)S(1)} %bitcast.22), custom_call_target="tpu_custom_call" | custom-call | bytes 3932160 | tf_op jit(solution)/shard_map/pallas_call | solution.py:106
  160.0 1.6 collective-permute-start.16
  161.6 10.8 %shard_map.77.refs_1_.own.refs_0_ = f32[40,2048]{1,0:T(8,128)} custom-call(s32[49]{0:T(128)} %copy-done.31, f32[40,2048]{1,0:T(8,128)} %get-tuple-element.88.own, f32[64,40,256]{2,1,0:T(8,128)} %bitcast.23, f32[64,40,256]{2,1,0:T(8,128)} %bitcast.24, f32[64,40,256]{2,1,0:T(8,128)} %bitcast.25, f32[64,40,256]{2,1,0:T(8,128)} %bitcast.26, ...), custom_call_target="tpu_custom_call" | custom-call | flops 880803840 | bytes 17301504 | tf_op jit(solution)/shard_map/pallas_call | solution.py:147
  173.8 2.3 shard_map.78
  176.1 13.3 %collective-permute-done.17.other = f32[40,2048]{1,0:T(8,128)S(1)} collective-permute-done((f32[40,2048]{1,0:T(8,128)}, f32[40,2048]{1,0:T(8,128)S(1)}, u32[]{:S(2)}, u32[]{:S(2)}) %collective-permute-start.17) | collective-permute-done | bytes 327712 | tf_op jit(solution)/shard_map/ppermute | solution.py:354
  191.3 6.3 %all-to-all-start.4 = ((f32[16,4,48,256]{3,2,1,0:T(8,128)}), f32[16,4,48,256]{3,2,1,0:T(8,128)S(1)}, u32[]{:S(2)}, u32[]{:S(2)}) async-start(f32[16,4,48,256]{3,2,1,0:T(8,128)} %shard_map.78), calls=%async_computation.4 | async-start | bytes 6291456 | tf_op jit(solution)/shard_map/all_to_all | solution.py:292
  199.1 2.7 shard_map.79
  201.8 2.1 collective-permute-start.18
  204.0 10.7 %shard_map.80.refs_1_.own.refs_0_ = f32[32,2048]{1,0:T(8,128)} custom-call(s32[49]{0:T(128)} %copy-done.31, f32[32,2048]{1,0:T(8,128)} %slice.15.own, f32[64,32,256]{2,1,0:T(8,128)} %bitcast.9.came.f0.f1.f2.f3.f4.f5, f32[64,32,256]{2,1,0:T(8,128)} %bitcast.9.came.f0.f1.f2.f3.f4.f5, f32[64,32,256]{2,1,0:T(8,128)} %bitcast.9.came.f0.f1.f2.f3.f4.f5, ...), custom_call_target="tpu_custom_call" | custom-call | flops 704643072 | bytes 16777216 | tf_op jit(solution)/shard_map/pallas_call | solution.py:147
  214.7 2.0 collective-permute-start.21
  217.7 2.3 shard_map.81
  220.0 7.1 %collective-permute-done.21.other = f32[32,2048]{1,0:T(8,128)S(1)} collective-permute-done((f32[32,2048]{1,0:T(8,128)}, f32[32,2048]{1,0:T(8,128)S(1)}, u32[]{:S(2)}, u32[]{:S(2)}) %collective-permute-start.21) | collective-permute-done | bytes 262176 | tf_op jit(solution)/shard_map/ppermute | solution.py:354
  229.4 4.9 %all-to-all-done.4 = f32[16,4,48,256]{3,2,1,0:T(8,128)S(1)} async-done(((f32[16,4,48,256]{3,2,1,0:T(8,128)}), f32[16,4,48,256]{3,2,1,0:T(8,128)S(1)}, u32[]{:S(2)}, u32[]{:S(2)}) %all-to-all-start.4) | async-done | bytes 3145760 | tf_op jit(solution)/shard_map/all_to_all | solution.py:292
  234.3 6.7 %all-to-all-start.5 = ((f32[16,4,40,256]{3,2,1,0:T(8,128)}), f32[16,4,40,256]{3,2,1,0:T(8,128)}, u32[]{:S(2)}, u32[]{:S(2)}) async-start(f32[16,4,40,256]{3,2,1,0:T(8,128)} %shard_map.81), calls=%async_computation.5 | async-start | bytes 5242880 | tf_op jit(solution)/shard_map/all_to_all | solution.py:292
  241.0 5.5 %shard_map.82 = (f32[14,48,256]{2,1,0:T(8,128)}, f32[14,48,256]{2,1,0:T(8,128)}, f32[14,48,256]{2,1,0:T(8,128)}, f32[14,48,256]{2,1,0:T(8,128)}) custom-call(s32[49]{0:T(128)S(1)} %copy-done.35, f32[64,48,256]{2,1,0:T(8,128)S(1)} %bitcast.29, f32[48,2048]{1,0:T(8,128)S(1)} %copy-done.3), custom_call_target="tpu_custom_call" | custom-call | bytes 5505024 | tf_op jit(solution)/shard_map/pallas_call | solution.py:106
  246.7 5.0 %collective-permute-start.23 = (f32[14,48,256]{2,1,0:T(8,128)}, f32[14,48,256]{2,1,0:T(8,128)}, u32[]{:S(2)}, u32[]{:S(2)}) collective-permute-start(f32[14,48,256]{2,1,0:T(8,128)} %get-tuple-element.128), channel_id=1, source_target_pairs={{0,32},{32,0},{64,96},{96,64},{1,33},{33,1},{65,97},{97,65},{2,34}... | collective-permute-start | bytes 2064392 | tf_op jit(solution)/shard_map/ppermute | solution.py:125
  254.1 2.3 shard_map.83
  256.5 16.4 %collective-permute-done.24.refs_2_ = f32[12,32,256]{2,1,0:T(8,128)} collective-permute-done((f32[12,32,256]{2,1,0:T(8,128)S(1)}, f32[12,32,256]{2,1,0:T(8,128)}, u32[]{:S(2)}, u32[]{:S(2)}) %collective-permute-start.24) | collective-permute-done | bytes 393248 | tf_op jit(solution)/shard_map/ppermute | solution.py:125
  272.9 6.8 %all-to-all-start.6 = ((f32[16,4,40,256]{3,2,1,0:T(8,128)}), f32[16,4,40,256]{3,2,1,0:T(8,128)S(1)}, u32[]{:S(2)}, u32[]{:S(2)}) async-start(f32[16,4,40,256]{3,2,1,0:T(8,128)} %shard_map.83), calls=%async_computation.6 | async-start | bytes 5242880 | tf_op jit(solution)/shard_map/all_to_all | solution.py:292
  279.7 4.2 %collective-permute-start.27 = (f32[14,48,256]{2,1,0:T(8,128)}, f32[14,48,256]{2,1,0:T(8,128)}, u32[]{:S(2)}, u32[]{:S(2)}) collective-permute-start(f32[14,48,256]{2,1,0:T(8,128)} %get-tuple-element.139), channel_id=1, source_target_pairs={{0,96},{32,64},{64,32},{96,0},{1,97},{33,65},{65,33},{97,1},{2,98}... | collective-permute-start | bytes 2064392 | tf_op jit(solution)/shard_map/ppermute | solution.py:125
  283.9 3.0 shard_map.84
  289.4 2.3 shard_map.85
  291.7 20.9 %collective-permute-done.25.refs_13_ = f32[14,40,256]{2,1,0:T(8,128)S(1)} collective-permute-done((f32[14,40,256]{2,1,0:T(8,128)}, f32[14,40,256]{2,1,0:T(8,128)S(1)}, u32[]{:S(2)}, u32[]{:S(2)}) %collective-permute-start.25) | collective-permute-done | bytes 573472 | tf_op jit(solution)/shard_map/ppermute | solution.py:125
  314.3 7.0 %all-to-all-start.7 = ((f32[16,4,32,256]{3,2,1,0:T(8,128)}), f32[16,4,32,256]{3,2,1,0:T(8,128)}, u32[]{:S(2)}, u32[]{:S(2)}) async-start(f32[16,4,32,256]{3,2,1,0:T(8,128)} %shard_map.85), calls=%async_computation.7 | async-start | bytes 4194304 | tf_op jit(solution)/shard_map/all_to_all | solution.py:292
  321.3 1.8 collective-permute-start.28
  323.1 4.9 %shard_map.88 = (f32[14,40,256]{2,1,0:T(8,128)}, f32[14,40,256]{2,1,0:T(8,128)}, f32[14,40,256]{2,1,0:T(8,128)}, f32[14,40,256]{2,1,0:T(8,128)}) custom-call(s32[49]{0:T(128)S(1)} %copy-done.35, f32[64,40,256]{2,1,0:T(8,128)S(1)} %bitcast.30, f32[40,2048]{1,0:T(8,128)S(1)} %copy-done.6), custom_call_target="tpu_custom_call" | custom-call | bytes 4587520 | tf_op jit(solution)/shard_map/pallas_call | solution.py:106
  330.0 7.3 %collective-permute-done.28.refs_14_ = f32[14,40,256]{2,1,0:T(8,128)S(1)} collective-permute-done((f32[14,40,256]{2,1,0:T(8,128)}, f32[14,40,256]{2,1,0:T(8,128)S(1)}, u32[]{:S(2)}, u32[]{:S(2)}) %collective-permute-start.28) | collective-permute-done | bytes 573472 | tf_op jit(solution)/shard_map/ppermute | solution.py:125
  338.1 8.7 %shard_map.86 = (f32[2,256,256]{2,1,0:T(8,128)}, f32[2,6,256,256]{3,2,1,0:T(8,128)}) custom-call(s32[1]{0:T(128)} %bitcast.me, f32[12,48,256]{2,1,0:T(8,128)} %get-tuple-element.93.refs_0_, f32[12,48,256]{2,1,0:T(8,128)} %collective-permute-done.7.refs_1_, f32[12,48,256]{2,1,0:T(8,128)} %collective-permute-done.12.refs_2_, ...), custom_call_target="tpu_custom_call" | custom-call | flops 3598712832 | bytes 17432576 | tf_op jit(solution)/shard_map/pallas_call | solution.py:237
  346.8 3.6 all-to-all-done.7
  351.5 2.9 shard_map.87
  354.8 3.2 collective-permute-start.30
  358.1 3.3 collective-permute-done.33.refs_6_
  362.5 7.3 %shard_map.89 = (f32[2,256,256]{2,1,0:T(8,128)}, f32[2,6,256,256]{3,2,1,0:T(8,128)}) custom-call(s32[1]{0:T(128)} %bitcast.me, f32[12,40,256]{2,1,0:T(8,128)} %get-tuple-element.107.refs_0_, f32[12,40,256]{2,1,0:T(8,128)} %copy-done.42, f32[12,40,256]{2,1,0:T(8,128)} %collective-permute-done.20.refs_2_, f32[12,40,256]{2,1,0:T(8,128)} %copy-done.43, ...), custom_call_target="tpu_custom_call" | custom-call | flops 1635778560 | bytes 11927552 | tf_op jit(solution)/shard_map/pallas_call | solution.py:237
  370.9 9.9 %collective-permute-done.30.refs_6_ = f32[14,32,256]{2,1,0:T(8,128)S(1)} collective-permute-done((f32[14,32,256]{2,1,0:T(8,128)}, f32[14,32,256]{2,1,0:T(8,128)S(1)}, u32[]{:S(2)}, u32[]{:S(2)}) %collective-permute-start.30) | collective-permute-done | bytes 458784 | tf_op jit(solution)/shard_map/ppermute | solution.py:125
  381.7 6.9 %shard_map.90 = (f32[2,256,256]{2,1,0:T(8,128)}, f32[2,6,256,256]{3,2,1,0:T(8,128)}) custom-call(s32[1]{0:T(128)} %bitcast.me, f32[12,32,256]{2,1,0:T(8,128)} %get-tuple-element.114.refs_0_, f32[12,32,256]{2,1,0:T(8,128)} %copy-done.47, f32[12,32,256]{2,1,0:T(8,128)} %collective-permute-done.24.refs_2_, f32[12,32,256]{2,1,0:T(8,128)} %copy-done.48, ...), custom_call_target="tpu_custom_call" | custom-call | flops 1308622848 | bytes 11010048 | tf_op jit(solution)/shard_map/pallas_call | solution.py:237
  (188 shorter events, 36.4 us)
Async XLA Ops:
  1.8 14.7 %copy-start.12 = (f32[48,2048]{1,0:T(8,128)}, f32[48,2048]{1,0:T(8,128)S(1)}, u32[]{:S(2)}) copy-start(f32[48,2048]{1,0:T(8,128)S(1)} %slice.12.own) | copy-start | bytes 1179652
  1.8 12.4 %collective-permute-start = (f32[48,2048]{1,0:T(8,128)S(1)}, f32[48,2048]{1,0:T(8,128)S(1)}, u32[]{:S(2)}, u32[]{:S(2)}) collective-permute-start(f32[48,2048]{1,0:T(8,128)S(1)} %slice.12.own), channel_id=1, source_target_pairs={{0,1},{1,0},{2,3},{3,2},{4,5},{5,4},{6,7},{7,6},{8,9},{9,8},{10,11... | collective-permute-start | bytes 1179656 | tf_op jit(solution)/shard_map/ppermute | solution.py:301
  16.5 10.9 %copy-start.13 = (f32[40,2048]{1,0:T(8,128)S(1)}, f32[40,2048]{1,0:T(8,128)}, u32[]{:S(2)}) copy-start(f32[40,2048]{1,0:T(8,128)} %get-tuple-element.88.own) | copy-start | bytes 983044
  16.6 46.8 %all-to-all-start = ((f32[16,4,48,256]{3,2,1,0:T(8,128)}), f32[16,4,48,256]{3,2,1,0:T(8,128)S(1)}, u32[]{:S(2)}, u32[]{:S(2)}) async-start(f32[16,4,48,256]{3,2,1,0:T(8,128)} %shard_map.68), calls=%async_computation | async-start | bytes 6291456 | tf_op jit(solution)/shard_map/all_to_all | solution.py:292
  24.3 12.4 %collective-permute-start.3 = (f32[32,2048]{1,0:T(8,128)}, f32[32,2048]{1,0:T(8,128)}, u32[]{:S(2)}, u32[]{:S(2)}) collective-permute-start(f32[32,2048]{1,0:T(8,128)} %slice.15.own), channel_id=1, source_target_pairs={{0,1},{1,0},{2,3},{3,2},{4,5},{5,4},{6,7},{7,6},{8,9},{9,8},{10,11... | collective-permute-start | bytes 786440 | tf_op jit(solution)/shard_map/ppermute | solution.py:306
  27.3 18.8 %copy-start.14 = (f32[40,2048]{1,0:T(8,128)S(1)}, f32[40,2048]{1,0:T(8,128)}, u32[]{:S(2)}) copy-start(f32[40,2048]{1,0:T(8,128)} %get-tuple-element.87.own) | copy-start | bytes 983044
  27.3 11.8 %collective-permute-start.1 = (f32[40,2048]{1,0:T(8,128)}, f32[40,2048]{1,0:T(8,128)S(1)}, u32[]{:S(2)}, u32[]{:S(2)}) collective-permute-start(f32[40,2048]{1,0:T(8,128)} %get-tuple-element.87.own), channel_id=1, source_target_pairs={{0,1},{1,0},{2,3},{3,2},{4,5},{5,4},{6,7},{7,6},{8,9},{9,8},{10,11... | collective-permute-start | bytes 983048 | tf_op jit(solution)/shard_map/ppermute | solution.py:306
  27.4 18.7 %collective-permute-start.2 = (f32[40,2048]{1,0:T(8,128)S(1)}, f32[40,2048]{1,0:T(8,128)S(1)}, u32[]{:S(2)}, u32[]{:S(2)}) collective-permute-start(f32[40,2048]{1,0:T(8,128)S(1)} %copy-done.13), channel_id=1, source_target_pairs={{0,1},{1,0},{2,3},{3,2},{4,5},{5,4},{6,7},{7,6},{8,9},{9,8},{10,11... | collective-permute-start | bytes 983048 | tf_op jit(solution)/shard_map/ppermute | solution.py:306
  32.4 21.0 %collective-permute-start.4 = (f32[160,512]{1,0:T(8,128)S(1)}, f32[160,512]{1,0:T(8,128)S(1)}, u32[]{:S(2)}, u32[]{:S(2)}) collective-permute-start(f32[160,512]{1,0:T(8,128)S(1)} %get-tuple-element.175), channel_id=1, source_target_pairs={{0,64},{32,96},{64,0},{96,32},{1,65},{33,97},{65,1},{97,33},{2,66}... | collective-permute-start | bytes 983048 | tf_op jit(solution)/shard_map/ppermute | solution.py:125
  32.9 29.7 %collective-permute-start.5 = (f32[160,512]{1,0:T(8,128)S(1)}, f32[160,512]{1,0:T(8,128)S(1)}, u32[]{:S(2)}, u32[]{:S(2)}) collective-permute-start(f32[160,512]{1,0:T(8,128)S(1)} %get-tuple-element.174), channel_id=1, source_target_pairs={{0,96},{32,64},{64,32},{96,0},{1,97},{33,65},{65,33},{97,1},{2,98}... | collective-permute-start | bytes 983048 | tf_op jit(solution)/shard_map/ppermute | solution.py:125
  36.7 26.6 %collective-permute-start.6 = (f32[160,512]{1,0:T(8,128)S(1)}, f32[160,512]{1,0:T(8,128)}, u32[]{:S(2)}, u32[]{:S(2)}) collective-permute-start(f32[160,512]{1,0:T(8,128)S(1)} %get-tuple-element.173), channel_id=1, source_target_pairs={{0,32},{32,0},{64,96},{96,64},{1,33},{33,1},{65,97},{97,65},{2,34}... | collective-permute-start | bytes 983048 | tf_op jit(solution)/shard_map/ppermute | solution.py:125
  46.1 16.4 %copy-start.19 = (f32[40,2048]{1,0:T(8,128)}, f32[40,2048]{1,0:T(8,128)S(1)}, u32[]{:S(2)}) copy-start(f32[40,2048]{1,0:T(8,128)S(1)} %collective-permute-done.2.refs_0_.other) | copy-start | bytes 983044
  63.3 40.2 %all-to-all-start.1 = ((f32[16,4,40,256]{3,2,1,0:T(8,128)}), f32[16,4,40,256]{3,2,1,0:T(8,128)}, u32[]{:S(2)}, u32[]{:S(2)}) async-start(f32[16,4,40,256]{3,2,1,0:T(8,128)} %shard_map.69), calls=%async_computation.1 | async-start | bytes 5242880 | tf_op jit(solution)/shard_map/all_to_all | solution.py:292
  76.4 27.2 %collective-permute-start.7 = (f32[12,48,256]{2,1,0:T(8,128)}, f32[12,48,256]{2,1,0:T(8,128)}, u32[]{:S(2)}, u32[]{:S(2)}) collective-permute-start(f32[12,48,256]{2,1,0:T(8,128)} %get-tuple-element.96), channel_id=1, source_target_pairs={{0,64},{32,96},{64,0},{96,32},{1,65},{33,97},{65,1},{97,33},{2,66}... | collective-permute-start | bytes 1769480 | tf_op jit(solution)/shard_map/ppermute | solution.py:125
  77.5 16.2 %copy-start.20 = (f32[40,2048]{1,0:T(8,128)S(1)}, f32[40,2048]{1,0:T(8,128)}, u32[]{:S(2)}) copy-start(f32[40,2048]{1,0:T(8,128)} %copy-done.19) | copy-start | bytes 983044
  77.5 16.2 %copy-start.22 = (f32[12,48,256]{2,1,0:T(8,128)S(1)}, f32[12,48,256]{2,1,0:T(8,128)}, u32[]{:S(2)}) copy-start(f32[12,48,256]{2,1,0:T(8,128)} %get-tuple-element.93.refs_0_) | copy-start | bytes 1769476
  77.5 26.0 %collective-permute-start.8 = (f32[12,48,256]{2,1,0:T(8,128)}, f32[12,48,256]{2,1,0:T(8,128)}, u32[]{:S(2)}, u32[]{:S(2)}) collective-permute-start(f32[12,48,256]{2,1,0:T(8,128)} %get-tuple-element.97), channel_id=1, source_target_pairs={{0,32},{32,0},{64,96},{96,64},{1,33},{33,1},{65,97},{97,65},{2,34}... | collective-permute-start | bytes 1769480 | tf_op jit(solution)/shard_map/ppermute | solution.py:125
  91.1 12.4 %collective-permute-start.9 = (f32[48,2048]{1,0:T(8,128)}, f32[48,2048]{1,0:T(8,128)S(1)}, u32[]{:S(2)}, u32[]{:S(2)}) collective-permute-start(f32[48,2048]{1,0:T(8,128)} %shard_map.70.refs_1_.own.refs_0_), channel_id=1, source_target_pairs={{0,1},{1,0},{2,3},{3,2},{4,5},{5,4},{6,7},{7,6},{8,9},{9,8},{10,11... | collective-permute-start | bytes 1179656 | tf_op jit(solution)/shard_map/ppermute | solution.py:354
  103.6 44.1 %all-to-all-start.2 = ((f32[16,4,40,256]{3,2,1,0:T(8,128)}), f32[16,4,40,256]{3,2,1,0:T(8,128)S(1)}, u32[]{:S(2)}, u32[]{:S(2)}) async-start(f32[16,4,40,256]{3,2,1,0:T(8,128)} %shard_map.72), calls=%async_computation.2 | async-start | bytes 5242880 | tf_op jit(solution)/shard_map/all_to_all | solution.py:292
  110.3 37.3 %collective-permute-start.12 = (f32[12,48,256]{2,1,0:T(8,128)}, f32[12,48,256]{2,1,0:T(8,128)}, u32[]{:S(2)}, u32[]{:S(2)}) collective-permute-start(f32[12,48,256]{2,1,0:T(8,128)} %get-tuple-element.105), channel_id=1, source_target_pairs={{0,96},{32,64},{64,32},{96,0},{1,97},{33,65},{65,33},{97,1},{2,98}... | collective-permute-start | bytes 1769480 | tf_op jit(solution)/shard_map/ppermute | solution.py:125
  115.4 31.3 %collective-permute-start.10 = (f32[12,40,256]{2,1,0:T(8,128)}, f32[12,40,256]{2,1,0:T(8,128)S(1)}, u32[]{:S(2)}, u32[]{:S(2)}) collective-permute-start(f32[12,40,256]{2,1,0:T(8,128)} %get-tuple-element.103), channel_id=1, source_target_pairs={{0,64},{32,96},{64,0},{96,32},{1,65},{33,97},{65,1},{97,33},{2,66}... | collective-permute-start | bytes 1474568 | tf_op jit(solution)/shard_map/ppermute | solution.py:125
  116.0 13.5 %copy-start.15 = (f32[32,2048]{1,0:T(8,128)S(1)}, f32[32,2048]{1,0:T(8,128)}, u32[]{:S(2)}) copy-start(f32[32,2048]{1,0:T(8,128)} %slice.15.own) | copy-start | bytes 786436
  116.0 13.5 %copy-start.24 = (f32[12,40,256]{2,1,0:T(8,128)S(1)}, f32[12,40,256]{2,1,0:T(8,128)}, u32[]{:S(2)}) copy-start(f32[12,40,256]{2,1,0:T(8,128)} %get-tuple-element.100.refs_0_.refs_4_) | copy-start | bytes 1474564
  116.0 30.8 %collective-permute-start.11 = (f32[12,40,256]{2,1,0:T(8,128)}, f32[12,40,256]{2,1,0:T(8,128)S(1)}, u32[]{:S(2)}, u32[]{:S(2)}) collective-permute-start(f32[12,40,256]{2,1,0:T(8,128)} %get-tuple-element.104), channel_id=1, source_target_pairs={{0,32},{32,0},{64,96},{96,64},{1,33},{33,1},{65,97},{97,65},{2,34}... | collective-permute-start | bytes 1474568 | tf_op jit(solution)/shard_map/ppermute | solution.py:125
  126.9 19.2 %collective-permute-start.13 = (f32[40,2048]{1,0:T(8,128)}, f32[40,2048]{1,0:T(8,128)S(1)}, u32[]{:S(2)}, u32[]{:S(2)}) collective-permute-start(f32[40,2048]{1,0:T(8,128)} %shard_map.74.refs_1_.own.refs_0_), channel_id=1, source_target_pairs={{0,1},{1,0},{2,3},{3,2},{4,5},{5,4},{6,7},{7,6},{8,9},{9,8},{10,11... | collective-permute-start | bytes 983048 | tf_op jit(solution)/shard_map/ppermute | solution.py:354
  133.2 21.2 %copy-start.33 = (s32[49]{0:T(128)S(1)}, s32[49]{0:T(128)}, u32[]{:S(2)}) copy-start(s32[49]{0:T(128)} %copy-done.31) | copy-start | bytes 592
  146.8 12.3 %copy-start.54 = (f32[12,40,256]{2,1,0:T(8,128)}, f32[12,40,256]{2,1,0:T(8,128)S(1)}, u32[]{:S(2)}) copy-start(f32[12,40,256]{2,1,0:T(8,128)S(1)} %collective-permute-done.10.refs_5_) | copy-start | bytes 1474564
  147.6 11.5 %copy-start.1 = (f32[16,4,40,256]{3,2,1,0:T(8,128)}, f32[16,4,40,256]{3,2,1,0:T(8,128)S(1)}, u32[]{:S(2)}) copy-start(f32[16,4,40,256]{3,2,1,0:T(8,128)S(1)} %all-to-all-done.2) | copy-start | bytes 7864324
  147.6 42.6 %all-to-all-start.3 = ((f32[16,4,32,256]{3,2,1,0:T(8,128)}), f32[16,4,32,256]{3,2,1,0:T(8,128)}, u32[]{:S(2)}, u32[]{:S(2)}) async-start(f32[16,4,32,256]{3,2,1,0:T(8,128)} %shard_map.75), calls=%async_computation.3 | async-start | bytes 4194304 | tf_op jit(solution)/shard_map/all_to_all | solution.py:292
  159.1 31.1 %collective-permute-start.14 = (f32[12,40,256]{2,1,0:T(8,128)}, f32[12,40,256]{2,1,0:T(8,128)S(1)}, u32[]{:S(2)}, u32[]{:S(2)}) collective-permute-start(f32[12,40,256]{2,1,0:T(8,128)} %get-tuple-element.110), channel_id=1, source_target_pairs={{0,64},{32,96},{64,0},{96,32},{1,65},{33,97},{65,1},{97,33},{2,66}... | collective-permute-start | bytes 1474568 | tf_op jit(solution)/shard_map/ppermute | solution.py:125
  159.2 13.6 %copy-start.3 = (f32[48,2048]{1,0:T(8,128)S(1)}, f32[48,2048]{1,0:T(8,128)}, u32[]{:S(2)}) copy-start(f32[48,2048]{1,0:T(8,128)} %shard_map.70.refs_1_.own.refs_0_) | copy-start | bytes 1179652
  159.2 13.6 %copy-start.17 = (f32[12,40,256]{2,1,0:T(8,128)S(1)}, f32[12,40,256]{2,1,0:T(8,128)}, u32[]{:S(2)}) copy-start(f32[12,40,256]{2,1,0:T(8,128)} %get-tuple-element.107.refs_0_) | copy-start | bytes 1474564
  159.2 31.0 %collective-permute-start.15 = (f32[12,40,256]{2,1,0:T(8,128)}, f32[12,40,256]{2,1,0:T(8,128)S(1)}, u32[]{:S(2)}, u32[]{:S(2)}) collective-permute-start(f32[12,40,256]{2,1,0:T(8,128)} %get-tuple-element.111), channel_id=1, source_target_pairs={{0,32},{32,0},{64,96},{96,64},{1,33},{33,1},{65,97},{97,65},{2,34}... | collective-permute-start | bytes 1474568 | tf_op jit(solution)/shard_map/ppermute | solution.py:125
  160.0 30.2 %collective-permute-start.16 = (f32[12,40,256]{2,1,0:T(8,128)S(1)}, f32[12,40,256]{2,1,0:T(8,128)S(1)}, u32[]{:S(2)}, u32[]{:S(2)}) collective-permute-start(f32[12,40,256]{2,1,0:T(8,128)S(1)} %copy-done.57), channel_id=1, source_target_pairs={{0,96},{32,64},{64,32},{96,0},{1,97},{33,65},{65,33},{97,1},{2,98}... | collective-permute-start | bytes 1474568 | tf_op jit(solution)/shard_map/ppermute | solution.py:125
  172.3 17.1 %collective-permute-start.17 = (f32[40,2048]{1,0:T(8,128)}, f32[40,2048]{1,0:T(8,128)S(1)}, u32[]{:S(2)}, u32[]{:S(2)}) collective-permute-start(f32[40,2048]{1,0:T(8,128)} %shard_map.77.refs_1_.own.refs_0_), channel_id=1, source_target_pairs={{0,1},{1,0},{2,3},{3,2},{4,5},{5,4},{6,7},{7,6},{8,9},{9,8},{10,11... | collective-permute-start | bytes 983048 | tf_op jit(solution)/shard_map/ppermute | solution.py:354
  191.3 42.9 %all-to-all-start.4 = ((f32[16,4,48,256]{3,2,1,0:T(8,128)}), f32[16,4,48,256]{3,2,1,0:T(8,128)S(1)}, u32[]{:S(2)}, u32[]{:S(2)}) async-start(f32[16,4,48,256]{3,2,1,0:T(8,128)} %shard_map.78), calls=%async_computation.4 | async-start | bytes 6291456 | tf_op jit(solution)/shard_map/all_to_all | solution.py:292
  197.6 31.8 %collective-permute-start.20 = (f32[12,40,256]{2,1,0:T(8,128)}, f32[12,40,256]{2,1,0:T(8,128)}, u32[]{:S(2)}, u32[]{:S(2)}) collective-permute-start(f32[12,40,256]{2,1,0:T(8,128)} %get-tuple-element.120), channel_id=1, source_target_pairs={{0,96},{32,64},{64,32},{96,0},{1,97},{33,65},{65,33},{97,1},{2,98}... | collective-permute-start | bytes 1474568 | tf_op jit(solution)/shard_map/ppermute | solution.py:125
  201.8 26.0 %collective-permute-start.18 = (f32[12,32,256]{2,1,0:T(8,128)}, f32[12,32,256]{2,1,0:T(8,128)S(1)}, u32[]{:S(2)}, u32[]{:S(2)}) collective-permute-start(f32[12,32,256]{2,1,0:T(8,128)} %get-tuple-element.118), channel_id=1, source_target_pairs={{0,64},{32,96},{64,0},{96,32},{1,65},{33,97},{65,1},{97,33},{2,66}... | collective-permute-start | bytes 1179656 | tf_op jit(solution)/shard_map/ppermute | solution.py:125
  204.0 12.7 %copy-start.8 = (f32[40,2048]{1,0:T(8,128)S(1)}, f32[40,2048]{1,0:T(8,128)}, u32[]{:S(2)}) copy-start(f32[40,2048]{1,0:T(8,128)} %shard_map.74.refs_1_.own.refs_0_) | copy-start | bytes 983044
  204.0 12.7 %copy-start.18 = (f32[12,32,256]{2,1,0:T(8,128)S(1)}, f32[12,32,256]{2,1,0:T(8,128)}, u32[]{:S(2)}) copy-start(f32[12,32,256]{2,1,0:T(8,128)} %get-tuple-element.114.refs_0_) | copy-start | bytes 1179652
  204.0 12.7 %copy-start.26 = (f32[40,2048]{1,0:T(8,128)S(1)}, f32[40,2048]{1,0:T(8,128)}, u32[]{:S(2)}) copy-start(f32[40,2048]{1,0:T(8,128)} %copy-done.25) | copy-start | bytes 983044
  204.0 23.9 %collective-permute-start.19 = (f32[12,32,256]{2,1,0:T(8,128)}, f32[12,32,256]{2,1,0:T(8,128)S(1)}, u32[]{:S(2)}, u32[]{:S(2)}) collective-permute-start(f32[12,32,256]{2,1,0:T(8,128)} %get-tuple-element.119), channel_id=1, source_target_pairs={{0,32},{32,0},{64,96},{96,64},{1,33},{33,1},{65,97},{97,65},{2,34}... | collective-permute-start | bytes 1179656 | tf_op jit(solution)/shard_map/ppermute | solution.py:125
  214.7 12.4 %collective-permute-start.21 = (f32[32,2048]{1,0:T(8,128)}, f32[32,2048]{1,0:T(8,128)S(1)}, u32[]{:S(2)}, u32[]{:S(2)}) collective-permute-start(f32[32,2048]{1,0:T(8,128)} %shard_map.80.refs_1_.own.refs_0_), channel_id=1, source_target_pairs={{0,1},{1,0},{2,3},{3,2},{4,5},{5,4},{6,7},{7,6},{8,9},{9,8},{10,11... | collective-permute-start | bytes 786440 | tf_op jit(solution)/shard_map/ppermute | solution.py:354
  234.3 38.6 %all-to-all-start.5 = ((f32[16,4,40,256]{3,2,1,0:T(8,128)}), f32[16,4,40,256]{3,2,1,0:T(8,128)}, u32[]{:S(2)}, u32[]{:S(2)}) async-start(f32[16,4,40,256]{3,2,1,0:T(8,128)} %shard_map.81), calls=%async_computation.5 | async-start | bytes 5242880 | tf_op jit(solution)/shard_map/all_to_all | solution.py:292
  241.0 10.7 %copy-start.58 = (f32[12,32,256]{2,1,0:T(8,128)S(1)}, f32[12,32,256]{2,1,0:T(8,128)}, u32[]{:S(2)}) copy-start(f32[12,32,256]{2,1,0:T(8,128)} %get-tuple-element.129) | copy-start | bytes 1179652
  241.0 12.0 %copy-start.5 = (f32[40,2048]{1,0:T(8,128)S(1)}, f32[40,2048]{1,0:T(8,128)}, u32[]{:S(2)}) copy-start(f32[40,2048]{1,0:T(8,128)} %shard_map.77.refs_1_.own.refs_0_) | copy-start | bytes 983044
  241.0 12.0 %copy-start.28 = (f32[40,2048]{1,0:T(8,128)S(1)}, f32[40,2048]{1,0:T(8,128)}, u32[]{:S(2)}) copy-start(f32[40,2048]{1,0:T(8,128)} %copy-done.27) | copy-start | bytes 983044
  246.6 26.3 %collective-permute-start.22 = (f32[14,48,256]{2,1,0:T(8,128)}, f32[14,48,256]{2,1,0:T(8,128)}, u32[]{:S(2)}, u32[]{:S(2)}) collective-permute-start(f32[14,48,256]{2,1,0:T(8,128)} %get-tuple-element.127), channel_id=1, source_target_pairs={{0,64},{32,96},{64,0},{96,32},{1,65},{33,97},{65,1},{97,33},{2,66}... | collective-permute-start | bytes 2064392 | tf_op jit(solution)/shard_map/ppermute | solution.py:125
  246.7 26.2 %collective-permute-start.23 = (f32[14,48,256]{2,1,0:T(8,128)}, f32[14,48,256]{2,1,0:T(8,128)}, u32[]{:S(2)}, u32[]{:S(2)}) collective-permute-start(f32[14,48,256]{2,1,0:T(8,128)} %get-tuple-element.128), channel_id=1, source_target_pairs={{0,32},{32,0},{64,96},{96,64},{1,33},{33,1},{65,97},{97,65},{2,34}... | collective-permute-start | bytes 2064392 | tf_op jit(solution)/shard_map/ppermute | solution.py:125
  251.7 21.1 %collective-permute-start.24 = (f32[12,32,256]{2,1,0:T(8,128)S(1)}, f32[12,32,256]{2,1,0:T(8,128)}, u32[]{:S(2)}, u32[]{:S(2)}) collective-permute-start(f32[12,32,256]{2,1,0:T(8,128)S(1)} %copy-done.58), channel_id=1, source_target_pairs={{0,96},{32,64},{64,32},{96,0},{1,97},{33,65},{65,33},{97,1},{2,98}... | collective-permute-start | bytes 1179656 | tf_op jit(solution)/shard_map/ppermute | solution.py:125
  272.9 11.0 %copy-start.9 = (f32[40,2048]{1,0:T(8,128)S(1)}, f32[40,2048]{1,0:T(8,128)}, u32[]{:S(2)}) copy-start(f32[40,2048]{1,0:T(8,128)} %shard_map.74.refs_1_.own.refs_0_) | copy-start | bytes 983044
  272.9 41.4 %all-to-all-start.6 = ((f32[16,4,40,256]{3,2,1,0:T(8,128)}), f32[16,4,40,256]{3,2,1,0:T(8,128)S(1)}, u32[]{:S(2)}, u32[]{:S(2)}) async-start(f32[16,4,40,256]{3,2,1,0:T(8,128)} %shard_map.83), calls=%async_computation.6 | async-start | bytes 5242880 | tf_op jit(solution)/shard_map/all_to_all | solution.py:292
  279.7 34.6 %collective-permute-start.27 = (f32[14,48,256]{2,1,0:T(8,128)}, f32[14,48,256]{2,1,0:T(8,128)}, u32[]{:S(2)}, u32[]{:S(2)}) collective-permute-start(f32[14,48,256]{2,1,0:T(8,128)} %get-tuple-element.139), channel_id=1, source_target_pairs={{0,96},{32,64},{64,32},{96,0},{1,97},{33,65},{65,33},{97,1},{2,98}... | collective-permute-start | bytes 2064392 | tf_op jit(solution)/shard_map/ppermute | solution.py:125
  286.9 25.7 %collective-permute-start.25 = (f32[14,40,256]{2,1,0:T(8,128)}, f32[14,40,256]{2,1,0:T(8,128)S(1)}, u32[]{:S(2)}, u32[]{:S(2)}) collective-permute-start(f32[14,40,256]{2,1,0:T(8,128)} %get-tuple-element.137), channel_id=1, source_target_pairs={{0,64},{32,96},{64,0},{96,32},{1,65},{33,97},{65,1},{97,33},{2,66}... | collective-permute-start | bytes 1720328 | tf_op jit(solution)/shard_map/ppermute | solution.py:125
  288.3 24.4 %collective-permute-start.26 = (f32[14,40,256]{2,1,0:T(8,128)}, f32[14,40,256]{2,1,0:T(8,128)S(1)}, u32[]{:S(2)}, u32[]{:S(2)}) collective-permute-start(f32[14,40,256]{2,1,0:T(8,128)} %get-tuple-element.138), channel_id=1, source_target_pairs={{0,32},{32,0},{64,96},{96,64},{1,33},{33,1},{65,97},{97,65},{2,34}... | collective-permute-start | bytes 1720328 | tf_op jit(solution)/shard_map/ppermute | solution.py:125
  291.7 31.4 %copy-start.6 = (f32[40,2048]{1,0:T(8,128)S(1)}, f32[40,2048]{1,0:T(8,128)}, u32[]{:S(2)}) copy-start(f32[40,2048]{1,0:T(8,128)} %shard_map.77.refs_1_.own.refs_0_) | copy-start | bytes 983044
  314.3 36.1 %all-to-all-start.7 = ((f32[16,4,32,256]{3,2,1,0:T(8,128)}), f32[16,4,32,256]{3,2,1,0:T(8,128)}, u32[]{:S(2)}, u32[]{:S(2)}) async-start(f32[16,4,32,256]{3,2,1,0:T(8,128)} %shard_map.85), calls=%async_computation.7 | async-start | bytes 4194304 | tf_op jit(solution)/shard_map/all_to_all | solution.py:292
  321.3 16.0 %collective-permute-start.28 = (f32[14,40,256]{2,1,0:T(8,128)}, f32[14,40,256]{2,1,0:T(8,128)S(1)}, u32[]{:S(2)}, u32[]{:S(2)}) collective-permute-start(f32[14,40,256]{2,1,0:T(8,128)} %get-tuple-element.151), channel_id=1, source_target_pairs={{0,96},{32,64},{64,32},{96,0},{1,97},{33,65},{65,33},{97,1},{2,98}... | collective-permute-start | bytes 1720328 | tf_op jit(solution)/shard_map/ppermute | solution.py:125
  328.0 29.9 %collective-permute-start.32 = (f32[14,40,256]{2,1,0:T(8,128)}, f32[14,40,256]{2,1,0:T(8,128)S(1)}, u32[]{:S(2)}, u32[]{:S(2)}) collective-permute-start(f32[14,40,256]{2,1,0:T(8,128)} %get-tuple-element.166), channel_id=1, source_target_pairs={{0,64},{32,96},{64,0},{96,32},{1,65},{33,97},{65,1},{97,33},{2,66}... | collective-permute-start | bytes 1720328 | tf_op jit(solution)/shard_map/ppermute | solution.py:125
  328.1 33.3 %collective-permute-start.33 = (f32[14,40,256]{2,1,0:T(8,128)}, f32[14,40,256]{2,1,0:T(8,128)S(1)}, u32[]{:S(2)}, u32[]{:S(2)}) collective-permute-start(f32[14,40,256]{2,1,0:T(8,128)} %get-tuple-element.167), channel_id=1, source_target_pairs={{0,96},{32,64},{64,32},{96,0},{1,97},{33,65},{65,33},{97,1},{2,98}... | collective-permute-start | bytes 1720328 | tf_op jit(solution)/shard_map/ppermute | solution.py:125
  329.4 32.0 %collective-permute-start.34 = (f32[14,40,256]{2,1,0:T(8,128)}, f32[14,40,256]{2,1,0:T(8,128)S(1)}, u32[]{:S(2)}, u32[]{:S(2)}) collective-permute-start(f32[14,40,256]{2,1,0:T(8,128)} %get-tuple-element.168), channel_id=1, source_target_pairs={{0,32},{32,0},{64,96},{96,64},{1,33},{33,1},{65,97},{97,65},{2,34}... | collective-permute-start | bytes 1720328 | tf_op jit(solution)/shard_map/ppermute | solution.py:125
  354.3 16.6 %collective-permute-start.29 = (f32[14,32,256]{2,1,0:T(8,128)}, f32[14,32,256]{2,1,0:T(8,128)S(1)}, u32[]{:S(2)}, u32[]{:S(2)}) collective-permute-start(f32[14,32,256]{2,1,0:T(8,128)} %get-tuple-element.158), channel_id=1, source_target_pairs={{0,64},{32,96},{64,0},{96,32},{1,65},{33,97},{65,1},{97,33},{2,66}... | collective-permute-start | bytes 1376264 | tf_op jit(solution)/shard_map/ppermute | solution.py:125
  354.8 26.0 %collective-permute-start.30 = (f32[14,32,256]{2,1,0:T(8,128)}, f32[14,32,256]{2,1,0:T(8,128)S(1)}, u32[]{:S(2)}, u32[]{:S(2)}) collective-permute-start(f32[14,32,256]{2,1,0:T(8,128)} %get-tuple-element.159), channel_id=1, source_target_pairs={{0,96},{32,64},{64,32},{96,0},{1,97},{33,65},{65,33},{97,1},{2,98}... | collective-permute-start | bytes 1376264 | tf_op jit(solution)/shard_map/ppermute | solution.py:125
  357.9 22.8 %collective-permute-start.31 = (f32[14,32,256]{2,1,0:T(8,128)}, f32[14,32,256]{2,1,0:T(8,128)S(1)}, u32[]{:S(2)}, u32[]{:S(2)}) collective-permute-start(f32[14,32,256]{2,1,0:T(8,128)} %get-tuple-element.160), channel_id=1, source_target_pairs={{0,32},{32,0},{64,96},{96,64},{1,33},{33,1},{65,97},{97,65},{2,34}... | collective-permute-start | bytes 1376264 | tf_op jit(solution)/shard_map/ppermute | solution.py:125
  (38 other events, 134.8 us)

commit v4 on v3

--- a/solution.py
+++ b/solution.py
@@ -11,6 +11,9 @@
 MOST = 2
 SIZES = (48, 40, 40, 32)
 LATE = 2
+ORDER = (3, 0, 1, 2)
+HOME = 1
+EARLY = 1
 SWAPPED = (0, 0, 0, 0)
 FLIPS = (0, 2, 3, 1)
 STEP = 0.5
@@ -294,16 +297,18 @@
 
     runs = range(len(SIZES))
     starts = tuple(sum(SIZES[:i]) for i in runs)
-    turns = [("x", i) for i in runs] + [("y", i) for i in runs]
+    turns = [("x", i) for i in ORDER] + [("y", i) for i in runs]
     own, other, shared, parts = {}, {}, {}, {}
     slices = [lax.slice_in_dim(expression, starts[i], starts[i] + SIZES[i], axis=0) for i in runs]
-    own["x", 0] = slices[0]
-    other["x", 0] = lax.ppermute(slices[0], "genes", swap)
-    sent = pack(send, own["x", 0], other["x", 0])
-    sent, expression, *slices[1:] = lax.optimization_barrier((sent, expression, *slices[1:]))
-    for i in runs[1:]:
-        own["x", i] = slices[i]
-        other["x", i] = lax.ppermute(slices[i], "genes", swap)
+    first = ORDER[0]
+    own["x", first] = slices[first]
+    other["x", first] = lax.ppermute(slices[first], "genes", swap)
+    sent = pack(send, own["x", first], other["x", first])
+    rest = [slices[i] for i in ORDER[1:]]
+    sent, expression, *rest = lax.optimization_barrier((sent, expression, *rest))
+    for i, piece in zip(ORDER[1:], rest):
+        own["x", i] = piece
+        other["x", i] = lax.ppermute(piece, "genes", swap)
     home = [
         lax.dynamic_slice_in_dim(expression, (me ^ flip) * 512, 512, axis=1) for flip in FLIPS
     ]
@@ -319,23 +324,27 @@
         if at + 1 < len(turns):
             then, before, ties = turns[at + 1], [], [arrived]
             if at == 0:
-                before = [other["x", j] for j in runs[2:]]
-                ties += home[1:]
+                before = [other["x", j] for j in ORDER[2 : 2 + EARLY]]
             else:
                 last = turns[at - 1]
                 before = [shared[last][0]]
+                if at == 1:
+                    before += [other["x", j] for j in ORDER[2 + EARLY :]]
                 ties += [shared[last][3], parts[last][1], parts[last][3]]
                 if last[0] == "x":
                     before.append(own["y", last[1]])
                 if at >= 2:
                     ties.append(parts[turns[at - 2]][2])
-                due = [j for j in runs if j + 1 + SWAPPED[j] == at]
+                due = [j for j in runs if ORDER.index(j) + 1 + SWAPPED[j] == at]
                 ties += [other["y", j] for j in due]
+            if at == HOME:
+                ties += home[1:]
             sent = pack(send, own[then], other[then], before)
             sent, arrived, *ties = lax.optimization_barrier((sent, *ties))
-            if at == 0:
-                home[1:] = ties
-            else:
+            if at == HOME:
+                home[1:] = ties[-3:]
+                ties = ties[:-3]
+            if at:
                 for j in reversed(due):
                     other["y", j] = ties.pop()
                 if at >= 2:

time: 391 us -> 391 us (level); the launches traced: 389 us -> 384 us
  waiting for transfers between devices: 132 us -> 127 us
  local copies, waits for them, and re-layouts: 25.4 us -> 29.6 us
  starting transfers between devices: 110 us -> 106 us
    ppermute x4, waiting for transfers between devices: 39.7 us -> 30.2 us  [per_device(): other['y', i] = lax.ppermute(own['y', i], 'genes', swap)]
    unnamed x119 -> x139, local copies, waits for them, and re-layouts: 18.9 us -> 24 us
where the time goes in v4:
time: 391 us; the launch traced here: 384 us
  waiting for transfers between devices  127 us (32%)
  Pallas kernels  117 us (30%)
  starting transfers between devices  106 us (27%)
  local copies, waits for them, and re-layouts  29.6 us (8%)
    ppermute x27, waiting for transfers between devices, handed(): return lax.ppermute(part, 'cells', [(c, c ^ flip) for c in range(4)])  70.3 us
    all_to_all x8, starting transfers between devices, exchange(): came = lax.all_to_all(sent, 'genes', 0, 0, axis_index_groups=planes)  52.2 us
    pallas_call x4, Pallas kernels, product(): pl.pallas_call(product_kernel, out_shape=jax.ShapeDtypeStruct(own.shape,...  42.8 us
    ppermute x27, starting transfers between devices, handed(): return lax.ppermute(part, 'cells', [(c, c ^ flip) for c in range(4)])  35.8 us
    pallas_call x8, Pallas kernels, share(): pl.pallas_call(share_kernel, out_shape=[part] * 4, in_specs=[pl.BlockSpec...  32.8 us
    ppermute x4, waiting for transfers between devices, per_device(): other['y', i] = lax.ppermute(own['y', i], 'genes', swap)  30.2 us
    unnamed x139, local copies, waits for them, and re-layouts  24 us
    pallas_call x3, Pallas kernels, gram(): pl.pallas_call(functools.partial(gram_kernel, starts, bool(sums), bool(ol...  22.9 us
  transfers between devices with their start and end apart: 43, of which 17 were waited for; matrix products, arithmetic and copies ran while one was open for 2% of the time, Pallas kernels for 28%

profile of v4, /device:TPU:1, one launch (start us, length us, event | category | flops | bytes accessed | tf_op | source)
XLA Modules:
  0.0 383.9 jit_solution(10765717793425723119)
XLA Ops:
  1.7 3.8 collective-permute-start
  11.3 2.3 shard_map.68
  13.7 7.6 %all-to-all-start = ((f32[16,4,32,256]{3,2,1,0:T(8,128)}), f32[16,4,32,256]{3,2,1,0:T(8,128)S(1)}, u32[]{:S(2)}, u32[]{:S(2)}) async-start(f32[16,4,32,256]{3,2,1,0:T(8,128)} %shard_map.68), calls=%async_computation | async-start | bytes 4194304 | tf_op jit(solution)/shard_map/all_to_all | solution.py:295
  21.3 3.0 collective-permute-start.1
  24.4 14.3 %collective-permute-done.2.refs_0_.other = f32[40,2048]{1,0:T(8,128)S(1)} collective-permute-done((f32[40,2048]{1,0:T(8,128)S(1)}, f32[40,2048]{1,0:T(8,128)S(1)}, u32[]{:S(2)}, u32[]{:S(2)}) %collective-permute-start.2) | collective-permute-done | bytes 327712 | tf_op jit(solution)/shard_map/ppermute | solution.py:311
  38.7 2.3 shard_map.69
  41.8 5.1 %all-to-all-done = f32[16,4,32,256]{3,2,1,0:T(8,128)S(1)} async-done(((f32[16,4,32,256]{3,2,1,0:T(8,128)}), f32[16,4,32,256]{3,2,1,0:T(8,128)S(1)}, u32[]{:S(2)}, u32[]{:S(2)}) %all-to-all-start) | async-done | bytes 2097184 | tf_op jit(solution)/shard_map/all_to_all | solution.py:295
  48.2 5.5 %all-to-all-start.1 = ((f32[16,4,48,256]{3,2,1,0:T(8,128)}), f32[16,4,48,256]{3,2,1,0:T(8,128)S(1)}, u32[]{:S(2)}, u32[]{:S(2)}) async-start(f32[16,4,48,256]{3,2,1,0:T(8,128)} %shard_map.69), calls=%async_computation.1 | async-start | bytes 6291456 | tf_op jit(solution)/shard_map/all_to_all | solution.py:295
  53.8 3.0 collective-permute-start.3
  56.8 2.1 constant_dynamic-slice_fusion
  60.1 4.0 %shard_map.70 = (f32[12,32,256]{2,1,0:T(8,128)}, f32[12,32,256]{2,1,0:T(8,128)}, f32[12,32,256]{2,1,0:T(8,128)}, f32[12,32,256]{2,1,0:T(8,128)}) custom-call(s32[49]{0:T(128)S(1)} %pad_add_fusion.pick, f32[64,32,256]{2,1,0:T(8,128)S(1)} %bitcast.35), custom_call_target="tpu_custom_call" | custom-call | bytes 3145728 | tf_op jit(solution)/shard_map/pallas_call | solution.py:109
  65.2 4.3 %collective-permute-start.5 = (f32[12,32,256]{2,1,0:T(8,128)}, f32[12,32,256]{2,1,0:T(8,128)}, u32[]{:S(2)}, u32[]{:S(2)}) collective-permute-start(f32[12,32,256]{2,1,0:T(8,128)} %get-tuple-element.96), channel_id=1, source_target_pairs={{0,32},{32,0},{64,96},{96,64},{1,33},{33,1},{65,97},{97,65},{2,34}... | collective-permute-start | bytes 1179656 | tf_op jit(solution)/shard_map/ppermute | solution.py:128
  70.4 10.6 %shard_map.71.refs_2_.own.refs_0_ = f32[32,2048]{1,0:T(8,128)} custom-call(s32[49]{0:T(128)} %copy-done.38, f32[32,2048]{1,0:T(8,128)} %copy-done.20, f32[64,32,256]{2,1,0:T(8,128)} %bitcast.29, f32[64,32,256]{2,1,0:T(8,128)} %bitcast.30, f32[64,32,256]{2,1,0:T(8,128)} %bitcast.31, f32[64,32,256]{2,1,0:T(8,128)} %bitcast.32, f32[64,32,256]{2,1,0:T(8,128)} %bitcast.33, ...), custom_call_target="tpu_custom_call" | custom-call | flops 704643072 | bytes 16777216 | tf_op jit(solution)/shard_map/pallas_call | solution.py:150
  81.1 2.1 collective-permute-start.6
  84.2 2.4 shard_map.72
  86.5 4.2 %collective-permute-done.8.refs_18_.refs_10_ = f32[160,512]{1,0:T(8,128)S(1)} collective-permute-done((f32[160,512]{1,0:T(8,128)S(1)}, f32[160,512]{1,0:T(8,128)S(1)}, u32[]{:S(2)}, u32[]{:S(2)}) %collective-permute-start.8) | collective-permute-done | bytes 327712 | tf_op jit(solution)/shard_map/ppermute | solution.py:128
  92.7 7.0 %all-to-all-start.2 = ((f32[16,4,40,256]{3,2,1,0:T(8,128)}), f32[16,4,40,256]{3,2,1,0:T(8,128)}, u32[]{:S(2)}, u32[]{:S(2)}) async-start(f32[16,4,40,256]{3,2,1,0:T(8,128)} %shard_map.72), calls=%async_computation.2 | async-start | bytes 5242880 | tf_op jit(solution)/shard_map/all_to_all | solution.py:295
  99.7 5.4 %shard_map.73 = (f32[12,48,256]{2,1,0:T(8,128)}, f32[12,48,256]{2,1,0:T(8,128)}, f32[12,48,256]{2,1,0:T(8,128)}, f32[12,48,256]{2,1,0:T(8,128)}) custom-call(s32[49]{0:T(128)S(1)} %copy-done.39, f32[64,48,256]{2,1,0:T(8,128)S(1)} %bitcast.15), custom_call_target="tpu_custom_call" | custom-call | bytes 4718592 | tf_op jit(solution)/shard_map/pallas_call | solution.py:109
  106.3 3.0 collective-permute-start.11
  109.3 10.7 %shard_map.74.refs_1_.own.refs_0_ = f32[48,2048]{1,0:T(8,128)} custom-call(s32[49]{0:T(128)} %copy-done.38, f32[48,2048]{1,0:T(8,128)} %copy-done.16, f32[64,48,256]{2,1,0:T(8,128)} %bitcast.16, f32[64,48,256]{2,1,0:T(8,128)} %bitcast.17, f32[64,48,256]{2,1,0:T(8,128)} %bitcast.18, f32[64,48,256]{2,1,0:T(8,128)} %bitcast.19, f32[64,48,256]{2,1,0:T(8,128)} %bitcast.20, ...), custom_call_target="tpu_custom_call" | custom-call | flops 1056964608 | bytes 17825792 | tf_op jit(solution)/shard_map/pallas_call | solution.py:150
  120.0 2.6 collective-permute-start.13
  123.8 2.3 shard_map.75
  126.2 6.2 %collective-permute-done.13.other = f32[48,2048]{1,0:T(8,128)S(1)} collective-permute-done((f32[48,2048]{1,0:T(8,128)}, f32[48,2048]{1,0:T(8,128)S(1)}, u32[]{:S(2)}, u32[]{:S(2)}) %collective-permute-start.13) | collective-permute-done | bytes 393248 | tf_op jit(solution)/shard_map/ppermute | solution.py:363
  133.1 7.5 %collective-permute-done.12.refs_2_ = f32[12,32,256]{2,1,0:T(8,128)} collective-permute-done((f32[12,32,256]{2,1,0:T(8,128)S(1)}, f32[12,32,256]{2,1,0:T(8,128)}, u32[]{:S(2)}, u32[]{:S(2)}) %collective-permute-start.12) | collective-permute-done | bytes 393248 | tf_op jit(solution)/shard_map/ppermute | solution.py:128
  140.6 6.9 %all-to-all-start.3 = ((f32[16,4,40,256]{3,2,1,0:T(8,128)}), f32[16,4,40,256]{3,2,1,0:T(8,128)S(1)}, u32[]{:S(2)}, u32[]{:S(2)}) async-start(f32[16,4,40,256]{3,2,1,0:T(8,128)} %shard_map.75), calls=%async_computation.3 | async-start | bytes 5242880 | tf_op jit(solution)/shard_map/all_to_all | solution.py:295
  147.6 2.0 collective-permute-start.16
  149.5 2.9 shard_map.76
  152.9 10.7 %shard_map.77.refs_1_.own.refs_0_ = f32[40,2048]{1,0:T(8,128)} custom-call(s32[49]{0:T(128)} %copy-done.38, f32[40,2048]{1,0:T(8,128)} %copy-done.18, f32[64,40,256]{2,1,0:T(8,128)} %bitcast.8.came.f0.f1.f2.f3.f4.f5, f32[64,40,256]{2,1,0:T(8,128)} %bitcast.8.came.f0.f1.f2.f3.f4.f5, f32[64,40,256]{2,1,0:T(8,128)} %bitcast.8.came.f0.f1.f2.f3.f4.f5, ...), custom_call_target="tpu_custom_call" | custom-call | flops 880803840 | bytes 17301504 | tf_op jit(solution)/shard_map/pallas_call | solution.py:150
  166.1 2.3 shard_map.78
  168.5 12.7 %collective-permute-done.17.other = f32[40,2048]{1,0:T(8,128)S(1)} collective-permute-done((f32[40,2048]{1,0:T(8,128)}, f32[40,2048]{1,0:T(8,128)S(1)}, u32[]{:S(2)}, u32[]{:S(2)}) %collective-permute-start.17) | collective-permute-done | bytes 327712 | tf_op jit(solution)/shard_map/ppermute | solution.py:363
  182.8 7.9 %all-to-all-start.4 = ((f32[16,4,48,256]{3,2,1,0:T(8,128)}), f32[16,4,48,256]{3,2,1,0:T(8,128)}, u32[]{:S(2)}, u32[]{:S(2)}) async-start(f32[16,4,48,256]{3,2,1,0:T(8,128)} %shard_map.78), calls=%async_computation.4 | async-start | bytes 6291456 | tf_op jit(solution)/shard_map/all_to_all | solution.py:295
  190.8 4.7 %shard_map.80 = (f32[12,40,256]{2,1,0:T(8,128)}, f32[12,40,256]{2,1,0:T(8,128)}, f32[12,40,256]{2,1,0:T(8,128)}, f32[12,40,256]{2,1,0:T(8,128)}) custom-call(s32[49]{0:T(128)S(1)} %copy-done.41, f32[64,40,256]{2,1,0:T(8,128)S(1)} %bitcast.22), custom_call_target="tpu_custom_call" | custom-call | bytes 3932160 | tf_op jit(solution)/shard_map/pallas_call | solution.py:109
  196.4 1.9 collective-permute-start.19
  198.7 10.7 %shard_map.79.refs_1_.own.refs_0_ = f32[40,2048]{1,0:T(8,128)} custom-call(s32[49]{0:T(128)} %copy-done.38, f32[40,2048]{1,0:T(8,128)} %get-tuple-element.92.own, f32[64,40,256]{2,1,0:T(8,128)} %bitcast.23, f32[64,40,256]{2,1,0:T(8,128)} %bitcast.24, f32[64,40,256]{2,1,0:T(8,128)} %bitcast.25, f32[64,40,256]{2,1,0:T(8,128)} %bitcast.26, ...), custom_call_target="tpu_custom_call" | custom-call | flops 880803840 | bytes 17301504 | tf_op jit(solution)/shard_map/pallas_call | solution.py:150
  209.5 1.6 collective-permute-start.21
  212.1 2.3 shard_map.81
  214.4 10.8 %collective-permute-done.21.other = f32[40,2048]{1,0:T(8,128)S(1)} collective-permute-done((f32[40,2048]{1,0:T(8,128)}, f32[40,2048]{1,0:T(8,128)S(1)}, u32[]{:S(2)}, u32[]{:S(2)}) %collective-permute-start.21) | collective-permute-done | bytes 327712 | tf_op jit(solution)/shard_map/ppermute | solution.py:363
  226.0 5.0 %all-to-all-done.4 = f32[16,4,48,256]{3,2,1,0:T(8,128)} async-done(((f32[16,4,48,256]{3,2,1,0:T(8,128)}), f32[16,4,48,256]{3,2,1,0:T(8,128)}, u32[]{:S(2)}, u32[]{:S(2)}) %all-to-all-start.4) | async-done | bytes 3145760 | tf_op jit(solution)/shard_map/all_to_all | solution.py:295
  231.0 3.7 all-to-all-start.5
  234.8 3.3 shard_map.82
  238.8 4.4 %collective-permute-start.23 = (f32[14,48,256]{2,1,0:T(8,128)}, f32[14,48,256]{2,1,0:T(8,128)}, u32[]{:S(2)}, u32[]{:S(2)}) collective-permute-start(f32[14,48,256]{2,1,0:T(8,128)} %get-tuple-element.131), channel_id=1, source_target_pairs={{0,32},{32,0},{64,96},{96,64},{1,33},{33,1},{65,97},{97,65},{2,34}... | collective-permute-start | bytes 2064392 | tf_op jit(solution)/shard_map/ppermute | solution.py:128
  244.9 2.3 shard_map.83
  247.3 19.1 %collective-permute-done.24.refs_2_ = f32[12,40,256]{2,1,0:T(8,128)S(1)} collective-permute-done((f32[12,40,256]{2,1,0:T(8,128)S(1)}, f32[12,40,256]{2,1,0:T(8,128)S(1)}, u32[]{:S(2)}, u32[]{:S(2)}) %collective-permute-start.24) | collective-permute-done | bytes 491552 | tf_op jit(solution)/shard_map/ppermute | solution.py:128
  268.0 1.5 copy-done.4
  269.5 6.6 %all-to-all-start.6 = ((f32[16,4,40,256]{3,2,1,0:T(8,128)}), f32[16,4,40,256]{3,2,1,0:T(8,128)S(1)}, u32[]{:S(2)}, u32[]{:S(2)}) async-start(f32[16,4,40,256]{3,2,1,0:T(8,128)} %shard_map.83), calls=%async_computation.6 | async-start | bytes 5242880 | tf_op jit(solution)/shard_map/all_to_all | solution.py:295
  276.1 2.8 collective-permute-start.27
  278.8 1.7 copy-done.5
  280.6 4.9 %shard_map.84 = (f32[14,40,256]{2,1,0:T(8,128)}, f32[14,40,256]{2,1,0:T(8,128)}, f32[14,40,256]{2,1,0:T(8,128)}, f32[14,40,256]{2,1,0:T(8,128)}) custom-call(s32[49]{0:T(128)S(1)} %copy-done.42, f32[64,40,256]{2,1,0:T(8,128)S(1)} %bitcast.37, f32[40,2048]{1,0:T(8,128)S(1)} %copy-done.9), custom_call_target="tpu_custom_call" | custom-call | bytes 4587520 | tf_op jit(solution)/shard_map/pallas_call | solution.py:109
  287.4 2.3 shard_map.85
  289.7 17.9 %collective-permute-done.25.refs_13_ = f32[14,40,256]{2,1,0:T(8,128)S(1)} collective-permute-done((f32[14,40,256]{2,1,0:T(8,128)}, f32[14,40,256]{2,1,0:T(8,128)S(1)}, u32[]{:S(2)}, u32[]{:S(2)}) %collective-permute-start.25) | collective-permute-done | bytes 573472 | tf_op jit(solution)/shard_map/ppermute | solution.py:128
  309.3 6.9 %all-to-all-start.7 = ((f32[16,4,32,256]{3,2,1,0:T(8,128)}), f32[16,4,32,256]{3,2,1,0:T(8,128)}, u32[]{:S(2)}, u32[]{:S(2)}) async-start(f32[16,4,32,256]{3,2,1,0:T(8,128)} %shard_map.85), calls=%async_computation.7 | async-start | bytes 4194304 | tf_op jit(solution)/shard_map/all_to_all | solution.py:295
  316.2 1.6 collective-permute-start.28
  317.9 4.9 %shard_map.88 = (f32[14,40,256]{2,1,0:T(8,128)}, f32[14,40,256]{2,1,0:T(8,128)}, f32[14,40,256]{2,1,0:T(8,128)}, f32[14,40,256]{2,1,0:T(8,128)}) custom-call(s32[49]{0:T(128)S(1)} %copy-done.42, f32[64,40,256]{2,1,0:T(8,128)S(1)} %bitcast.36, f32[40,2048]{1,0:T(8,128)S(1)} %copy-done.12), custom_call_target="tpu_custom_call" | custom-call | bytes 4587520 | tf_op jit(solution)/shard_map/pallas_call | solution.py:109
  324.7 7.1 %collective-permute-done.28.refs_14_ = f32[14,40,256]{2,1,0:T(8,128)S(1)} collective-permute-done((f32[14,40,256]{2,1,0:T(8,128)}, f32[14,40,256]{2,1,0:T(8,128)S(1)}, u32[]{:S(2)}, u32[]{:S(2)}) %collective-permute-start.28) | collective-permute-done | bytes 573472 | tf_op jit(solution)/shard_map/ppermute | solution.py:128
  332.6 8.8 %shard_map.86 = (f32[2,256,256]{2,1,0:T(8,128)}, f32[2,6,256,256]{3,2,1,0:T(8,128)}) custom-call(s32[1]{0:T(128)} %bitcast.me, f32[12,48,256]{2,1,0:T(8,128)} %get-tuple-element.100.refs_0_, f32[12,48,256]{2,1,0:T(8,128)} %collective-permute-done.10.refs_1_, f32[12,48,256]{2,1,0:T(8,128)} %collective-permute-done.16.refs_2_, ...), custom_call_target="tpu_custom_call" | custom-call | flops 3598712832 | bytes 17432576 | tf_op jit(solution)/shard_map/pallas_call | solution.py:240
  341.4 1.7 all-to-all-done.7
  344.1 2.8 shard_map.87
  346.9 2.2 collective-permute-start.29
  349.2 3.9 %collective-permute-start.30 = (f32[14,32,256]{2,1,0:T(8,128)}, f32[14,32,256]{2,1,0:T(8,128)S(1)}, u32[]{:S(2)}, u32[]{:S(2)}) collective-permute-start(f32[14,32,256]{2,1,0:T(8,128)} %get-tuple-element.159), channel_id=1, source_target_pairs={{0,96},{32,64},{64,32},{96,0},{1,97},{33,65},{65,33},{97,1},{2,98}... | collective-permute-start | bytes 1376264 | tf_op jit(solution)/shard_map/ppermute | solution.py:128
  353.1 3.2 collective-permute-done.33.refs_6_
  357.3 7.3 %shard_map.89 = (f32[2,256,256]{2,1,0:T(8,128)}, f32[2,6,256,256]{3,2,1,0:T(8,128)}) custom-call(s32[1]{0:T(128)} %bitcast.me, f32[12,40,256]{2,1,0:T(8,128)} %get-tuple-element.119.refs_0_, f32[12,40,256]{2,1,0:T(8,128)} %copy-done.50, f32[12,40,256]{2,1,0:T(8,128)} %copy-done.52, f32[12,40,256]{2,1,0:T(8,128)} %copy-done.51, ...), custom_call_target="tpu_custom_call" | custom-call | flops 1635778560 | bytes 11927552 | tf_op jit(solution)/shard_map/pallas_call | solution.py:240
  364.6 2.0 collective-permute-done.29.refs_5_
  366.6 9.3 %collective-permute-done.30.refs_6_ = f32[14,32,256]{2,1,0:T(8,128)S(1)} collective-permute-done((f32[14,32,256]{2,1,0:T(8,128)}, f32[14,32,256]{2,1,0:T(8,128)S(1)}, u32[]{:S(2)}, u32[]{:S(2)}) %collective-permute-start.30) | collective-permute-done | bytes 458784 | tf_op jit(solution)/shard_map/ppermute | solution.py:128
  376.9 6.9 %shard_map.90 = (f32[2,256,256]{2,1,0:T(8,128)}, f32[2,6,256,256]{3,2,1,0:T(8,128)}) custom-call(s32[1]{0:T(128)} %bitcast.me, f32[12,32,256]{2,1,0:T(8,128)} %get-tuple-element.91.refs_0_, f32[12,32,256]{2,1,0:T(8,128)} %copy-done.56, f32[12,32,256]{2,1,0:T(8,128)} %collective-permute-done.12.refs_2_, f32[12,32,256]{2,1,0:T(8,128)} %collective-permute-done.5.refs_3_, ...), custom_call_target="tpu_custom_call" | custom-call | flops 1308622848 | bytes 11010048 | tf_op jit(solution)/shard_map/pallas_call | solution.py:240
  (208 shorter events, 39.2 us)
Async XLA Ops:
  0.6 9.6 %copy-start.43 = (f32[160,2048]{1,0:T(8,128)S(1)}, f32[160,2048]{1,0:T(8,128)}, u32[]{:S(2)}) copy-start(f32[160,2048]{1,0:T(8,128)} %param.5) | copy-start | bytes 3932164
  1.7 11.9 %copy-start.20 = (f32[32,2048]{1,0:T(8,128)}, f32[32,2048]{1,0:T(8,128)S(1)}, u32[]{:S(2)}) copy-start(f32[32,2048]{1,0:T(8,128)S(1)} %slice.12.own) | copy-start | bytes 786436
  1.7 9.6 %collective-permute-start = (f32[32,2048]{1,0:T(8,128)S(1)}, f32[32,2048]{1,0:T(8,128)S(1)}, u32[]{:S(2)}, u32[]{:S(2)}) collective-permute-start(f32[32,2048]{1,0:T(8,128)S(1)} %slice.12.own), channel_id=1, source_target_pairs={{0,1},{1,0},{2,3},{3,2},{4,5},{5,4},{6,7},{7,6},{8,9},{9,8},{10,11... | collective-permute-start | bytes 786440 | tf_op jit(solution)/shard_map/ppermute | solution.py:305
  7.7 31.0 %copy-start.16 = (f32[48,2048]{1,0:T(8,128)}, f32[48,2048]{1,0:T(8,128)S(1)}, u32[]{:S(2)}) copy-start(f32[48,2048]{1,0:T(8,128)S(1)} %slice.13.own) | copy-start | bytes 1179652
  11.0 13.3 %copy-start.18 = (f32[40,2048]{1,0:T(8,128)}, f32[40,2048]{1,0:T(8,128)S(1)}, u32[]{:S(2)}) copy-start(f32[40,2048]{1,0:T(8,128)S(1)} %get-tuple-element.88.own) | copy-start | bytes 983044
  13.7 33.2 %all-to-all-start = ((f32[16,4,32,256]{3,2,1,0:T(8,128)}), f32[16,4,32,256]{3,2,1,0:T(8,128)S(1)}, u32[]{:S(2)}, u32[]{:S(2)}) async-start(f32[16,4,32,256]{3,2,1,0:T(8,128)} %shard_map.68), calls=%async_computation | async-start | bytes 4194304 | tf_op jit(solution)/shard_map/all_to_all | solution.py:295
  21.3 17.4 %collective-permute-start.1 = (f32[48,2048]{1,0:T(8,128)S(1)}, f32[48,2048]{1,0:T(8,128)S(1)}, u32[]{:S(2)}, u32[]{:S(2)}) collective-permute-start(f32[48,2048]{1,0:T(8,128)S(1)} %slice.13.own), channel_id=1, source_target_pairs={{0,1},{1,0},{2,3},{3,2},{4,5},{5,4},{6,7},{7,6},{8,9},{9,8},{10,11... | collective-permute-start | bytes 1179656 | tf_op jit(solution)/shard_map/ppermute | solution.py:311
  24.3 14.4 %collective-permute-start.2 = (f32[40,2048]{1,0:T(8,128)S(1)}, f32[40,2048]{1,0:T(8,128)S(1)}, u32[]{:S(2)}, u32[]{:S(2)}) collective-permute-start(f32[40,2048]{1,0:T(8,128)S(1)} %get-tuple-element.88.own), channel_id=1, source_target_pairs={{0,1},{1,0},{2,3},{3,2},{4,5},{5,4},{6,7},{7,6},{8,9},{9,8},{10,11... | collective-permute-start | bytes 983048 | tf_op jit(solution)/shard_map/ppermute | solution.py:311
  48.2 44.5 %all-to-all-start.1 = ((f32[16,4,48,256]{3,2,1,0:T(8,128)}), f32[16,4,48,256]{3,2,1,0:T(8,128)S(1)}, u32[]{:S(2)}, u32[]{:S(2)}) async-start(f32[16,4,48,256]{3,2,1,0:T(8,128)} %shard_map.69), calls=%async_computation.1 | async-start | bytes 6291456 | tf_op jit(solution)/shard_map/all_to_all | solution.py:295
  53.8 16.1 %collective-permute-start.3 = (f32[40,2048]{1,0:T(8,128)S(1)}, f32[40,2048]{1,0:T(8,128)S(1)}, u32[]{:S(2)}, u32[]{:S(2)}) collective-permute-start(f32[40,2048]{1,0:T(8,128)S(1)} %copy-done.17), channel_id=1, source_target_pairs={{0,1},{1,0},{2,3},{3,2},{4,5},{5,4},{6,7},{7,6},{8,9},{9,8},{10,11... | collective-permute-start | bytes 983048 | tf_op jit(solution)/shard_map/ppermute | solution.py:311
  58.9 22.2 %collective-permute-start.7 = (f32[160,512]{1,0:T(8,128)S(1)}, f32[160,512]{1,0:T(8,128)S(1)}, u32[]{:S(2)}, u32[]{:S(2)}) collective-permute-start(f32[160,512]{1,0:T(8,128)S(1)} %get-tuple-element.175), channel_id=1, source_target_pairs={{0,64},{32,96},{64,0},{96,32},{1,65},{33,97},{65,1},{97,33},{2,66}... | collective-permute-start | bytes 983048 | tf_op jit(solution)/shard_map/ppermute | solution.py:128
  60.1 10.4 %copy-start.38 = (s32[49]{0:T(128)}, s32[49]{0:T(128)S(1)}, u32[]{:S(2)}) copy-start(s32[49]{0:T(128)S(1)} %pad_add_fusion.pick) | copy-start | bytes 592
  64.1 27.9 %collective-permute-start.4 = (f32[12,32,256]{2,1,0:T(8,128)}, f32[12,32,256]{2,1,0:T(8,128)S(1)}, u32[]{:S(2)}, u32[]{:S(2)}) collective-permute-start(f32[12,32,256]{2,1,0:T(8,128)} %get-tuple-element.95), channel_id=1, source_target_pairs={{0,64},{32,96},{64,0},{96,32},{1,65},{33,97},{65,1},{97,33},{2,66}... | collective-permute-start | bytes 1179656 | tf_op jit(solution)/shard_map/ppermute | solution.py:128
  65.2 27.5 %collective-permute-start.5 = (f32[12,32,256]{2,1,0:T(8,128)}, f32[12,32,256]{2,1,0:T(8,128)}, u32[]{:S(2)}, u32[]{:S(2)}) collective-permute-start(f32[12,32,256]{2,1,0:T(8,128)} %get-tuple-element.96), channel_id=1, source_target_pairs={{0,32},{32,0},{64,96},{96,64},{1,33},{33,1},{65,97},{97,65},{2,34}... | collective-permute-start | bytes 1179656 | tf_op jit(solution)/shard_map/ppermute | solution.py:128
  69.6 21.2 %collective-permute-start.8 = (f32[160,512]{1,0:T(8,128)S(1)}, f32[160,512]{1,0:T(8,128)S(1)}, u32[]{:S(2)}, u32[]{:S(2)}) collective-permute-start(f32[160,512]{1,0:T(8,128)S(1)} %get-tuple-element.174), channel_id=1, source_target_pairs={{0,96},{32,64},{64,32},{96,0},{1,97},{33,65},{65,33},{97,1},{2,98}... | collective-permute-start | bytes 983048 | tf_op jit(solution)/shard_map/ppermute | solution.py:128
  69.8 13.3 %copy-start.26 = (f32[40,2048]{1,0:T(8,128)}, f32[40,2048]{1,0:T(8,128)S(1)}, u32[]{:S(2)}) copy-start(f32[40,2048]{1,0:T(8,128)S(1)} %collective-permute-done.3.refs_1_.other) | copy-start | bytes 983044
  69.8 13.3 %copy-start.19 = (f32[40,2048]{1,0:T(8,128)S(1)}, f32[40,2048]{1,0:T(8,128)}, u32[]{:S(2)}) copy-start(f32[40,2048]{1,0:T(8,128)} %copy-done.18) | copy-start | bytes 983044
  69.8 13.3 %copy-start.23 = (f32[12,32,256]{2,1,0:T(8,128)S(1)}, f32[12,32,256]{2,1,0:T(8,128)}, u32[]{:S(2)}) copy-start(f32[12,32,256]{2,1,0:T(8,128)} %get-tuple-element.91.refs_0_) | copy-start | bytes 1179652
  69.8 13.3 %copy-start.25 = (f32[40,2048]{1,0:T(8,128)S(1)}, f32[40,2048]{1,0:T(8,128)}, u32[]{:S(2)}) copy-start(f32[40,2048]{1,0:T(8,128)} %copy-done.24) | copy-start | bytes 983044
  69.9 20.9 %collective-permute-start.9 = (f32[160,512]{1,0:T(8,128)S(1)}, f32[160,512]{1,0:T(8,128)S(1)}, u32[]{:S(2)}, u32[]{:S(2)}) collective-permute-start(f32[160,512]{1,0:T(8,128)S(1)} %get-tuple-element.173), channel_id=1, source_target_pairs={{0,32},{32,0},{64,96},{96,64},{1,33},{33,1},{65,97},{97,65},{2,34}... | collective-permute-start | bytes 983048 | tf_op jit(solution)/shard_map/ppermute | solution.py:128
  81.0 10.9 %copy-start.44 = (f32[160,512]{1,0:T(8,128)}, f32[160,512]{1,0:T(8,128)S(1)}, u32[]{:S(2)}) copy-start(f32[160,512]{1,0:T(8,128)S(1)} %collective-permute-done.7.refs_17_.refs_9_) | copy-start | bytes 983044
  81.1 10.2 %collective-permute-start.6 = (f32[32,2048]{1,0:T(8,128)}, f32[32,2048]{1,0:T(8,128)S(1)}, u32[]{:S(2)}, u32[]{:S(2)}) collective-permute-start(f32[32,2048]{1,0:T(8,128)} %shard_map.71.refs_2_.own.refs_0_), channel_id=1, source_target_pairs={{0,1},{1,0},{2,3},{3,2},{4,5},{5,4},{6,7},{7,6},{8,9},{9,8},{10,11... | collective-permute-start | bytes 786440 | tf_op jit(solution)/shard_map/ppermute | solution.py:363
  92.7 47.9 %all-to-all-start.2 = ((f32[16,4,40,256]{3,2,1,0:T(8,128)}), f32[16,4,40,256]{3,2,1,0:T(8,128)}, u32[]{:S(2)}, u32[]{:S(2)}) async-start(f32[16,4,40,256]{3,2,1,0:T(8,128)} %shard_map.72), calls=%async_computation.2 | async-start | bytes 5242880 | tf_op jit(solution)/shard_map/all_to_all | solution.py:295
  105.1 35.5 %collective-permute-start.10 = (f32[12,48,256]{2,1,0:T(8,128)}, f32[12,48,256]{2,1,0:T(8,128)}, u32[]{:S(2)}, u32[]{:S(2)}) collective-permute-start(f32[12,48,256]{2,1,0:T(8,128)} %get-tuple-element.103), channel_id=1, source_target_pairs={{0,64},{32,96},{64,0},{96,32},{1,65},{33,97},{65,1},{97,33},{2,66}... | collective-permute-start | bytes 1769480 | tf_op jit(solution)/shard_map/ppermute | solution.py:128
  106.3 16.4 %copy-start.68 = (f32[12,32,256]{2,1,0:T(8,128)S(1)}, f32[12,32,256]{2,1,0:T(8,128)}, u32[]{:S(2)}) copy-start(f32[12,32,256]{2,1,0:T(8,128)} %get-tuple-element.105) | copy-start | bytes 1179652
  106.3 16.6 %copy-start.27 = (f32[40,2048]{1,0:T(8,128)S(1)}, f32[40,2048]{1,0:T(8,128)}, u32[]{:S(2)}) copy-start(f32[40,2048]{1,0:T(8,128)} %copy-done.26) | copy-start | bytes 983044
  106.3 16.6 %copy-start.29 = (f32[12,48,256]{2,1,0:T(8,128)S(1)}, f32[12,48,256]{2,1,0:T(8,128)}, u32[]{:S(2)}) copy-start(f32[12,48,256]{2,1,0:T(8,128)} %get-tuple-element.100.refs_0_) | copy-start | bytes 1769476
  106.3 34.3 %collective-permute-start.11 = (f32[12,48,256]{2,1,0:T(8,128)}, f32[12,48,256]{2,1,0:T(8,128)}, u32[]{:S(2)}, u32[]{:S(2)}) collective-permute-start(f32[12,48,256]{2,1,0:T(8,128)} %get-tuple-element.104), channel_id=1, source_target_pairs={{0,32},{32,0},{64,96},{96,64},{1,33},{33,1},{65,97},{97,65},{2,34}... | collective-permute-start | bytes 1769480 | tf_op jit(solution)/shard_map/ppermute | solution.py:128
  120.0 12.4 %collective-permute-start.13 = (f32[48,2048]{1,0:T(8,128)}, f32[48,2048]{1,0:T(8,128)S(1)}, u32[]{:S(2)}, u32[]{:S(2)}) collective-permute-start(f32[48,2048]{1,0:T(8,128)} %shard_map.74.refs_1_.own.refs_0_), channel_id=1, source_target_pairs={{0,1},{1,0},{2,3},{3,2},{4,5},{5,4},{6,7},{7,6},{8,9},{9,8},{10,11... | collective-permute-start | bytes 1179656 | tf_op jit(solution)/shard_map/ppermute | solution.py:363
  122.6 18.0 %collective-permute-start.12 = (f32[12,32,256]{2,1,0:T(8,128)S(1)}, f32[12,32,256]{2,1,0:T(8,128)}, u32[]{:S(2)}, u32[]{:S(2)}) collective-permute-start(f32[12,32,256]{2,1,0:T(8,128)S(1)} %copy-done.68), channel_id=1, source_target_pairs={{0,96},{32,64},{64,32},{96,0},{1,97},{33,65},{65,33},{97,1},{2,98}... | collective-permute-start | bytes 1179656 | tf_op jit(solution)/shard_map/ppermute | solution.py:128
  140.6 42.1 %all-to-all-start.3 = ((f32[16,4,40,256]{3,2,1,0:T(8,128)}), f32[16,4,40,256]{3,2,1,0:T(8,128)S(1)}, u32[]{:S(2)}, u32[]{:S(2)}) async-start(f32[16,4,40,256]{3,2,1,0:T(8,128)} %shard_map.75), calls=%async_computation.3 | async-start | bytes 5242880 | tf_op jit(solution)/shard_map/all_to_all | solution.py:295
  147.6 35.2 %collective-permute-start.16 = (f32[12,48,256]{2,1,0:T(8,128)}, f32[12,48,256]{2,1,0:T(8,128)}, u32[]{:S(2)}, u32[]{:S(2)}) collective-permute-start(f32[12,48,256]{2,1,0:T(8,128)} %get-tuple-element.116), channel_id=1, source_target_pairs={{0,96},{32,64},{64,32},{96,0},{1,97},{33,65},{65,33},{97,1},{2,98}... | collective-permute-start | bytes 1769480 | tf_op jit(solution)/shard_map/ppermute | solution.py:128
  152.4 28.7 %collective-permute-start.14 = (f32[12,40,256]{2,1,0:T(8,128)}, f32[12,40,256]{2,1,0:T(8,128)S(1)}, u32[]{:S(2)}, u32[]{:S(2)}) collective-permute-start(f32[12,40,256]{2,1,0:T(8,128)} %get-tuple-element.114), channel_id=1, source_target_pairs={{0,64},{32,96},{64,0},{96,32},{1,65},{33,97},{65,1},{97,33},{2,66}... | collective-permute-start | bytes 1474568 | tf_op jit(solution)/shard_map/ppermute | solution.py:128
  152.5 12.6 %copy-start.7 = (f32[48,2048]{1,0:T(8,128)S(1)}, f32[48,2048]{1,0:T(8,128)}, u32[]{:S(2)}) copy-start(f32[48,2048]{1,0:T(8,128)} %shard_map.74.refs_1_.own.refs_0_) | copy-start | bytes 1179652
  152.5 12.6 %copy-start.31 = (f32[12,40,256]{2,1,0:T(8,128)S(1)}, f32[12,40,256]{2,1,0:T(8,128)}, u32[]{:S(2)}) copy-start(f32[12,40,256]{2,1,0:T(8,128)} %get-tuple-element.111.refs_0_.refs_4_) | copy-start | bytes 1474564
  152.5 12.6 %copy-start.33 = (f32[48,2048]{1,0:T(8,128)S(1)}, f32[48,2048]{1,0:T(8,128)}, u32[]{:S(2)}) copy-start(f32[48,2048]{1,0:T(8,128)} %copy-done.32) | copy-start | bytes 1179652
  152.6 28.6 %collective-permute-start.15 = (f32[12,40,256]{2,1,0:T(8,128)}, f32[12,40,256]{2,1,0:T(8,128)S(1)}, u32[]{:S(2)}, u32[]{:S(2)}) collective-permute-start(f32[12,40,256]{2,1,0:T(8,128)} %get-tuple-element.115), channel_id=1, source_target_pairs={{0,32},{32,0},{64,96},{96,64},{1,33},{33,1},{65,97},{97,65},{2,34}... | collective-permute-start | bytes 1474568 | tf_op jit(solution)/shard_map/ppermute | solution.py:128
  163.7 17.5 %collective-permute-start.17 = (f32[40,2048]{1,0:T(8,128)}, f32[40,2048]{1,0:T(8,128)S(1)}, u32[]{:S(2)}, u32[]{:S(2)}) collective-permute-start(f32[40,2048]{1,0:T(8,128)} %shard_map.77.refs_1_.own.refs_0_), channel_id=1, source_target_pairs={{0,1},{1,0},{2,3},{3,2},{4,5},{5,4},{6,7},{7,6},{8,9},{9,8},{10,11... | collective-permute-start | bytes 983048 | tf_op jit(solution)/shard_map/ppermute | solution.py:363
  182.8 48.2 %all-to-all-start.4 = ((f32[16,4,48,256]{3,2,1,0:T(8,128)}), f32[16,4,48,256]{3,2,1,0:T(8,128)}, u32[]{:S(2)}, u32[]{:S(2)}) async-start(f32[16,4,48,256]{3,2,1,0:T(8,128)} %shard_map.78), calls=%async_computation.4 | async-start | bytes 6291456 | tf_op jit(solution)/shard_map/all_to_all | solution.py:295
  195.5 30.5 %collective-permute-start.18 = (f32[12,40,256]{2,1,0:T(8,128)}, f32[12,40,256]{2,1,0:T(8,128)S(1)}, u32[]{:S(2)}, u32[]{:S(2)}) collective-permute-start(f32[12,40,256]{2,1,0:T(8,128)} %get-tuple-element.122), channel_id=1, source_target_pairs={{0,64},{32,96},{64,0},{96,32},{1,65},{33,97},{65,1},{97,33},{2,66}... | collective-permute-start | bytes 1474568 | tf_op jit(solution)/shard_map/ppermute | solution.py:128
  196.4 14.6 %copy-start.9 = (f32[40,2048]{1,0:T(8,128)S(1)}, f32[40,2048]{1,0:T(8,128)}, u32[]{:S(2)}) copy-start(f32[40,2048]{1,0:T(8,128)} %shard_map.77.refs_1_.own.refs_0_) | copy-start | bytes 983044
  196.4 14.7 %copy-start.22 = (f32[12,40,256]{2,1,0:T(8,128)S(1)}, f32[12,40,256]{2,1,0:T(8,128)}, u32[]{:S(2)}) copy-start(f32[12,40,256]{2,1,0:T(8,128)} %get-tuple-element.119.refs_0_) | copy-start | bytes 1474564
  196.4 29.5 %collective-permute-start.19 = (f32[12,40,256]{2,1,0:T(8,128)}, f32[12,40,256]{2,1,0:T(8,128)S(1)}, u32[]{:S(2)}, u32[]{:S(2)}) collective-permute-start(f32[12,40,256]{2,1,0:T(8,128)} %get-tuple-element.123), channel_id=1, source_target_pairs={{0,32},{32,0},{64,96},{96,64},{1,33},{33,1},{65,97},{97,65},{2,34}... | collective-permute-start | bytes 1474568 | tf_op jit(solution)/shard_map/ppermute | solution.py:128
  198.3 27.6 %collective-permute-start.20 = (f32[12,40,256]{2,1,0:T(8,128)S(1)}, f32[12,40,256]{2,1,0:T(8,128)S(1)}, u32[]{:S(2)}, u32[]{:S(2)}) collective-permute-start(f32[12,40,256]{2,1,0:T(8,128)S(1)} %copy-done.66), channel_id=1, source_target_pairs={{0,96},{32,64},{64,32},{96,0},{1,97},{33,65},{65,33},{97,1},{2,98}... | collective-permute-start | bytes 1474568 | tf_op jit(solution)/shard_map/ppermute | solution.py:128
  209.5 15.7 %collective-permute-start.21 = (f32[40,2048]{1,0:T(8,128)}, f32[40,2048]{1,0:T(8,128)S(1)}, u32[]{:S(2)}, u32[]{:S(2)}) collective-permute-start(f32[40,2048]{1,0:T(8,128)} %shard_map.79.refs_1_.own.refs_0_), channel_id=1, source_target_pairs={{0,1},{1,0},{2,3},{3,2},{4,5},{5,4},{6,7},{7,6},{8,9},{9,8},{10,11... | collective-permute-start | bytes 983048 | tf_op jit(solution)/shard_map/ppermute | solution.py:363
  231.0 37.0 %all-to-all-start.5 = ((f32[16,4,40,256]{3,2,1,0:T(8,128)}), f32[16,4,40,256]{3,2,1,0:T(8,128)S(1)}, u32[]{:S(2)}, u32[]{:S(2)}) async-start(f32[16,4,40,256]{3,2,1,0:T(8,128)} %shard_map.81), calls=%async_computation.5 | async-start | bytes 5242880 | tf_op jit(solution)/shard_map/all_to_all | solution.py:295
  238.1 28.3 %collective-permute-start.22 = (f32[14,48,256]{2,1,0:T(8,128)}, f32[14,48,256]{2,1,0:T(8,128)S(1)}, u32[]{:S(2)}, u32[]{:S(2)}) collective-permute-start(f32[14,48,256]{2,1,0:T(8,128)} %get-tuple-element.130), channel_id=1, source_target_pairs={{0,64},{32,96},{64,0},{96,32},{1,65},{33,97},{65,1},{97,33},{2,66}... | collective-permute-start | bytes 2064392 | tf_op jit(solution)/shard_map/ppermute | solution.py:128
  238.8 29.2 %collective-permute-start.23 = (f32[14,48,256]{2,1,0:T(8,128)}, f32[14,48,256]{2,1,0:T(8,128)}, u32[]{:S(2)}, u32[]{:S(2)}) collective-permute-start(f32[14,48,256]{2,1,0:T(8,128)} %get-tuple-element.131), channel_id=1, source_target_pairs={{0,32},{32,0},{64,96},{96,64},{1,33},{33,1},{65,97},{97,65},{2,34}... | collective-permute-start | bytes 2064392 | tf_op jit(solution)/shard_map/ppermute | solution.py:128
  243.2 23.1 %collective-permute-start.24 = (f32[12,40,256]{2,1,0:T(8,128)S(1)}, f32[12,40,256]{2,1,0:T(8,128)S(1)}, u32[]{:S(2)}, u32[]{:S(2)}) collective-permute-start(f32[12,40,256]{2,1,0:T(8,128)S(1)} %copy-done.67), channel_id=1, source_target_pairs={{0,96},{32,64},{64,32},{96,0},{1,97},{33,65},{65,33},{97,1},{2,98}... | collective-permute-start | bytes 1474568 | tf_op jit(solution)/shard_map/ppermute | solution.py:128
  269.5 39.8 %all-to-all-start.6 = ((f32[16,4,40,256]{3,2,1,0:T(8,128)}), f32[16,4,40,256]{3,2,1,0:T(8,128)S(1)}, u32[]{:S(2)}, u32[]{:S(2)}) async-start(f32[16,4,40,256]{3,2,1,0:T(8,128)} %shard_map.83), calls=%async_computation.6 | async-start | bytes 5242880 | tf_op jit(solution)/shard_map/all_to_all | solution.py:295
  276.1 33.2 %collective-permute-start.27 = (f32[14,48,256]{2,1,0:T(8,128)}, f32[14,48,256]{2,1,0:T(8,128)}, u32[]{:S(2)}, u32[]{:S(2)}) collective-permute-start(f32[14,48,256]{2,1,0:T(8,128)} %get-tuple-element.139), channel_id=1, source_target_pairs={{0,96},{32,64},{64,32},{96,0},{1,97},{33,65},{65,33},{97,1},{2,98}... | collective-permute-start | bytes 2064392 | tf_op jit(solution)/shard_map/ppermute | solution.py:128
  285.5 22.1 %collective-permute-start.25 = (f32[14,40,256]{2,1,0:T(8,128)}, f32[14,40,256]{2,1,0:T(8,128)S(1)}, u32[]{:S(2)}, u32[]{:S(2)}) collective-permute-start(f32[14,40,256]{2,1,0:T(8,128)} %get-tuple-element.137), channel_id=1, source_target_pairs={{0,64},{32,96},{64,0},{96,32},{1,65},{33,97},{65,1},{97,33},{2,66}... | collective-permute-start | bytes 1720328 | tf_op jit(solution)/shard_map/ppermute | solution.py:128
  286.3 21.3 %collective-permute-start.26 = (f32[14,40,256]{2,1,0:T(8,128)}, f32[14,40,256]{2,1,0:T(8,128)S(1)}, u32[]{:S(2)}, u32[]{:S(2)}) collective-permute-start(f32[14,40,256]{2,1,0:T(8,128)} %get-tuple-element.138), channel_id=1, source_target_pairs={{0,32},{32,0},{64,96},{96,64},{1,33},{33,1},{65,97},{97,65},{2,34}... | collective-permute-start | bytes 1720328 | tf_op jit(solution)/shard_map/ppermute | solution.py:128
  289.7 28.1 %copy-start.12 = (f32[40,2048]{1,0:T(8,128)S(1)}, f32[40,2048]{1,0:T(8,128)}, u32[]{:S(2)}) copy-start(f32[40,2048]{1,0:T(8,128)} %shard_map.79.refs_1_.own.refs_0_) | copy-start | bytes 983044
  309.3 33.8 %all-to-all-start.7 = ((f32[16,4,32,256]{3,2,1,0:T(8,128)}), f32[16,4,32,256]{3,2,1,0:T(8,128)}, u32[]{:S(2)}, u32[]{:S(2)}) async-start(f32[16,4,32,256]{3,2,1,0:T(8,128)} %shard_map.85), calls=%async_computation.7 | async-start | bytes 4194304 | tf_op jit(solution)/shard_map/all_to_all | solution.py:295
  316.2 15.6 %collective-permute-start.28 = (f32[14,40,256]{2,1,0:T(8,128)}, f32[14,40,256]{2,1,0:T(8,128)S(1)}, u32[]{:S(2)}, u32[]{:S(2)}) collective-permute-start(f32[14,40,256]{2,1,0:T(8,128)} %get-tuple-element.151), channel_id=1, source_target_pairs={{0,96},{32,64},{64,32},{96,0},{1,97},{33,65},{65,33},{97,1},{2,98}... | collective-permute-start | bytes 1720328 | tf_op jit(solution)/shard_map/ppermute | solution.py:128
  322.8 30.3 %collective-permute-start.32 = (f32[14,40,256]{2,1,0:T(8,128)}, f32[14,40,256]{2,1,0:T(8,128)S(1)}, u32[]{:S(2)}, u32[]{:S(2)}) collective-permute-start(f32[14,40,256]{2,1,0:T(8,128)} %get-tuple-element.166), channel_id=1, source_target_pairs={{0,64},{32,96},{64,0},{96,32},{1,65},{33,97},{65,1},{97,33},{2,66}... | collective-permute-start | bytes 1720328 | tf_op jit(solution)/shard_map/ppermute | solution.py:128
  323.8 32.4 %collective-permute-start.33 = (f32[14,40,256]{2,1,0:T(8,128)}, f32[14,40,256]{2,1,0:T(8,128)S(1)}, u32[]{:S(2)}, u32[]{:S(2)}) collective-permute-start(f32[14,40,256]{2,1,0:T(8,128)} %get-tuple-element.167), channel_id=1, source_target_pairs={{0,96},{32,64},{64,32},{96,0},{1,97},{33,65},{65,33},{97,1},{2,98}... | collective-permute-start | bytes 1720328 | tf_op jit(solution)/shard_map/ppermute | solution.py:128
  324.1 32.1 %collective-permute-start.34 = (f32[14,40,256]{2,1,0:T(8,128)}, f32[14,40,256]{2,1,0:T(8,128)S(1)}, u32[]{:S(2)}, u32[]{:S(2)}) collective-permute-start(f32[14,40,256]{2,1,0:T(8,128)} %get-tuple-element.168), channel_id=1, source_target_pairs={{0,32},{32,0},{64,96},{96,64},{1,33},{33,1},{65,97},{97,65},{2,34}... | collective-permute-start | bytes 1720328 | tf_op jit(solution)/shard_map/ppermute | solution.py:128
  332.6 10.4 %copy-start.15 = (f32[32,2048]{1,0:T(8,128)S(1)}, f32[32,2048]{1,0:T(8,128)}, u32[]{:S(2)}) copy-start(f32[32,2048]{1,0:T(8,128)} %shard_map.71.refs_2_.own.refs_0_) | copy-start | bytes 786436
  346.9 19.7 %collective-permute-start.29 = (f32[14,32,256]{2,1,0:T(8,128)}, f32[14,32,256]{2,1,0:T(8,128)S(1)}, u32[]{:S(2)}, u32[]{:S(2)}) collective-permute-start(f32[14,32,256]{2,1,0:T(8,128)} %get-tuple-element.158), channel_id=1, source_target_pairs={{0,64},{32,96},{64,0},{96,32},{1,65},{33,97},{65,1},{97,33},{2,66}... | collective-permute-start | bytes 1376264 | tf_op jit(solution)/shard_map/ppermute | solution.py:128
  349.2 26.8 %collective-permute-start.30 = (f32[14,32,256]{2,1,0:T(8,128)}, f32[14,32,256]{2,1,0:T(8,128)S(1)}, u32[]{:S(2)}, u32[]{:S(2)}) collective-permute-start(f32[14,32,256]{2,1,0:T(8,128)} %get-tuple-element.159), channel_id=1, source_target_pairs={{0,96},{32,64},{64,32},{96,0},{1,97},{33,65},{65,33},{97,1},{2,98}... | collective-permute-start | bytes 1376264 | tf_op jit(solution)/shard_map/ppermute | solution.py:128
  353.1 22.9 %collective-permute-start.31 = (f32[14,32,256]{2,1,0:T(8,128)}, f32[14,32,256]{2,1,0:T(8,128)S(1)}, u32[]{:S(2)}, u32[]{:S(2)}) collective-permute-start(f32[14,32,256]{2,1,0:T(8,128)} %get-tuple-element.160), channel_id=1, source_target_pairs={{0,32},{32,0},{64,96},{96,64},{1,33},{33,1},{65,97},{97,65},{2,34}... | collective-permute-start | bytes 1376264 | tf_op jit(solution)/shard_map/ppermute | solution.py:128
  366.6 9.4 %copy-start.53 = (f32[14,32,256]{2,1,0:T(8,128)}, f32[14,32,256]{2,1,0:T(8,128)S(1)}, u32[]{:S(2)}) copy-start(f32[14,32,256]{2,1,0:T(8,128)S(1)} %collective-permute-done.29.refs_5_) | copy-start | bytes 1376260
  (48 other events, 156.7 us)

commit v5 on v4

--- a/solution.py
+++ b/solution.py
@@ -13,7 +13,7 @@
 LATE = 2
 ORDER = (3, 0, 1, 2)
 HOME = 1
-EARLY = 1
+EARLY = 0
 SWAPPED = (0, 0, 0, 0)
 FLIPS = (0, 2, 3, 1)
 STEP = 0.5

time: 391 us -> 402 us (1.028)
  starting transfers between devices: 106 us -> 118 us
    ppermute x27, starting transfers between devices: 35.8 us -> 44.9 us  [handed(): return lax.ppermute(part, 'cells', [(c, c ^ flip) for c in range(4)])]
    all_to_all x8, waiting for transfers between devices: 11.8 us -> 19.1 us  [exchange(): came = lax.all_to_all(sent, 'genes', 0, 0, axis_index_groups=planes)]
    ppermute x3, waiting for transfers between devices: 14.3 us -> 7.38 us  [per_device(): other['x', i] = lax.ppermute(piece, 'genes', swap)]
    unnamed x139 -> x133, local copies, waits for them, and re-layouts: 24 us -> 24.2 us
  transfers between devices with their start and end apart: 43 -> 43, of which waited for: 17 -> 16; matrix products, arithmetic and copies ran while one was open for 2% -> 2% of each run, Pallas kernels for 28% -> 27%
where the time goes in v5:
time: 402 us; the launch traced here: 398 us
  waiting for transfers between devices  130 us (32%)
  starting transfers between devices  118 us (29%)
  Pallas kernels  117 us (29%)
  local copies, waits for them, and re-layouts  29.9 us (7%)
    ppermute x27, waiting for transfers between devices, handed(): return lax.ppermute(part, 'cells', [(c, c ^ flip) for c in range(4)])  72.4 us
    all_to_all x8, starting transfers between devices, exchange(): came = lax.all_to_all(sent, 'genes', 0, 0, axis_index_groups=planes)  53.8 us
    ppermute x27, starting transfers between devices, handed(): return lax.ppermute(part, 'cells', [(c, c ^ flip) for c in range(4)])  44.9 us
    pallas_call x4, Pallas kernels, product(): pl.pallas_call(product_kernel, out_shape=jax.ShapeDtypeStruct(own.shape,...  42.8 us
    pallas_call x8, Pallas kernels, share(): pl.pallas_call(share_kernel, out_shape=[part] * 4, in_specs=[pl.BlockSpec...  32.8 us
    ppermute x4, waiting for transfers between devices, per_device(): other['y', i] = lax.ppermute(own['y', i], 'genes', swap)  30.9 us
    unnamed x133, local copies, waits for them, and re-layouts  24.2 us
    pallas_call x3, Pallas kernels, gram(): pl.pallas_call(functools.partial(gram_kernel, starts, bool(sums), bool(ol...  22.9 us
  transfers between devices with their start and end apart: 43, of which 16 were waited for; matrix products, arithmetic and copies ran while one was open for 2% of the time, Pallas kernels for 27%

profile of v5, /device:TPU:1, one launch (start us, length us, event | category | flops | bytes accessed | tf_op | source)
XLA Modules:
  0.0 398.4 jit_solution(8709171830013605013)
XLA Ops:
  1.7 3.8 collective-permute-start
  11.3 2.3 shard_map.68
  13.6 7.6 %all-to-all-start = ((f32[16,4,32,256]{3,2,1,0:T(8,128)}), f32[16,4,32,256]{3,2,1,0:T(8,128)S(1)}, u32[]{:S(2)}, u32[]{:S(2)}) async-start(f32[16,4,32,256]{3,2,1,0:T(8,128)} %shard_map.68), calls=%async_computation | async-start | bytes 4194304 | tf_op jit(solution)/shard_map/all_to_all | solution.py:295
  21.3 3.0 collective-permute-start.1
  24.3 7.4 %collective-permute-done.1.other = f32[48,2048]{1,0:T(8,128)S(1)} collective-permute-done((f32[48,2048]{1,0:T(8,128)S(1)}, f32[48,2048]{1,0:T(8,128)S(1)}, u32[]{:S(2)}, u32[]{:S(2)}) %collective-permute-start.1) | collective-permute-done | bytes 393248 | tf_op jit(solution)/shard_map/ppermute | solution.py:311
  31.6 2.3 shard_map.69
  34.0 12.9 %all-to-all-done = f32[16,4,32,256]{3,2,1,0:T(8,128)S(1)} async-done(((f32[16,4,32,256]{3,2,1,0:T(8,128)}), f32[16,4,32,256]{3,2,1,0:T(8,128)S(1)}, u32[]{:S(2)}, u32[]{:S(2)}) %all-to-all-start) | async-done | bytes 2097184 | tf_op jit(solution)/shard_map/all_to_all | solution.py:295
  48.2 5.5 %all-to-all-start.1 = ((f32[16,4,48,256]{3,2,1,0:T(8,128)}), f32[16,4,48,256]{3,2,1,0:T(8,128)S(1)}, u32[]{:S(2)}, u32[]{:S(2)}) async-start(f32[16,4,48,256]{3,2,1,0:T(8,128)} %shard_map.69), calls=%async_computation.1 | async-start | bytes 6291456 | tf_op jit(solution)/shard_map/all_to_all | solution.py:295
  53.7 3.0 collective-permute-start.2
  56.8 2.1 constant_dynamic-slice_fusion
  60.3 4.0 %shard_map.70 = (f32[12,32,256]{2,1,0:T(8,128)}, f32[12,32,256]{2,1,0:T(8,128)}, f32[12,32,256]{2,1,0:T(8,128)}, f32[12,32,256]{2,1,0:T(8,128)}) custom-call(s32[49]{0:T(128)S(1)} %pad_add_fusion.pick, f32[64,32,256]{2,1,0:T(8,128)S(1)} %bitcast.35), custom_call_target="tpu_custom_call" | custom-call | bytes 3145728 | tf_op jit(solution)/shard_map/pallas_call | solution.py:109
  64.6 4.6 %collective-permute-start.5 = (f32[12,32,256]{2,1,0:T(8,128)}, f32[12,32,256]{2,1,0:T(8,128)}, u32[]{:S(2)}, u32[]{:S(2)}) collective-permute-start(f32[12,32,256]{2,1,0:T(8,128)} %get-tuple-element.96), channel_id=1, source_target_pairs={{0,32},{32,0},{64,96},{96,64},{1,33},{33,1},{65,97},{97,65},{2,34}... | collective-permute-start | bytes 1179656 | tf_op jit(solution)/shard_map/ppermute | solution.py:128
  69.2 1.7 collective-permute-start.8
  70.9 5.8 %collective-permute-start.9 = (f32[160,512]{1,0:T(8,128)S(1)}, f32[160,512]{1,0:T(8,128)S(1)}, u32[]{:S(2)}, u32[]{:S(2)}) collective-permute-start(f32[160,512]{1,0:T(8,128)S(1)} %get-tuple-element.173), channel_id=1, source_target_pairs={{0,32},{32,0},{64,96},{96,64},{1,33},{33,1},{65,97},{97,65},{2,34}... | collective-permute-start | bytes 983048 | tf_op jit(solution)/shard_map/ppermute | solution.py:128
  76.7 10.6 %shard_map.71.refs_3_.own.refs_0_ = f32[32,2048]{1,0:T(8,128)} custom-call(s32[49]{0:T(128)} %copy-done.37, f32[32,2048]{1,0:T(8,128)} %copy-done.19, f32[64,32,256]{2,1,0:T(8,128)} %bitcast.29, f32[64,32,256]{2,1,0:T(8,128)} %bitcast.30, f32[64,32,256]{2,1,0:T(8,128)} %bitcast.31, f32[64,32,256]{2,1,0:T(8,128)} %bitcast.32, f32[64,32,256]{2,1,0:T(8,128)} %bitcast.33, ...), custom_call_target="tpu_custom_call" | custom-call | flops 704643072 | bytes 16777216 | tf_op jit(solution)/shard_map/pallas_call | solution.py:150
  87.3 3.0 collective-permute-start.6
  91.3 2.3 shard_map.72
  93.6 4.3 %collective-permute-done.8.refs_18_.refs_10_ = f32[160,512]{1,0:T(8,128)S(1)} collective-permute-done((f32[160,512]{1,0:T(8,128)S(1)}, f32[160,512]{1,0:T(8,128)S(1)}, u32[]{:S(2)}, u32[]{:S(2)}) %collective-permute-start.8) | collective-permute-done | bytes 327712 | tf_op jit(solution)/shard_map/ppermute | solution.py:128
  99.6 6.5 %all-to-all-start.2 = ((f32[16,4,40,256]{3,2,1,0:T(8,128)}), f32[16,4,40,256]{3,2,1,0:T(8,128)}, u32[]{:S(2)}, u32[]{:S(2)}) async-start(f32[16,4,40,256]{3,2,1,0:T(8,128)} %shard_map.72), calls=%async_computation.2 | async-start | bytes 5242880 | tf_op jit(solution)/shard_map/all_to_all | solution.py:295
  106.2 5.4 %shard_map.73 = (f32[12,48,256]{2,1,0:T(8,128)}, f32[12,48,256]{2,1,0:T(8,128)}, f32[12,48,256]{2,1,0:T(8,128)}, f32[12,48,256]{2,1,0:T(8,128)}) custom-call(s32[49]{0:T(128)S(1)} %copy-done.38, f32[64,48,256]{2,1,0:T(8,128)S(1)} %bitcast.15), custom_call_target="tpu_custom_call" | custom-call | bytes 4718592 | tf_op jit(solution)/shard_map/pallas_call | solution.py:109
  112.7 3.6 collective-permute-start.11
  116.3 10.7 %shard_map.74.refs_1_.own.refs_0_ = f32[48,2048]{1,0:T(8,128)} custom-call(s32[49]{0:T(128)} %copy-done.37, f32[48,2048]{1,0:T(8,128)} %copy-done.16, f32[64,48,256]{2,1,0:T(8,128)} %bitcast.16, f32[64,48,256]{2,1,0:T(8,128)} %bitcast.17, f32[64,48,256]{2,1,0:T(8,128)} %bitcast.18, f32[64,48,256]{2,1,0:T(8,128)} %bitcast.19, f32[64,48,256]{2,1,0:T(8,128)} %bitcast.20, ...), custom_call_target="tpu_custom_call" | custom-call | flops 1056964608 | bytes 17825792 | tf_op jit(solution)/shard_map/pallas_call | solution.py:150
  127.0 2.6 collective-permute-start.13
  130.9 2.3 shard_map.75
  133.2 6.2 %collective-permute-done.13.other = f32[48,2048]{1,0:T(8,128)S(1)} collective-permute-done((f32[48,2048]{1,0:T(8,128)}, f32[48,2048]{1,0:T(8,128)S(1)}, u32[]{:S(2)}, u32[]{:S(2)}) %collective-permute-start.13) | collective-permute-done | bytes 393248 | tf_op jit(solution)/shard_map/ppermute | solution.py:363
  140.2 7.5 %collective-permute-done.12.refs_2_ = f32[12,32,256]{2,1,0:T(8,128)} collective-permute-done((f32[12,32,256]{2,1,0:T(8,128)S(1)}, f32[12,32,256]{2,1,0:T(8,128)}, u32[]{:S(2)}, u32[]{:S(2)}) %collective-permute-start.12) | collective-permute-done | bytes 393248 | tf_op jit(solution)/shard_map/ppermute | solution.py:128
  147.7 6.9 %all-to-all-start.3 = ((f32[16,4,40,256]{3,2,1,0:T(8,128)}), f32[16,4,40,256]{3,2,1,0:T(8,128)S(1)}, u32[]{:S(2)}, u32[]{:S(2)}) async-start(f32[16,4,40,256]{3,2,1,0:T(8,128)} %shard_map.75), calls=%async_computation.3 | async-start | bytes 5242880 | tf_op jit(solution)/shard_map/all_to_all | solution.py:295
  154.6 2.0 collective-permute-start.16
  156.6 2.9 shard_map.76
  160.0 10.8 %shard_map.77.refs_1_.own.refs_0_ = f32[40,2048]{1,0:T(8,128)} custom-call(s32[49]{0:T(128)} %copy-done.37, f32[40,2048]{1,0:T(8,128)} %get-tuple-element.91.own, f32[64,40,256]{2,1,0:T(8,128)} %bitcast.8.came.f0.f1.f2.f3.f4.f5, f32[64,40,256]{2,1,0:T(8,128)} %bitcast.8.came.f0.f1.f2.f3.f4.f5, f32[64,40,256]{2,1,0:T(8,128)} %bitcast.8.came.f0.f1.f2.f3.f4.f5, ...), custom_call_target="tpu_custom_call" | custom-call | flops 880803840 | bytes 17301504 | tf_op jit(solution)/shard_map/pallas_call | solution.py:150
  172.9 2.3 shard_map.78
  175.2 13.0 %collective-permute-done.17.other = f32[40,2048]{1,0:T(8,128)S(1)} collective-permute-done((f32[40,2048]{1,0:T(8,128)}, f32[40,2048]{1,0:T(8,128)S(1)}, u32[]{:S(2)}, u32[]{:S(2)}) %collective-permute-start.17) | collective-permute-done | bytes 327712 | tf_op jit(solution)/shard_map/ppermute | solution.py:363
  190.6 7.2 %all-to-all-start.4 = ((f32[16,4,48,256]{3,2,1,0:T(8,128)}), f32[16,4,48,256]{3,2,1,0:T(8,128)}, u32[]{:S(2)}, u32[]{:S(2)}) async-start(f32[16,4,48,256]{3,2,1,0:T(8,128)} %shard_map.78), calls=%async_computation.4 | async-start | bytes 6291456 | tf_op jit(solution)/shard_map/all_to_all | solution.py:295
  197.8 4.7 %shard_map.80 = (f32[12,40,256]{2,1,0:T(8,128)}, f32[12,40,256]{2,1,0:T(8,128)}, f32[12,40,256]{2,1,0:T(8,128)}, f32[12,40,256]{2,1,0:T(8,128)}) custom-call(s32[49]{0:T(128)S(1)} %copy-done.40, f32[64,40,256]{2,1,0:T(8,128)S(1)} %bitcast.22), custom_call_target="tpu_custom_call" | custom-call | bytes 3932160 | tf_op jit(solution)/shard_map/pallas_call | solution.py:109
  203.5 1.9 collective-permute-start.19
  205.4 10.7 %shard_map.79.refs_1_.own.refs_0_ = f32[40,2048]{1,0:T(8,128)} custom-call(s32[49]{0:T(128)} %copy-done.37, f32[40,2048]{1,0:T(8,128)} %get-tuple-element.92.own, f32[64,40,256]{2,1,0:T(8,128)} %bitcast.23, f32[64,40,256]{2,1,0:T(8,128)} %bitcast.24, f32[64,40,256]{2,1,0:T(8,128)} %bitcast.25, f32[64,40,256]{2,1,0:T(8,128)} %bitcast.26, ...), custom_call_target="tpu_custom_call" | custom-call | flops 880803840 | bytes 17301504 | tf_op jit(solution)/shard_map/pallas_call | solution.py:150
  216.1 2.2 collective-permute-start.21
  219.4 2.3 shard_map.81
  221.7 11.7 %collective-permute-done.21.other = f32[40,2048]{1,0:T(8,128)S(1)} collective-permute-done((f32[40,2048]{1,0:T(8,128)}, f32[40,2048]{1,0:T(8,128)S(1)}, u32[]{:S(2)}, u32[]{:S(2)}) %collective-permute-start.21) | collective-permute-done | bytes 327712 | tf_op jit(solution)/shard_map/ppermute | solution.py:363
  234.2 3.9 all-to-all-done.4
  238.1 9.0 %all-to-all-start.5 = ((f32[16,4,40,256]{3,2,1,0:T(8,128)}), f32[16,4,40,256]{3,2,1,0:T(8,128)S(1)}, u32[]{:S(2)}, u32[]{:S(2)}) async-start(f32[16,4,40,256]{3,2,1,0:T(8,128)} %shard_map.81), calls=%async_computation.5 | async-start | bytes 5242880 | tf_op jit(solution)/shard_map/all_to_all | solution.py:295
  247.2 3.3 shard_map.82
  250.5 2.3 collective-permute-start.23
  252.8 1.5 collective-permute-start.24
  255.4 2.3 shard_map.83
  257.8 20.9 %collective-permute-done.24.refs_2_ = f32[12,40,256]{2,1,0:T(8,128)S(1)} collective-permute-done((f32[12,40,256]{2,1,0:T(8,128)S(1)}, f32[12,40,256]{2,1,0:T(8,128)S(1)}, u32[]{:S(2)}, u32[]{:S(2)}) %collective-permute-start.24) | collective-permute-done | bytes 491552 | tf_op jit(solution)/shard_map/ppermute | solution.py:128
  281.9 6.7 %all-to-all-start.6 = ((f32[16,4,40,256]{3,2,1,0:T(8,128)}), f32[16,4,40,256]{3,2,1,0:T(8,128)S(1)}, u32[]{:S(2)}, u32[]{:S(2)}) async-start(f32[16,4,40,256]{3,2,1,0:T(8,128)} %shard_map.83), calls=%async_computation.6 | async-start | bytes 5242880 | tf_op jit(solution)/shard_map/all_to_all | solution.py:295
  288.6 1.7 copy-done.5
  290.4 4.9 %shard_map.84 = (f32[14,40,256]{2,1,0:T(8,128)}, f32[14,40,256]{2,1,0:T(8,128)}, f32[14,40,256]{2,1,0:T(8,128)}, f32[14,40,256]{2,1,0:T(8,128)}) custom-call(s32[49]{0:T(128)S(1)} %copy-done.41, f32[64,40,256]{2,1,0:T(8,128)S(1)} %bitcast.37, f32[40,2048]{1,0:T(8,128)S(1)} %copy-done.9), custom_call_target="tpu_custom_call" | custom-call | bytes 4587520 | tf_op jit(solution)/shard_map/pallas_call | solution.py:109
  295.3 2.5 collective-permute-start.25
  298.9 2.3 shard_map.85
  301.2 17.9 %collective-permute-done.25.refs_13_ = f32[14,40,256]{2,1,0:T(8,128)S(1)} collective-permute-done((f32[14,40,256]{2,1,0:T(8,128)}, f32[14,40,256]{2,1,0:T(8,128)S(1)}, u32[]{:S(2)}, u32[]{:S(2)}) %collective-permute-start.25) | collective-permute-done | bytes 573472 | tf_op jit(solution)/shard_map/ppermute | solution.py:128
  320.8 2.3 all-to-all-done.6
  323.0 4.5 %all-to-all-start.7 = ((f32[16,4,32,256]{3,2,1,0:T(8,128)}), f32[16,4,32,256]{3,2,1,0:T(8,128)}, u32[]{:S(2)}, u32[]{:S(2)}) async-start(f32[16,4,32,256]{3,2,1,0:T(8,128)} %shard_map.85), calls=%async_computation.7 | async-start | bytes 4194304 | tf_op jit(solution)/shard_map/all_to_all | solution.py:295
  327.5 6.2 %collective-permute-start.28 = (f32[14,40,256]{2,1,0:T(8,128)}, f32[14,40,256]{2,1,0:T(8,128)S(1)}, u32[]{:S(2)}, u32[]{:S(2)}) collective-permute-start(f32[14,40,256]{2,1,0:T(8,128)} %get-tuple-element.151), channel_id=1, source_target_pairs={{0,96},{32,64},{64,32},{96,0},{1,97},{33,65},{65,33},{97,1},{2,98}... | collective-permute-start | bytes 1720328 | tf_op jit(solution)/shard_map/ppermute | solution.py:128
  333.7 4.9 %shard_map.88 = (f32[14,40,256]{2,1,0:T(8,128)}, f32[14,40,256]{2,1,0:T(8,128)}, f32[14,40,256]{2,1,0:T(8,128)}, f32[14,40,256]{2,1,0:T(8,128)}) custom-call(s32[49]{0:T(128)S(1)} %copy-done.41, f32[64,40,256]{2,1,0:T(8,128)S(1)} %bitcast.36, f32[40,2048]{1,0:T(8,128)S(1)} %copy-done.12), custom_call_target="tpu_custom_call" | custom-call | bytes 4587520 | tf_op jit(solution)/shard_map/pallas_call | solution.py:109
  340.6 7.4 %collective-permute-done.28.refs_14_ = f32[14,40,256]{2,1,0:T(8,128)S(1)} collective-permute-done((f32[14,40,256]{2,1,0:T(8,128)}, f32[14,40,256]{2,1,0:T(8,128)S(1)}, u32[]{:S(2)}, u32[]{:S(2)}) %collective-permute-start.28) | collective-permute-done | bytes 573472 | tf_op jit(solution)/shard_map/ppermute | solution.py:128
  348.7 8.8 %shard_map.86 = (f32[2,256,256]{2,1,0:T(8,128)}, f32[2,6,256,256]{3,2,1,0:T(8,128)}) custom-call(s32[1]{0:T(128)} %bitcast.me, f32[12,48,256]{2,1,0:T(8,128)} %get-tuple-element.100.refs_0_, f32[12,48,256]{2,1,0:T(8,128)} %collective-permute-done.10.refs_1_, f32[12,48,256]{2,1,0:T(8,128)} %collective-permute-done.16.refs_2_, ...), custom_call_target="tpu_custom_call" | custom-call | flops 3598712832 | bytes 17432576 | tf_op jit(solution)/shard_map/pallas_call | solution.py:240
  358.6 2.8 shard_map.87
  362.1 5.2 %collective-permute-start.30 = (f32[14,32,256]{2,1,0:T(8,128)}, f32[14,32,256]{2,1,0:T(8,128)S(1)}, u32[]{:S(2)}, u32[]{:S(2)}) collective-permute-start(f32[14,32,256]{2,1,0:T(8,128)} %get-tuple-element.159), channel_id=1, source_target_pairs={{0,96},{32,64},{64,32},{96,0},{1,97},{33,65},{65,33},{97,1},{2,98}... | collective-permute-start | bytes 1376264 | tf_op jit(solution)/shard_map/ppermute | solution.py:128
  367.7 4.4 %collective-permute-done.33.refs_6_ = f32[14,40,256]{2,1,0:T(8,128)S(1)} collective-permute-done((f32[14,40,256]{2,1,0:T(8,128)}, f32[14,40,256]{2,1,0:T(8,128)S(1)}, u32[]{:S(2)}, u32[]{:S(2)}) %collective-permute-start.33) | collective-permute-done | bytes 573472 | tf_op jit(solution)/shard_map/ppermute | solution.py:128
  373.1 7.3 %shard_map.89 = (f32[2,256,256]{2,1,0:T(8,128)}, f32[2,6,256,256]{3,2,1,0:T(8,128)}) custom-call(s32[1]{0:T(128)} %bitcast.me, f32[12,40,256]{2,1,0:T(8,128)} %get-tuple-element.119.refs_0_, f32[12,40,256]{2,1,0:T(8,128)} %copy-done.49, f32[12,40,256]{2,1,0:T(8,128)} %copy-done.51, f32[12,40,256]{2,1,0:T(8,128)} %copy-done.50, ...), custom_call_target="tpu_custom_call" | custom-call | flops 1635778560 | bytes 11927552 | tf_op jit(solution)/shard_map/pallas_call | solution.py:240
  381.2 9.3 %collective-permute-done.30.refs_6_ = f32[14,32,256]{2,1,0:T(8,128)S(1)} collective-permute-done((f32[14,32,256]{2,1,0:T(8,128)}, f32[14,32,256]{2,1,0:T(8,128)S(1)}, u32[]{:S(2)}, u32[]{:S(2)}) %collective-permute-start.30) | collective-permute-done | bytes 458784 | tf_op jit(solution)/shard_map/ppermute | solution.py:128
  391.4 6.9 %shard_map.90 = (f32[2,256,256]{2,1,0:T(8,128)}, f32[2,6,256,256]{3,2,1,0:T(8,128)}) custom-call(s32[1]{0:T(128)} %bitcast.me, f32[12,32,256]{2,1,0:T(8,128)} %get-tuple-element.90.refs_0_, f32[12,32,256]{2,1,0:T(8,128)} %copy-done.55, f32[12,32,256]{2,1,0:T(8,128)} %collective-permute-done.12.refs_2_, f32[12,32,256]{2,1,0:T(8,128)} %collective-permute-done.5.refs_3_, ...), custom_call_target="tpu_custom_call" | custom-call | flops 1308622848 | bytes 11010048 | tf_op jit(solution)/shard_map/pallas_call | solution.py:240
  (202 shorter events, 38.1 us)
Async XLA Ops:
  0.6 9.5 %copy-start.42 = (f32[160,2048]{1,0:T(8,128)S(1)}, f32[160,2048]{1,0:T(8,128)}, u32[]{:S(2)}) copy-start(f32[160,2048]{1,0:T(8,128)} %param.5) | copy-start | bytes 3932164
  1.7 11.9 %copy-start.19 = (f32[32,2048]{1,0:T(8,128)}, f32[32,2048]{1,0:T(8,128)S(1)}, u32[]{:S(2)}) copy-start(f32[32,2048]{1,0:T(8,128)S(1)} %slice.12.own) | copy-start | bytes 786436
  1.7 9.6 %collective-permute-start = (f32[32,2048]{1,0:T(8,128)S(1)}, f32[32,2048]{1,0:T(8,128)S(1)}, u32[]{:S(2)}, u32[]{:S(2)}) collective-permute-start(f32[32,2048]{1,0:T(8,128)S(1)} %slice.12.own), channel_id=1, source_target_pairs={{0,1},{1,0},{2,3},{3,2},{4,5},{5,4},{6,7},{7,6},{8,9},{9,8},{10,11... | collective-permute-start | bytes 786440 | tf_op jit(solution)/shard_map/ppermute | solution.py:305
  7.7 24.0 %copy-start.16 = (f32[48,2048]{1,0:T(8,128)}, f32[48,2048]{1,0:T(8,128)S(1)}, u32[]{:S(2)}) copy-start(f32[48,2048]{1,0:T(8,128)S(1)} %slice.13.own) | copy-start | bytes 1179652
  13.6 33.2 %all-to-all-start = ((f32[16,4,32,256]{3,2,1,0:T(8,128)}), f32[16,4,32,256]{3,2,1,0:T(8,128)S(1)}, u32[]{:S(2)}, u32[]{:S(2)}) async-start(f32[16,4,32,256]{3,2,1,0:T(8,128)} %shard_map.68), calls=%async_computation | async-start | bytes 4194304 | tf_op jit(solution)/shard_map/all_to_all | solution.py:295
  21.3 10.4 %collective-permute-start.1 = (f32[48,2048]{1,0:T(8,128)S(1)}, f32[48,2048]{1,0:T(8,128)S(1)}, u32[]{:S(2)}, u32[]{:S(2)}) collective-permute-start(f32[48,2048]{1,0:T(8,128)S(1)} %slice.13.own), channel_id=1, source_target_pairs={{0,1},{1,0},{2,3},{3,2},{4,5},{5,4},{6,7},{7,6},{8,9},{9,8},{10,11... | collective-permute-start | bytes 1179656 | tf_op jit(solution)/shard_map/ppermute | solution.py:311
  48.2 51.4 %all-to-all-start.1 = ((f32[16,4,48,256]{3,2,1,0:T(8,128)}), f32[16,4,48,256]{3,2,1,0:T(8,128)S(1)}, u32[]{:S(2)}, u32[]{:S(2)}) async-start(f32[16,4,48,256]{3,2,1,0:T(8,128)} %shard_map.69), calls=%async_computation.1 | async-start | bytes 6291456 | tf_op jit(solution)/shard_map/all_to_all | solution.py:295
  53.7 15.4 %collective-permute-start.2 = (f32[40,2048]{1,0:T(8,128)}, f32[40,2048]{1,0:T(8,128)S(1)}, u32[]{:S(2)}, u32[]{:S(2)}) collective-permute-start(f32[40,2048]{1,0:T(8,128)} %get-tuple-element.91.own), channel_id=1, source_target_pairs={{0,1},{1,0},{2,3},{3,2},{4,5},{5,4},{6,7},{7,6},{8,9},{9,8},{10,11... | collective-permute-start | bytes 983048 | tf_op jit(solution)/shard_map/ppermute | solution.py:311
  56.7 14.1 %collective-permute-start.3 = (f32[40,2048]{1,0:T(8,128)S(1)}, f32[40,2048]{1,0:T(8,128)S(1)}, u32[]{:S(2)}, u32[]{:S(2)}) collective-permute-start(f32[40,2048]{1,0:T(8,128)S(1)} %copy-done.17), channel_id=1, source_target_pairs={{0,1},{1,0},{2,3},{3,2},{4,5},{5,4},{6,7},{7,6},{8,9},{9,8},{10,11... | collective-permute-start | bytes 983048 | tf_op jit(solution)/shard_map/ppermute | solution.py:311
  58.9 28.3 %collective-permute-start.7 = (f32[160,512]{1,0:T(8,128)S(1)}, f32[160,512]{1,0:T(8,128)S(1)}, u32[]{:S(2)}, u32[]{:S(2)}) collective-permute-start(f32[160,512]{1,0:T(8,128)S(1)} %get-tuple-element.175), channel_id=1, source_target_pairs={{0,64},{32,96},{64,0},{96,32},{1,65},{33,97},{65,1},{97,33},{2,66}... | collective-permute-start | bytes 983048 | tf_op jit(solution)/shard_map/ppermute | solution.py:128
  60.3 16.4 %copy-start.37 = (s32[49]{0:T(128)}, s32[49]{0:T(128)S(1)}, u32[]{:S(2)}) copy-start(s32[49]{0:T(128)S(1)} %pad_add_fusion.pick) | copy-start | bytes 592
  64.3 34.4 %collective-permute-start.4 = (f32[12,32,256]{2,1,0:T(8,128)}, f32[12,32,256]{2,1,0:T(8,128)S(1)}, u32[]{:S(2)}, u32[]{:S(2)}) collective-permute-start(f32[12,32,256]{2,1,0:T(8,128)} %get-tuple-element.95), channel_id=1, source_target_pairs={{0,64},{32,96},{64,0},{96,32},{1,65},{33,97},{65,1},{97,33},{2,66}... | collective-permute-start | bytes 1179656 | tf_op jit(solution)/shard_map/ppermute | solution.py:128
  64.6 35.0 %collective-permute-start.5 = (f32[12,32,256]{2,1,0:T(8,128)}, f32[12,32,256]{2,1,0:T(8,128)}, u32[]{:S(2)}, u32[]{:S(2)}) collective-permute-start(f32[12,32,256]{2,1,0:T(8,128)} %get-tuple-element.96), channel_id=1, source_target_pairs={{0,32},{32,0},{64,96},{96,64},{1,33},{33,1},{65,97},{97,65},{2,34}... | collective-permute-start | bytes 1179656 | tf_op jit(solution)/shard_map/ppermute | solution.py:128
  69.2 28.7 %collective-permute-start.8 = (f32[160,512]{1,0:T(8,128)S(1)}, f32[160,512]{1,0:T(8,128)S(1)}, u32[]{:S(2)}, u32[]{:S(2)}) collective-permute-start(f32[160,512]{1,0:T(8,128)S(1)} %get-tuple-element.174), channel_id=1, source_target_pairs={{0,96},{32,64},{64,32},{96,0},{1,97},{33,65},{65,33},{97,1},{2,98}... | collective-permute-start | bytes 983048 | tf_op jit(solution)/shard_map/ppermute | solution.py:128
  70.8 19.4 %copy-start.23 = (f32[40,2048]{1,0:T(8,128)}, f32[40,2048]{1,0:T(8,128)S(1)}, u32[]{:S(2)}) copy-start(f32[40,2048]{1,0:T(8,128)S(1)} %collective-permute-done.3.refs_2_.other) | copy-start | bytes 983044
  70.8 19.4 %copy-start.18 = (f32[40,2048]{1,0:T(8,128)S(1)}, f32[40,2048]{1,0:T(8,128)}, u32[]{:S(2)}) copy-start(f32[40,2048]{1,0:T(8,128)} %get-tuple-element.91.own) | copy-start | bytes 983044
  70.9 19.4 %copy-start.22 = (f32[12,32,256]{2,1,0:T(8,128)S(1)}, f32[12,32,256]{2,1,0:T(8,128)}, u32[]{:S(2)}) copy-start(f32[12,32,256]{2,1,0:T(8,128)} %get-tuple-element.90.refs_0_) | copy-start | bytes 1179652
  70.9 27.1 %collective-permute-start.9 = (f32[160,512]{1,0:T(8,128)S(1)}, f32[160,512]{1,0:T(8,128)S(1)}, u32[]{:S(2)}, u32[]{:S(2)}) collective-permute-start(f32[160,512]{1,0:T(8,128)S(1)} %get-tuple-element.173), channel_id=1, source_target_pairs={{0,32},{32,0},{64,96},{96,64},{1,33},{33,1},{65,97},{97,65},{2,34}... | collective-permute-start | bytes 983048 | tf_op jit(solution)/shard_map/ppermute | solution.py:128
  87.3 11.4 %copy-start.43 = (f32[160,512]{1,0:T(8,128)}, f32[160,512]{1,0:T(8,128)S(1)}, u32[]{:S(2)}) copy-start(f32[160,512]{1,0:T(8,128)S(1)} %collective-permute-done.7.refs_17_.refs_9_) | copy-start | bytes 983044
  87.3 10.6 %collective-permute-start.6 = (f32[32,2048]{1,0:T(8,128)}, f32[32,2048]{1,0:T(8,128)S(1)}, u32[]{:S(2)}, u32[]{:S(2)}) collective-permute-start(f32[32,2048]{1,0:T(8,128)} %shard_map.71.refs_3_.own.refs_0_), channel_id=1, source_target_pairs={{0,1},{1,0},{2,3},{3,2},{4,5},{5,4},{6,7},{7,6},{8,9},{9,8},{10,11... | collective-permute-start | bytes 786440 | tf_op jit(solution)/shard_map/ppermute | solution.py:363
  99.6 48.0 %all-to-all-start.2 = ((f32[16,4,40,256]{3,2,1,0:T(8,128)}), f32[16,4,40,256]{3,2,1,0:T(8,128)}, u32[]{:S(2)}, u32[]{:S(2)}) async-start(f32[16,4,40,256]{3,2,1,0:T(8,128)} %shard_map.72), calls=%async_computation.2 | async-start | bytes 5242880 | tf_op jit(solution)/shard_map/all_to_all | solution.py:295
  111.5 36.1 %collective-permute-start.10 = (f32[12,48,256]{2,1,0:T(8,128)}, f32[12,48,256]{2,1,0:T(8,128)}, u32[]{:S(2)}, u32[]{:S(2)}) collective-permute-start(f32[12,48,256]{2,1,0:T(8,128)} %get-tuple-element.103), channel_id=1, source_target_pairs={{0,64},{32,96},{64,0},{96,32},{1,65},{33,97},{65,1},{97,33},{2,66}... | collective-permute-start | bytes 1769480 | tf_op jit(solution)/shard_map/ppermute | solution.py:128
  112.7 17.0 %copy-start.65 = (f32[12,32,256]{2,1,0:T(8,128)S(1)}, f32[12,32,256]{2,1,0:T(8,128)}, u32[]{:S(2)}) copy-start(f32[12,32,256]{2,1,0:T(8,128)} %get-tuple-element.105) | copy-start | bytes 1179652
  112.7 17.1 %copy-start.24 = (f32[40,2048]{1,0:T(8,128)S(1)}, f32[40,2048]{1,0:T(8,128)}, u32[]{:S(2)}) copy-start(f32[40,2048]{1,0:T(8,128)} %copy-done.23) | copy-start | bytes 983044
  112.7 17.1 %copy-start.26 = (f32[12,48,256]{2,1,0:T(8,128)S(1)}, f32[12,48,256]{2,1,0:T(8,128)}, u32[]{:S(2)}) copy-start(f32[12,48,256]{2,1,0:T(8,128)} %get-tuple-element.100.refs_0_) | copy-start | bytes 1769476
  112.7 34.9 %collective-permute-start.11 = (f32[12,48,256]{2,1,0:T(8,128)}, f32[12,48,256]{2,1,0:T(8,128)}, u32[]{:S(2)}, u32[]{:S(2)}) collective-permute-start(f32[12,48,256]{2,1,0:T(8,128)} %get-tuple-element.104), channel_id=1, source_target_pairs={{0,32},{32,0},{64,96},{96,64},{1,33},{33,1},{65,97},{97,65},{2,34}... | collective-permute-start | bytes 1769480 | tf_op jit(solution)/shard_map/ppermute | solution.py:128
  127.0 12.4 %collective-permute-start.13 = (f32[48,2048]{1,0:T(8,128)}, f32[48,2048]{1,0:T(8,128)S(1)}, u32[]{:S(2)}, u32[]{:S(2)}) collective-permute-start(f32[48,2048]{1,0:T(8,128)} %shard_map.74.refs_1_.own.refs_0_), channel_id=1, source_target_pairs={{0,1},{1,0},{2,3},{3,2},{4,5},{5,4},{6,7},{7,6},{8,9},{9,8},{10,11... | collective-permute-start | bytes 1179656 | tf_op jit(solution)/shard_map/ppermute | solution.py:363
  129.7 18.0 %collective-permute-start.12 = (f32[12,32,256]{2,1,0:T(8,128)S(1)}, f32[12,32,256]{2,1,0:T(8,128)}, u32[]{:S(2)}, u32[]{:S(2)}) collective-permute-start(f32[12,32,256]{2,1,0:T(8,128)S(1)} %copy-done.65), channel_id=1, source_target_pairs={{0,96},{32,64},{64,32},{96,0},{1,97},{33,65},{65,33},{97,1},{2,98}... | collective-permute-start | bytes 1179656 | tf_op jit(solution)/shard_map/ppermute | solution.py:128
  147.7 8.9 %copy-start.39 = (s32[49]{0:T(128)S(1)}, s32[49]{0:T(128)}, u32[]{:S(2)}) copy-start(s32[49]{0:T(128)} %copy-done.37) | copy-start | bytes 592
  147.7 42.9 %all-to-all-start.3 = ((f32[16,4,40,256]{3,2,1,0:T(8,128)}), f32[16,4,40,256]{3,2,1,0:T(8,128)S(1)}, u32[]{:S(2)}, u32[]{:S(2)}) async-start(f32[16,4,40,256]{3,2,1,0:T(8,128)} %shard_map.75), calls=%async_computation.3 | async-start | bytes 5242880 | tf_op jit(solution)/shard_map/all_to_all | solution.py:295
  154.6 36.0 %collective-permute-start.16 = (f32[12,48,256]{2,1,0:T(8,128)}, f32[12,48,256]{2,1,0:T(8,128)}, u32[]{:S(2)}, u32[]{:S(2)}) collective-permute-start(f32[12,48,256]{2,1,0:T(8,128)} %get-tuple-element.116), channel_id=1, source_target_pairs={{0,96},{32,64},{64,32},{96,0},{1,97},{33,65},{65,33},{97,1},{2,98}... | collective-permute-start | bytes 1769480 | tf_op jit(solution)/shard_map/ppermute | solution.py:128
  159.5 29.5 %collective-permute-start.14 = (f32[12,40,256]{2,1,0:T(8,128)}, f32[12,40,256]{2,1,0:T(8,128)S(1)}, u32[]{:S(2)}, u32[]{:S(2)}) collective-permute-start(f32[12,40,256]{2,1,0:T(8,128)} %get-tuple-element.114), channel_id=1, source_target_pairs={{0,64},{32,96},{64,0},{96,32},{1,65},{33,97},{65,1},{97,33},{2,66}... | collective-permute-start | bytes 1474568 | tf_op jit(solution)/shard_map/ppermute | solution.py:128
  159.6 12.3 %copy-start.7 = (f32[48,2048]{1,0:T(8,128)S(1)}, f32[48,2048]{1,0:T(8,128)}, u32[]{:S(2)}) copy-start(f32[48,2048]{1,0:T(8,128)} %shard_map.74.refs_1_.own.refs_0_) | copy-start | bytes 1179652
  159.6 12.3 %copy-start.28 = (f32[12,40,256]{2,1,0:T(8,128)S(1)}, f32[12,40,256]{2,1,0:T(8,128)}, u32[]{:S(2)}) copy-start(f32[12,40,256]{2,1,0:T(8,128)} %get-tuple-element.111.refs_0_.refs_4_) | copy-start | bytes 1474564
  159.6 12.3 %copy-start.30 = (f32[48,2048]{1,0:T(8,128)S(1)}, f32[48,2048]{1,0:T(8,128)}, u32[]{:S(2)}) copy-start(f32[48,2048]{1,0:T(8,128)} %copy-done.29) | copy-start | bytes 1179652
  159.6 29.3 %collective-permute-start.15 = (f32[12,40,256]{2,1,0:T(8,128)}, f32[12,40,256]{2,1,0:T(8,128)S(1)}, u32[]{:S(2)}, u32[]{:S(2)}) collective-permute-start(f32[12,40,256]{2,1,0:T(8,128)} %get-tuple-element.115), channel_id=1, source_target_pairs={{0,32},{32,0},{64,96},{96,64},{1,33},{33,1},{65,97},{97,65},{2,34}... | collective-permute-start | bytes 1474568 | tf_op jit(solution)/shard_map/ppermute | solution.py:128
  170.8 17.5 %collective-permute-start.17 = (f32[40,2048]{1,0:T(8,128)}, f32[40,2048]{1,0:T(8,128)S(1)}, u32[]{:S(2)}, u32[]{:S(2)}) collective-permute-start(f32[40,2048]{1,0:T(8,128)} %shard_map.77.refs_1_.own.refs_0_), channel_id=1, source_target_pairs={{0,1},{1,0},{2,3},{3,2},{4,5},{5,4},{6,7},{7,6},{8,9},{9,8},{10,11... | collective-permute-start | bytes 983048 | tf_op jit(solution)/shard_map/ppermute | solution.py:363
  190.6 47.6 %all-to-all-start.4 = ((f32[16,4,48,256]{3,2,1,0:T(8,128)}), f32[16,4,48,256]{3,2,1,0:T(8,128)}, u32[]{:S(2)}, u32[]{:S(2)}) async-start(f32[16,4,48,256]{3,2,1,0:T(8,128)} %shard_map.78), calls=%async_computation.4 | async-start | bytes 6291456 | tf_op jit(solution)/shard_map/all_to_all | solution.py:295
  202.5 31.7 %collective-permute-start.18 = (f32[12,40,256]{2,1,0:T(8,128)}, f32[12,40,256]{2,1,0:T(8,128)S(1)}, u32[]{:S(2)}, u32[]{:S(2)}) collective-permute-start(f32[12,40,256]{2,1,0:T(8,128)} %get-tuple-element.122), channel_id=1, source_target_pairs={{0,64},{32,96},{64,0},{96,32},{1,65},{33,97},{65,1},{97,33},{2,66}... | collective-permute-start | bytes 1474568 | tf_op jit(solution)/shard_map/ppermute | solution.py:128
  203.5 14.9 %copy-start.9 = (f32[40,2048]{1,0:T(8,128)S(1)}, f32[40,2048]{1,0:T(8,128)}, u32[]{:S(2)}) copy-start(f32[40,2048]{1,0:T(8,128)} %shard_map.77.refs_1_.own.refs_0_) | copy-start | bytes 983044
  203.5 14.9 %copy-start.21 = (f32[12,40,256]{2,1,0:T(8,128)S(1)}, f32[12,40,256]{2,1,0:T(8,128)}, u32[]{:S(2)}) copy-start(f32[12,40,256]{2,1,0:T(8,128)} %get-tuple-element.119.refs_0_) | copy-start | bytes 1474564
  203.5 14.9 %copy-start.32 = (f32[40,2048]{1,0:T(8,128)S(1)}, f32[40,2048]{1,0:T(8,128)}, u32[]{:S(2)}) copy-start(f32[40,2048]{1,0:T(8,128)} %copy-done.31) | copy-start | bytes 983044
  203.5 30.7 %collective-permute-start.19 = (f32[12,40,256]{2,1,0:T(8,128)}, f32[12,40,256]{2,1,0:T(8,128)S(1)}, u32[]{:S(2)}, u32[]{:S(2)}) collective-permute-start(f32[12,40,256]{2,1,0:T(8,128)} %get-tuple-element.123), channel_id=1, source_target_pairs={{0,32},{32,0},{64,96},{96,64},{1,33},{33,1},{65,97},{97,65},{2,34}... | collective-permute-start | bytes 1474568 | tf_op jit(solution)/shard_map/ppermute | solution.py:128
  205.4 28.8 %collective-permute-start.20 = (f32[12,40,256]{2,1,0:T(8,128)S(1)}, f32[12,40,256]{2,1,0:T(8,128)S(1)}, u32[]{:S(2)}, u32[]{:S(2)}) collective-permute-start(f32[12,40,256]{2,1,0:T(8,128)S(1)} %copy-done.63), channel_id=1, source_target_pairs={{0,96},{32,64},{64,32},{96,0},{1,97},{33,65},{65,33},{97,1},{2,98}... | collective-permute-start | bytes 1474568 | tf_op jit(solution)/shard_map/ppermute | solution.py:128
  216.1 17.3 %collective-permute-start.21 = (f32[40,2048]{1,0:T(8,128)}, f32[40,2048]{1,0:T(8,128)S(1)}, u32[]{:S(2)}, u32[]{:S(2)}) collective-permute-start(f32[40,2048]{1,0:T(8,128)} %shard_map.79.refs_1_.own.refs_0_), channel_id=1, source_target_pairs={{0,1},{1,0},{2,3},{3,2},{4,5},{5,4},{6,7},{7,6},{8,9},{9,8},{10,11... | collective-permute-start | bytes 983048 | tf_op jit(solution)/shard_map/ppermute | solution.py:363
  238.1 9.0 %copy-start.41 = (s32[49]{0:T(128)S(1)}, s32[49]{0:T(128)}, u32[]{:S(2)}) copy-start(s32[49]{0:T(128)} %copy-done.37) | copy-start | bytes 592
  238.1 42.2 %all-to-all-start.5 = ((f32[16,4,40,256]{3,2,1,0:T(8,128)}), f32[16,4,40,256]{3,2,1,0:T(8,128)S(1)}, u32[]{:S(2)}, u32[]{:S(2)}) async-start(f32[16,4,40,256]{3,2,1,0:T(8,128)} %shard_map.81), calls=%async_computation.5 | async-start | bytes 5242880 | tf_op jit(solution)/shard_map/all_to_all | solution.py:295
  250.4 28.3 %collective-permute-start.22 = (f32[14,48,256]{2,1,0:T(8,128)}, f32[14,48,256]{2,1,0:T(8,128)S(1)}, u32[]{:S(2)}, u32[]{:S(2)}) collective-permute-start(f32[14,48,256]{2,1,0:T(8,128)} %get-tuple-element.130), channel_id=1, source_target_pairs={{0,64},{32,96},{64,0},{96,32},{1,65},{33,97},{65,1},{97,33},{2,66}... | collective-permute-start | bytes 2064392 | tf_op jit(solution)/shard_map/ppermute | solution.py:128
  250.5 29.8 %collective-permute-start.23 = (f32[14,48,256]{2,1,0:T(8,128)}, f32[14,48,256]{2,1,0:T(8,128)}, u32[]{:S(2)}, u32[]{:S(2)}) collective-permute-start(f32[14,48,256]{2,1,0:T(8,128)} %get-tuple-element.131), channel_id=1, source_target_pairs={{0,32},{32,0},{64,96},{96,64},{1,33},{33,1},{65,97},{97,65},{2,34}... | collective-permute-start | bytes 2064392 | tf_op jit(solution)/shard_map/ppermute | solution.py:128
  252.8 25.9 %collective-permute-start.24 = (f32[12,40,256]{2,1,0:T(8,128)S(1)}, f32[12,40,256]{2,1,0:T(8,128)S(1)}, u32[]{:S(2)}, u32[]{:S(2)}) collective-permute-start(f32[12,40,256]{2,1,0:T(8,128)S(1)} %copy-done.64), channel_id=1, source_target_pairs={{0,96},{32,64},{64,32},{96,0},{1,97},{33,65},{65,33},{97,1},{2,98}... | collective-permute-start | bytes 1474568 | tf_op jit(solution)/shard_map/ppermute | solution.py:128
  281.9 41.2 %all-to-all-start.6 = ((f32[16,4,40,256]{3,2,1,0:T(8,128)}), f32[16,4,40,256]{3,2,1,0:T(8,128)S(1)}, u32[]{:S(2)}, u32[]{:S(2)}) async-start(f32[16,4,40,256]{3,2,1,0:T(8,128)} %shard_map.83), calls=%async_computation.6 | async-start | bytes 5242880 | tf_op jit(solution)/shard_map/all_to_all | solution.py:295
  288.5 32.3 %collective-permute-start.27 = (f32[14,48,256]{2,1,0:T(8,128)}, f32[14,48,256]{2,1,0:T(8,128)}, u32[]{:S(2)}, u32[]{:S(2)}) collective-permute-start(f32[14,48,256]{2,1,0:T(8,128)} %get-tuple-element.139), channel_id=1, source_target_pairs={{0,96},{32,64},{64,32},{96,0},{1,97},{33,65},{65,33},{97,1},{2,98}... | collective-permute-start | bytes 2064392 | tf_op jit(solution)/shard_map/ppermute | solution.py:128
  295.3 23.9 %collective-permute-start.25 = (f32[14,40,256]{2,1,0:T(8,128)}, f32[14,40,256]{2,1,0:T(8,128)S(1)}, u32[]{:S(2)}, u32[]{:S(2)}) collective-permute-start(f32[14,40,256]{2,1,0:T(8,128)} %get-tuple-element.137), channel_id=1, source_target_pairs={{0,64},{32,96},{64,0},{96,32},{1,65},{33,97},{65,1},{97,33},{2,66}... | collective-permute-start | bytes 1720328 | tf_op jit(solution)/shard_map/ppermute | solution.py:128
  297.8 21.3 %collective-permute-start.26 = (f32[14,40,256]{2,1,0:T(8,128)}, f32[14,40,256]{2,1,0:T(8,128)S(1)}, u32[]{:S(2)}, u32[]{:S(2)}) collective-permute-start(f32[14,40,256]{2,1,0:T(8,128)} %get-tuple-element.138), channel_id=1, source_target_pairs={{0,32},{32,0},{64,96},{96,64},{1,33},{33,1},{65,97},{97,65},{2,34}... | collective-permute-start | bytes 1720328 | tf_op jit(solution)/shard_map/ppermute | solution.py:128
  301.2 32.5 %copy-start.12 = (f32[40,2048]{1,0:T(8,128)S(1)}, f32[40,2048]{1,0:T(8,128)}, u32[]{:S(2)}) copy-start(f32[40,2048]{1,0:T(8,128)} %shard_map.79.refs_1_.own.refs_0_) | copy-start | bytes 983044
  323.0 34.5 %all-to-all-start.7 = ((f32[16,4,32,256]{3,2,1,0:T(8,128)}), f32[16,4,32,256]{3,2,1,0:T(8,128)}, u32[]{:S(2)}, u32[]{:S(2)}) async-start(f32[16,4,32,256]{3,2,1,0:T(8,128)} %shard_map.85), calls=%async_computation.7 | async-start | bytes 4194304 | tf_op jit(solution)/shard_map/all_to_all | solution.py:295
  327.5 20.4 %collective-permute-start.28 = (f32[14,40,256]{2,1,0:T(8,128)}, f32[14,40,256]{2,1,0:T(8,128)S(1)}, u32[]{:S(2)}, u32[]{:S(2)}) collective-permute-start(f32[14,40,256]{2,1,0:T(8,128)} %get-tuple-element.151), channel_id=1, source_target_pairs={{0,96},{32,64},{64,32},{96,0},{1,97},{33,65},{65,33},{97,1},{2,98}... | collective-permute-start | bytes 1720328 | tf_op jit(solution)/shard_map/ppermute | solution.py:128
  338.6 28.7 %collective-permute-start.32 = (f32[14,40,256]{2,1,0:T(8,128)}, f32[14,40,256]{2,1,0:T(8,128)S(1)}, u32[]{:S(2)}, u32[]{:S(2)}) collective-permute-start(f32[14,40,256]{2,1,0:T(8,128)} %get-tuple-element.166), channel_id=1, source_target_pairs={{0,64},{32,96},{64,0},{96,32},{1,65},{33,97},{65,1},{97,33},{2,66}... | collective-permute-start | bytes 1720328 | tf_op jit(solution)/shard_map/ppermute | solution.py:128
  338.7 33.4 %collective-permute-start.33 = (f32[14,40,256]{2,1,0:T(8,128)}, f32[14,40,256]{2,1,0:T(8,128)S(1)}, u32[]{:S(2)}, u32[]{:S(2)}) collective-permute-start(f32[14,40,256]{2,1,0:T(8,128)} %get-tuple-element.167), channel_id=1, source_target_pairs={{0,96},{32,64},{64,32},{96,0},{1,97},{33,65},{65,33},{97,1},{2,98}... | collective-permute-start | bytes 1720328 | tf_op jit(solution)/shard_map/ppermute | solution.py:128
  339.5 32.6 %collective-permute-start.34 = (f32[14,40,256]{2,1,0:T(8,128)}, f32[14,40,256]{2,1,0:T(8,128)S(1)}, u32[]{:S(2)}, u32[]{:S(2)}) collective-permute-start(f32[14,40,256]{2,1,0:T(8,128)} %get-tuple-element.168), channel_id=1, source_target_pairs={{0,32},{32,0},{64,96},{96,64},{1,33},{33,1},{65,97},{97,65},{2,34}... | collective-permute-start | bytes 1720328 | tf_op jit(solution)/shard_map/ppermute | solution.py:128
  361.4 19.8 %collective-permute-start.29 = (f32[14,32,256]{2,1,0:T(8,128)}, f32[14,32,256]{2,1,0:T(8,128)S(1)}, u32[]{:S(2)}, u32[]{:S(2)}) collective-permute-start(f32[14,32,256]{2,1,0:T(8,128)} %get-tuple-element.158), channel_id=1, source_target_pairs={{0,64},{32,96},{64,0},{96,32},{1,65},{33,97},{65,1},{97,33},{2,66}... | collective-permute-start | bytes 1376264 | tf_op jit(solution)/shard_map/ppermute | solution.py:128
  362.1 28.3 %collective-permute-start.30 = (f32[14,32,256]{2,1,0:T(8,128)}, f32[14,32,256]{2,1,0:T(8,128)S(1)}, u32[]{:S(2)}, u32[]{:S(2)}) collective-permute-start(f32[14,32,256]{2,1,0:T(8,128)} %get-tuple-element.159), channel_id=1, source_target_pairs={{0,96},{32,64},{64,32},{96,0},{1,97},{33,65},{65,33},{97,1},{2,98}... | collective-permute-start | bytes 1376264 | tf_op jit(solution)/shard_map/ppermute | solution.py:128
  367.3 23.1 %collective-permute-start.31 = (f32[14,32,256]{2,1,0:T(8,128)}, f32[14,32,256]{2,1,0:T(8,128)S(1)}, u32[]{:S(2)}, u32[]{:S(2)}) collective-permute-start(f32[14,32,256]{2,1,0:T(8,128)} %get-tuple-element.160), channel_id=1, source_target_pairs={{0,32},{32,0},{64,96},{96,64},{1,33},{33,1},{65,97},{97,65},{2,34}... | collective-permute-start | bytes 1376264 | tf_op jit(solution)/shard_map/ppermute | solution.py:128
  381.2 9.3 %copy-start.52 = (f32[14,32,256]{2,1,0:T(8,128)}, f32[14,32,256]{2,1,0:T(8,128)S(1)}, u32[]{:S(2)}) copy-start(f32[14,32,256]{2,1,0:T(8,128)S(1)} %collective-permute-done.29.refs_5_) | copy-start | bytes 1376260
  (45 other events, 137.0 us)
